TPU v7x, 32 devices: a whole 2x2x4 slice. The times are simulated.
32 devices in a mesh: dp: 8 (over z, x), cores: 4 (over y, core).
Axes of the slice: x: 2, y: 2, z: 4, core: 2. Of those that a mesh axis runs over, the one named last changes fastest.
Arguments:
- features: bfloat16 [65536, 1027], P(('dp', 'cores')), may hold values from -6 to 6
- labels: int32 [65536], P(('dp', 'cores')), may hold values 0 or 1
- days: int32 [65536], P(('dp', 'cores')), may hold values from 0 to 23, as said below
- master: float32 [4214944], P(('dp', 'cores'))
- moment_one: float32 [4214944], P(('dp', 'cores'))
- moment_two: float32 [4214944], P(('dp', 'cores')), as said below
Outputs:
- logits: float32 [65536], P(('dp', 'cores'))
- loss: float32 [], replicated
- feature_grad: float32 [65536, 1027], P(('dp', 'cores'))
- flat_grad: float32 [4214944], P(('dp', 'cores'))
- new_moment_one: float32 [4214944], P(('dp', 'cores'))
- new_moment_two: float32 [4214944], P(('dp', 'cores'))
- new_master: float32 [4214944], P(('dp', 'cores'))
- new_bias: float32 [4192], P(('dp', 'cores'))
Inputs may be any that keep to these rules, and one draw needn't show every extreme that they name: Each of the 24 days holds at least one example; day numbers mostly grow with the example's index. `moment_two`: Positive.
All inputs are finite; a program needn't handle non-finite values. No bound on the sum of `labels` on one device may be relied on, other than what follows from the above.
Results may differ from a plain program's by a relative error of at most 0.012.
The roundings to bfloat16 on the way count: a program that leaves them out, or rounds other values in their place, can miss the bound.
Values may be sent and summed in bfloat16 or wider, within the bound.
No kernel may reach another device: no remote copies, remote signals or barrier semaphores. Data moves between devices by JAX's collectives and lax.ppermute only.
A program may use at most 256 MiB of HBM per device.

v0:
```python
import functools
import math

import jax
import jax.numpy as jnp
from jax import lax
from jax.experimental import pallas as pl
from jax.experimental.pallas import tpu as pltpu
from jax.sharding import PartitionSpec as P

D = 1027
H = 1024
DAYS = 24
STEP = 10
AXES = ("dp", "cores")
EXTRA = D - H
LANES = 128
WIDE = H + LANES
AUX_ROWS = 16
SPILL_ROWS = 4
MISC_ROW = 12
UNIT_LINES = 15
TILE = 512
TALL = H + 16
MIB = 1024 * 1024
F32 = jnp.float32
LOW = jnp.bfloat16
SMEM = pl.BlockSpec(memory_space=pltpu.SMEM)
VMEM = pl.BlockSpec(memory_space=pltpu.VMEM)
PARAMS = pltpu.CompilerParams(vmem_limit_bytes=56 * MIB)


def shapes():
    return [(D, D), (D,), (D, D), (D,), (D, H), (H,), (H, H), (H,), (H,), (1,)]


def piece_sizes(count):
    return [(math.prod(shape) + count - 1) // count for shape in shapes()[:-1]] + [1]


def starts_of(count):
    starts = []
    position = 0
    for piece in piece_sizes(count):
        starts.append(position)
        position += piece
    return starts


def to_block(piece, index, width, rows, count):
    excess = piece.shape[0] - rows * width
    size = (rows + SPILL_ROWS) * width
    lead = (count - 1) * excess
    padded = jnp.pad(piece, (lead, max(0, size - piece.shape[0])))
    line = lax.dynamic_slice(padded, (lead - index * excess,), (size,))
    return line.reshape(rows + SPILL_ROWS, width)


def from_block(block, index, piece, rows, count):
    width = block.shape[1]
    excess = piece - rows * width
    last = (count - 1) * excess
    line = jnp.pad(block.reshape(-1), (0, max(0, last + piece - block.size)))
    return lax.dynamic_slice(line, (index * excess,), (piece,))


def bit_groups(mesh):
    devices = mesh.devices.reshape(-1)
    groups = {"z": [], "plane": [], "core": []}
    bit = 1
    while bit < devices.size:
        here = getattr(devices[0], "coords", None)
        there = getattr(devices[bit], "coords", None)
        if here is None or there is None:
            name = "core" if bit == 1 else "plane" if bit <= 4 else "z"
        elif tuple(here) == tuple(there):
            name = "core"
        elif here[2] != there[2]:
            name = "z"
        else:
            name = "plane"
        groups[name].append(bit)
        bit *= 2
    return groups


def masks_of(bits):
    masks = [0]
    for bit in bits:
        masks = masks + [mask | bit for mask in masks]
    return masks


def teams(bits, count):
    masks = masks_of(bits)
    return [[k | mask for mask in masks] for k in range(count) if not k & masks[-1]]


def owner(index, mask, groups, by_z):
    if by_z:
        index = jnp.bitwise_and(index, ~masks_of(groups["z"])[-1])
    return jnp.bitwise_xor(index, mask)


def swap(value, mask, count):
    return lax.ppermute(value, AXES, [(k, k ^ mask) for k in range(count)])


def join(parts, after):
    def kernel(*refs):
        for j in range(len(parts)):
            refs[-1][j] = refs[j][...]

    return pl.pallas_call(
        kernel,
        out_shape=jax.ShapeDtypeStruct((len(parts),) + parts[0].shape, parts[0].dtype),
        in_specs=[VMEM] * len(parts) + [pl.BlockSpec(memory_space=pl.ANY)] * len(after),
        out_specs=VMEM,
        compiler_params=PARAMS,
        name="join",
    )(*parts, *after)


def gather(block, groups, count, direct=False, after=()):
    z_masks = masks_of(groups["z"])
    core_masks = masks_of(groups["core"])
    line = [block] + [swap(block, mask, count) for mask in z_masks[1:]]
    line = join(line, after) if after else jnp.stack(line)
    plane = [(line, z_masks)]
    if len(groups["plane"]) == 2 and len(z_masks) > 1 and not direct:
        one, two = groups["plane"]
        half = len(z_masks) // 2
        by_one = swap(line, one, count)
        by_two = swap(line, two, count)
        plane.append((by_one, [one ^ z for z in z_masks]))
        plane.append((by_two, [two ^ z for z in z_masks]))
        both = one ^ two
        plane.append((swap(by_one[:half], two, count), [both ^ z for z in z_masks[:half]]))
        plane.append((swap(by_two[half:], one, count), [both ^ z for z in z_masks[half:]]))
    else:
        for mask in masks_of(groups["plane"])[1:]:
            plane.append((swap(line, mask, count), [mask ^ z for z in z_masks]))
    result = list(plane)
    for core in core_masks[1:]:
        result += [(swap(value, core, count), [core ^ m for m in row]) for value, row in plane]
    return result


def place(index, stacks, rows, count, parts, aux=None):
    sources = [value for value, _ in stacks]
    masks = [row for _, row in stacks]
    carries = aux is None
    top = min(16, rows)

    def kernel(index_ref, *refs):
        refs = list(refs)
        aux_ref = refs.pop() if carries else refs.pop(0)
        outs = refs[len(sources) :]
        for ref, row in zip(refs, masks):
            for j, mask in enumerate(row):
                at = jnp.bitwise_xor(index_ref[0], mask)
                for i, out_ref in enumerate(outs):
                    out_ref[at] = ref[j, i * rows : (i + 1) * rows]
                if carries:
                    aux_ref[at] = ref[j, len(outs) * rows :]
        for spill_at, out_ref in zip(parts, outs):
            if spill_at is None:
                continue
            for k in range(1, count):
                spill = aux_ref[k - 1].astype(F32)[spill_at : spill_at + SPILL_ROWS]
                old = out_ref[k, :top].astype(F32)
                new = old[:SPILL_ROWS] + spill
                if top > SPILL_ROWS:
                    new = jnp.concatenate([new, old[SPILL_ROWS:]], axis=0)
                out_ref[k, :top] = new.astype(LOW)

    out_shape = [jax.ShapeDtypeStruct((count, rows, H), LOW)] * len(parts)
    if carries:
        out_shape.append(jax.ShapeDtypeStruct((count, AUX_ROWS, H), LOW))
    extra = [] if carries else [aux]
    result = pl.pallas_call(
        kernel,
        out_shape=out_shape,
        in_specs=[SMEM] + [VMEM] * (len(extra) + len(sources)),
        out_specs=[VMEM] * len(out_shape),
        compiler_params=PARAMS,
        name="place",
    )(index, *extra, *sources)
    return [value.reshape(H, H) for value in result[: len(parts)]] + list(result[len(parts) :])


def split(index, value, masks, kinds, groups, by_z):
    def kernel(index_ref, value_ref, *out_refs):
        for ref, row, kind in zip(out_refs, masks, kinds):
            for j, mask in enumerate(row):
                ref[j] = value_ref[owner(index_ref[0], mask, groups, by_z)].astype(kind)

    shape = value.shape[1:]
    return pl.pallas_call(
        kernel,
        out_shape=[
            jax.ShapeDtypeStruct((len(row),) + shape, kind) for row, kind in zip(masks, kinds)
        ],
        in_specs=[SMEM, VMEM],
        out_specs=[VMEM] * len(masks),
        compiler_params=PARAMS,
        name="split",
    )(index, value)


def halves(groups):
    z_masks, plane_masks, core_masks = (masks_of(groups[g]) for g in ("z", "plane", "core"))
    inner = [p ^ z for p in plane_masks for z in z_masks]
    return [[core ^ m for m in inner] for core in core_masks]


def kinds_of(groups):
    return [F32] + [LOW] * (len(halves(groups)) - 1)


def adder(name, body, ins, outs, after):
    def kernel(*refs):
        body(refs[: len(ins)], refs[len(ins) + len(after) :])

    result = pl.pallas_call(
        kernel,
        out_shape=outs,
        in_specs=[VMEM] * len(ins) + [pl.BlockSpec(memory_space=pl.ANY)] * len(after),
        out_specs=[VMEM] * len(outs),
        compiler_params=PARAMS,
        name=name,
    )(*ins, *after)
    return list(result)


def core_stage(stacks, groups, count, after=()):
    z_count, plane_count = len(masks_of(groups["z"])), len(masks_of(groups["plane"]))
    cores = masks_of(groups["core"])[1:]
    gotten = [swap(stack, core, count) for core, stack in zip(cores, stacks[1:])]
    shape = (z_count,) + stacks[0].shape[1:]

    def body(ins, outs):
        for p, out_ref in enumerate(outs):
            for z in range(z_count):
                total = ins[0][p * z_count + z]
                for ref in ins[1:]:
                    total = total + ref[p * z_count + z].astype(F32)
                out_ref[z] = total.astype(out_ref.dtype)

    outs = [jax.ShapeDtypeStruct(shape, F32 if p == 0 else LOW) for p in range(plane_count)]
    return adder("core_sum", body, [stacks[0]] + gotten, outs, after)


def plane_swaps(parts, groups, count):
    masks = masks_of(groups["plane"])[1:]
    return [parts[0]] + [swap(part, mask, count) for mask, part in zip(masks, parts[1:])]


def plane_stage(parts, groups, count, after=()):
    def body(ins, outs):
        for z in range(ins[0].shape[0]):
            total = ins[0][z]
            for ref in ins[1:]:
                total = total + ref[z].astype(F32)
            outs[0][z] = total

    outs = [jax.ShapeDtypeStruct(parts[0].shape, F32)]
    return adder("plane_sum", body, plane_swaps(parts, groups, count), outs, after)[0]


def plane_stage_z(parts, groups, count, after=()):
    def body(ins, outs):
        for z, out_ref in enumerate(outs):
            total = ins[0][z]
            for ref in ins[1:]:
                total = total + ref[z].astype(F32)
            out_ref[...] = total.astype(out_ref.dtype)

    many, rows, width = parts[0].shape
    outs = [jax.ShapeDtypeStruct((rows, width), F32 if z == 0 else LOW) for z in range(many)]
    return adder("plane_sum", body, plane_swaps(parts, groups, count), outs, after)


def z_stage(parts, groups, count):
    own = parts[0]
    for mask, part in zip(masks_of(groups["z"])[1:], parts[1:]):
        own = own + swap(part, mask, count).astype(F32)
    return own


def z_scatter(total, groups, count):
    if not groups["z"]:
        return total[0]
    return lax.psum_scatter(
        total, AXES, scatter_dimension=0, axis_index_groups=teams(groups["z"], count)
    )


def product(left, right):
    return lax.dot_general(left, right, (((1,), (0,)), ((), ())), preferred_element_type=F32)


def outer(left, right):
    return lax.dot_general(left, right, (((1,), (1,)), ((), ())), preferred_element_type=F32)


def gelu_both(value):
    scale = math.sqrt(2.0 / math.pi)
    square = value * value
    share = 0.5 + 0.5 * jnp.tanh(value * (scale + scale * 0.044715 * square))
    result = value * share
    slope = share + result * (1.0 - share) * (2.0 * scale + 6.0 * scale * 0.044715 * square)
    return result, slope


def columns(height, tile=TILE):
    return pl.BlockSpec((height, tile), lambda i: (0, i))


def whole(*shape):
    return pl.BlockSpec(shape, lambda i: (0,) * len(shape))


def once(*shape):
    return pl.BlockSpec(shape, lambda i: (0,) * len(shape), pipeline_mode=pl.Buffered(1))


def shaped(kind, *shape):
    return jax.ShapeDtypeStruct(shape, kind)


def pieces_of(width):
    return [(a, a + 256) for a in range(0, width, 256)]


def run(name, kernel, batch, in_specs, out_specs, out_shape, scratch, flops, *args, tile=TILE):
    moved = sum(a.size * a.dtype.itemsize for a in args)
    moved += sum(math.prod(o.shape) * o.dtype.itemsize for o in out_shape)
    return pl.pallas_call(
        kernel,
        grid=(batch // tile,),
        in_specs=in_specs,
        out_specs=out_specs,
        out_shape=out_shape,
        scratch_shapes=scratch,
        compiler_params=PARAMS,
        cost_estimate=pl.CostEstimate(flops=flops, bytes_accessed=moved, transcendentals=0),
        name=name,
    )(*args)


def first_step():
    return pl.when(pl.program_id(0) == 0)


def last_step():
    return pl.when(pl.program_id(0) == pl.num_programs(0) - 1)


def turn(out_ref, matrix_ref, tail_ref=None, edge_ref=None):
    for a, b in pieces_of(H):
        out_ref[a:b, :H] = matrix_ref[:, a:b].T
    if tail_ref is not None:
        out_ref[:H, H:] = tail_ref[...].T
    if edge_ref is not None:
        out_ref[H:, :] = edge_ref[...]


def straight(out_ref, matrix_ref, tail_ref, edge_ref=None):
    out_ref[:H, :H] = matrix_ref[...]
    row = lax.broadcasted_iota(jnp.int32, (TALL - H, H), 0)
    tail = tail_ref[: TALL - H, :].astype(F32)
    out_ref[H:, :H] = jnp.where(row < EXTRA, tail, 0.0).astype(LOW)
    if edge_ref is not None:
        lane = lax.broadcasted_iota(jnp.int32, (TALL - H, WIDE), 1)
        edge = jnp.where(lane < D, edge_ref[...].astype(F32), 0.0)
        edge = jnp.concatenate([edge, jnp.zeros((LANES - (TALL - H), WIDE), F32)])
        out_ref[:, H:] = edge.T[:TALL].astype(LOW)


def widen(out_ref, value_ref):
    @first_step()
    def _():
        out_ref[TALL:] = jnp.zeros((WIDE - TALL, out_ref.shape[1]), LOW)

    out_ref[:TALL] = value_ref[...]


class Spread:
    def __init__(self, groups, rows, count, parts=1, below=False, by_z=False):
        self.groups, self.by_z = groups, by_z
        self.masks = halves(groups)
        self.kinds = kinds_of(groups)
        self.rows, self.count, self.parts, self.below = rows, count, parts, below
        self.direct = rows % 16 == 0

    def shapes(self):
        if not self.direct:
            return [shaped(F32, TALL, H)] * self.parts
        height = self.rows * self.parts + (AUX_ROWS if self.below else 0)
        outs = [shaped(kind, len(row), height, H) for row, kind in zip(self.masks, self.kinds)]
        overs = 0 if self.below else self.parts
        return outs + [shaped(F32, self.count, 8, H)] * overs

    def specs(self):
        return [whole(*s.shape) for s in self.shapes()]

    def write(self, acc_refs, index_ref, out_refs, over_refs=None):
        if not self.direct:
            for acc_ref, ref in zip(acc_refs, out_refs):
                ref[...] = acc_ref[...]
            return
        rows = self.rows
        for ref, row, kind in zip(out_refs, self.masks, self.kinds):
            for j, mask in enumerate(row):
                at = owner(index_ref[0], mask, self.groups, self.by_z)
                start = pl.multiple_of(at * rows, rows)
                for i, acc_ref in enumerate(acc_refs):
                    block = acc_ref[pl.ds(start, rows), :]
                    ref[j, i * rows : (i + 1) * rows] = block.astype(kind)
                if self.below:
                    mine = acc_ref[pl.ds(pl.multiple_of(start + rows, 8), 8), :]
                    parts = [mine[:SPILL_ROWS]] + [v[at][:SPILL_ROWS] for v in over_refs]
                    parts.append(jnp.zeros((AUX_ROWS - MISC_ROW, H), F32))
                    ref[j, rows:] = jnp.concatenate(parts).astype(kind)
        if not self.below:
            for acc_ref, ref in zip(acc_refs, out_refs[len(self.masks) :]):
                for k in range(self.count):
                    ref[k] = acc_ref[(k + 1) * rows : (k + 1) * rows + 8, :]

    def finish(self, outs, index, overs=None):
        if self.direct:
            return list(outs)
        rows, count = self.rows, self.count
        blocks = [grad[:H].reshape(count, rows, H) for grad in outs]
        own = [
            jnp.stack([grad[(k + 1) * rows : (k + 1) * rows + 8] for k in range(count)])
            for grad in outs
        ]
        if self.below:
            blocks += [v[:, :SPILL_ROWS] for v in own + list(overs)]
            blocks.append(jnp.zeros((count, AUX_ROWS - MISC_ROW, H), F32))
        stacks = split(
            index, jnp.concatenate(blocks, axis=1), self.masks, self.kinds, self.groups, self.by_z
        )
        stacks = list(stacks)
        return stacks if self.below else stacks + own


ANY = pl.BlockSpec(memory_space=pl.ANY)
REST = TALL - H


def forward_cross(features, one, two):
    batch = features.shape[1]

    def kernel(f_ref, *refs):
        x_ref, mixer_one_ref, mixer_two_ref, one_ref, two_ref = refs[6:11]
        turned_one, turned_two, wide_ref = refs[11:]

        @first_step()
        def _():
            turn(turned_one, *refs[:3])
            turn(turned_two, *refs[3:6])

        x_ref[:H] = f_ref[:H]
        last = f_ref[H:].astype(F32)
        last = jnp.concatenate([last, jnp.ones((1, TILE), F32), jnp.zeros((TALL - D - 1, TILE), F32)])
        x_ref[H:] = last.astype(LOW)
        widen(wide_ref, x_ref)
        layers = []
        for a, b in [(0, TILE)]:
            mixer = product(turned_one[...], wide_ref[:, a:b])
            mixer_one_ref[:, a:b] = mixer.astype(LOW)
            part = x_ref[:, a:b].astype(F32)
            layer = part * mixer + part
            layers.append(layer)
            one_ref[:, a:b] = layer.astype(LOW)
        wide_ref[:TALL] = one_ref[...]
        for (a, b), layer in zip([(0, TILE)], layers):
            mixer = product(turned_two[...], wide_ref[:, a:b])
            mixer_two_ref[:, a:b] = mixer.astype(LOW)
            two_ref[:, a:b] = (x_ref[:, a:b].astype(F32) * mixer + layer).astype(LOW)

    return run(
        "forward_cross",
        kernel,
        batch,
        [columns(D)] + [once(H, H), once(LANES, H), once(REST, WIDE)] * 2,
        [columns(TALL)] * 5,
        [shaped(LOW, TALL, batch)] * 5,
        [pltpu.VMEM((TALL, WIDE), LOW)] * 2 + [pltpu.VMEM((WIDE, TILE), LOW)],
        4 * batch * TALL * TALL,
        features, *one, *two,
    )


def deep(spread, index, layer_low, examples, matrix_one, tail, matrix, lines, inverse):
    batch = layer_low.shape[1]
    days = inverse.shape[0]

    def kernel(k_ref, l_ref, x_ref, w_one_ref, t_ref, w_ref, n_ref, i_ref, *refs):
        logit_ref, back_ref, line_ref, sum_ref = refs[:4]
        out_refs = refs[4:-8]
        turned_one, turned, acc_ref, hidden_ref, slope_ref, low_ref, part_ref, wide_ref = refs[-8:]

        @first_step()
        def _():
            turn(turned_one, w_one_ref, t_ref)
            turn(turned, w_ref)
            acc_ref[...] = jnp.zeros_like(acc_ref)
            sum_ref[...] = jnp.zeros_like(sum_ref)
            part_ref[...] = jnp.zeros_like(part_ref)
            row = lax.broadcasted_iota(jnp.int32, (REST, TILE), 0)
            hidden_ref[H:] = jnp.where(row == 0, 1.0, 0.0).astype(LOW)

        widen(wide_ref, l_ref)
        for a, b in pieces_of(TILE):
            hidden, slope = gelu_both(product(turned_one[...], wide_ref[:, a:b]))
            hidden_ref[:H, a:b] = hidden.astype(LOW)
            slope_ref[:, a:b] = slope
        head = n_ref[:, 1:2]
        for a, b in pieces_of(TILE):
            two, slope = gelu_both(product(turned[...], hidden_ref[:H, a:b]) + n_ref[:, 0:1])
            two = two.astype(LOW).astype(F32)
            logits = n_ref[0:1, 2:3] + jnp.sum(two * head, axis=0, keepdims=True)
            label = x_ref[0:1, a:b]
            day = x_ref[1:2, a:b].astype(jnp.int32)
            row = lax.broadcasted_iota(jnp.int32, (days, b - a), 0)
            weight = jnp.sum(jnp.where(row == day, i_ref[:, 0:1], 0.0), axis=0, keepdims=True)
            decay = jnp.exp(-jnp.abs(logits))
            entropy = jnp.maximum(logits, 0.0) + jnp.log1p(decay) - label * logits
            chance = jnp.where(logits >= 0.0, 1.0, decay) / (1.0 + decay)
            logit_grad = (chance - label) * weight
            logit_ref[:, a:b] = logits
            sum_ref[0:1, a:b] += logit_grad
            sum_ref[1:2, a:b] += entropy * weight
            low_ref[:, a:b] = ((logit_grad * head) * slope).astype(LOW)
            one = logit_grad * two
            part = one[:, :LANES]
            for at in range(LANES, b - a, LANES):
                part = part + one[:, at : at + LANES]
            part_ref[...] += part
        for a, b in pieces_of(TILE):
            back_ref[:, a:b] = (product(w_ref[...], low_ref[:, a:b]) * slope_ref[:, a:b]).astype(LOW)
        for a, b in pieces_of(H):
            acc_ref[:, a:b] += outer(hidden_ref[...], low_ref[a:b])

        @last_step()
        def _():
            line_ref[0:8] = jnp.broadcast_to(
                jnp.sum(part_ref[...].T, axis=0, keepdims=True), (8, H)
            )
            line_ref[8:16] = acc_ref[H : H + 8]
            spread.write([acc_ref], k_ref, out_refs)

    return run(
        "deep",
        kernel,
        batch,
        [
            SMEM,
            columns(TALL),
            columns(2),
            once(H, H),
            once(LANES, H),
            once(H, H),
            whole(H, LANES),
            whole(days, LANES),
        ],
        [columns(1), columns(H), whole(16, H), whole(8, TILE)] + spread.specs(),
        [
            shaped(F32, 1, batch),
            shaped(LOW, H, batch),
            shaped(F32, 16, H),
            shaped(F32, 8, TILE),
        ]
        + spread.shapes(),
        [
            pltpu.VMEM((H, WIDE), LOW),
            pltpu.VMEM((H, H), LOW),
            pltpu.VMEM((TALL, H), F32),
            pltpu.VMEM((TALL, TILE), LOW),
            pltpu.VMEM((H, TILE), F32),
            pltpu.VMEM((H, TILE), LOW),
            pltpu.VMEM((H, LANES), F32),
            pltpu.VMEM((WIDE, TILE), LOW),
        ],
        8 * batch * H * H,
        index, layer_low, examples, matrix_one, tail, matrix, lines, inverse,
    )


def back_deep(spread, index, grad_low, layer_low, features, matrix, tail, after):
    batch = features.shape[1]

    def kernel(k_ref, g_ref, l_ref, x_ref, w_ref, t_ref, *refs):
        refs = refs[len(after) :]
        layer_ref, mixer_ref, line_ref = refs[:3]
        out_refs = refs[3:-2]
        held, acc_ref = refs[-2:]

        @first_step()
        def _():
            straight(held, w_ref, t_ref)
            acc_ref[...] = jnp.zeros_like(acc_ref)

        for a, b in pieces_of(TILE):
            layer = product(held[...], g_ref[:, a:b])
            layer_ref[:, a:b] = layer
            mixer_ref[:, a:b] = (layer * x_ref[:, a:b].astype(F32)).astype(LOW)
        for a, b in pieces_of(H):
            acc_ref[:, a:b] += outer(l_ref[...], g_ref[a:b])

        @last_step()
        def _():
            line_ref[...] = acc_ref[H:]
            spread.write([acc_ref], k_ref, out_refs)

    return run(
        "back_deep",
        kernel,
        batch,
        [SMEM, columns(H), columns(TALL), columns(TALL), once(H, H), once(LANES, H)]
        + [ANY] * len(after),
        [columns(TALL), columns(TALL), whole(REST, H)] + spread.specs(),
        [shaped(F32, TALL, batch), shaped(LOW, TALL, batch), shaped(F32, REST, H)]
        + spread.shapes(),
        [pltpu.VMEM((TALL, H), LOW), pltpu.VMEM((TALL, H), F32)],
        4 * batch * TALL * H,
        index, grad_low, layer_low, features, matrix, tail, *after,
    )


def back_two(
    spread, index, mixer_low, layer_low, layer_grad, features, mixer_one, mixer_two, matrix, tail,
    edge, lines, after,
):
    batch = features.shape[1]

    def kernel(k_ref, g_ref, l_ref, d_ref, x_ref, one_ref, two_ref, w_ref, t_ref, e_ref, *refs):
        top_ref, deep_ref, sums_ref = refs[:3]
        refs = refs[3 + len(after) :]
        part_ref, mixer_ref, vector_ref = refs[:3]
        out_refs = refs[3:-6]
        held, acc_ref, wide_ref, sum_ref, side_ref, next_side_ref = refs[-6:]

        @first_step()
        def _():
            straight(held, w_ref, t_ref, e_ref)
            acc_ref[...] = jnp.zeros_like(acc_ref)
            side_ref[...] = jnp.zeros_like(side_ref)
            next_side_ref[...] = jnp.zeros_like(next_side_ref)
            sum_ref[...] = jnp.zeros_like(sum_ref)

        widen(wide_ref, g_ref)
        for a, b in pieces_of(TILE):
            above = d_ref[:, a:b]
            layer = product(held[...], wide_ref[:, a:b]) + above
            mixer = (layer * x_ref[:, a:b].astype(F32)).astype(LOW)
            mixer_ref[:, a:b] = mixer
            mixer = mixer[:H].astype(F32)
            total = mixer[:, :LANES]
            for at in range(LANES, b - a, LANES):
                total = total + mixer[:, at : at + LANES]
            sum_ref[...] += total
            part = above * two_ref[:, a:b].astype(F32)
            part = part + layer * (one_ref[:, a:b].astype(F32) + 1.0)
            part_ref[:, a:b] = part.astype(LOW)
        for a, b in pieces_of(H):
            acc_ref[:, a:b] += outer(l_ref[...], g_ref[a:b])
        side_ref[...] += outer(g_ref[H:], l_ref[...])
        next_side_ref[...] += outer(mixer_ref[H:], x_ref[...])

        @last_step()
        def _():
            vector_ref[...] = jnp.zeros_like(vector_ref)
            vector_ref[0:1, :H] = jnp.sum(sum_ref[...].T, axis=0, keepdims=True)
            vector_ref[1:2, :H] = acc_ref[D : D + 1]
            vector_ref[2:3, :H] = deep_ref[EXTRA : EXTRA + 1]
            vector_ref[3:4, :H] = top_ref[8:9]
            vector_ref[4:5, :H] = top_ref[0:1]
            vector_ref[5:8, :TALL] = next_side_ref[:EXTRA]
            vector_ref[8:11, :TALL] = side_ref[:EXTRA]
            lane = lax.broadcasted_iota(jnp.int32, (1, LANES), 1)
            bias = jnp.sum(sums_ref[0:1], axis=1, keepdims=True)
            loss = jnp.sum(sums_ref[1:2], axis=1, keepdims=True)
            vector_ref[11:12, :LANES] = jnp.where(lane == 0, bias, jnp.where(lane == 1, loss, 0.0))
            spread.write([acc_ref], k_ref, out_refs)

    return run(
        "back_two",
        kernel,
        batch,
        [SMEM]
        + [columns(TALL)] * 6
        + [once(H, H), once(LANES, H), once(REST, WIDE)]
        + [whole(*v.shape) for v in lines]
        + [ANY] * len(after),
        [columns(TALL), columns(TALL)]
        + [whole(16, WIDE)]
        + spread.specs(),
        [
            shaped(LOW, TALL, batch),
            shaped(LOW, TALL, batch),
            shaped(F32, 16, WIDE),
        ]
        + spread.shapes(),
        [
            pltpu.VMEM((TALL, WIDE), LOW),
            pltpu.VMEM((TALL, H), F32),
            pltpu.VMEM((WIDE, TILE), LOW),
            pltpu.VMEM((H, LANES), F32),
            pltpu.VMEM((REST, TALL), F32),
            pltpu.VMEM((REST, TALL), F32),
        ],
        4 * batch * TALL * TALL,
        index, mixer_low, layer_low, layer_grad, features, mixer_one, mixer_two, matrix, tail,
        edge, *lines, *after,
    )


def grad_one(spread, index, mixer_low, features, overs, after):
    batch = features.shape[1]

    def kernel(k_ref, g_ref, x_ref, *refs):
        over_refs = refs[: len(overs)]
        out_refs = refs[len(overs) + len(after) : -1]
        acc_ref = refs[-1]

        @first_step()
        def _():
            acc_ref[...] = jnp.zeros_like(acc_ref)

        for a, b in pieces_of(H):
            acc_ref[:, a:b] += outer(x_ref[...], g_ref[a:b])

        @last_step()
        def _():
            spread.write([acc_ref], k_ref, out_refs, over_refs)

    return run(
        "grad_one",
        kernel,
        batch,
        [SMEM, columns(TALL), columns(TALL)]
        + [once(*v.shape) for v in overs]
        + [ANY] * len(after),
        spread.specs(),
        spread.shapes(),
        [pltpu.VMEM((TALL, H), F32)],
        2 * batch * TALL * TALL,
        index, mixer_low, features, *overs, *after,
    )


def back_one(mixer_low, part, matrix, tail, edge, after):
    batch = part.shape[1]

    def kernel(g_ref, p_ref, w_ref, t_ref, e_ref, *refs):
        out_ref, held, wide_ref = refs[len(after) :]

        @first_step()
        def _():
            straight(held, w_ref, t_ref, e_ref)

        widen(wide_ref, g_ref)
        for a, b in [(0, TILE)]:
            value = p_ref[:, a:b].astype(F32) + product(held[...], wide_ref[:, a:b])
            out_ref[:H, a:b] = value[:H]
            out_ref[H:, a:b] = value[H:D]

    return run(
        "back_one",
        kernel,
        batch,
        [columns(TALL), columns(TALL), whole(H, H), whole(LANES, H), whole(REST, WIDE)]
        + [ANY] * len(after),
        [columns(D)],
        [shaped(F32, D, batch)],
        [pltpu.VMEM((TALL, WIDE), LOW), pltpu.VMEM((WIDE, TILE), LOW)],
        2 * batch * TALL * TALL,
        mixer_low, part, matrix, tail, edge, *after,
    )[0]


def local(groups, features, labels, days, master, moment_one, moment_two):
    count = lax.axis_size(AXES)
    index = lax.axis_index(AXES)
    slot = index[None].astype(jnp.int32)
    rows = H // count
    starts = starts_of(count)
    sizes = piece_sizes(count)
    wide_piece = sizes[1]
    piece = [master[a : a + l] for a, l in zip(starts, sizes)]
    block_one = to_block(piece[0], index, D, rows, count)
    block_two = to_block(piece[2], index, D, rows, count)
    block_deep = to_block(piece[4], index, H, rows, count)

    day_hot = (days[:, None] == jnp.arange(DAYS, dtype=jnp.int32)[None, :]).astype(F32)
    own_counts = jnp.sum(day_hot, axis=0)
    counts_high = jnp.floor(own_counts / 64.0)
    counts_low = own_counts - 64.0 * counts_high

    def spill_side(block):
        side = block[rows:, H:].T
        return jnp.pad(side, ((0, 0), (0, rows - SPILL_ROWS)))

    misc = [
        piece[5],
        piece[7],
        piece[8],
        block_one[:rows, H:].T,
        block_two[:rows, H:].T,
        spill_side(block_one),
        spill_side(block_two),
        piece[1],
        piece[3],
        piece[9],
        counts_high,
        counts_low,
    ]
    misc = jnp.concatenate([part.reshape(-1) for part in misc])
    misc = jnp.pad(misc, (0, (AUX_ROWS - MISC_ROW) * H - misc.shape[0])).reshape(-1, H)
    first = jnp.concatenate(
        [
            block_one[:rows, :H],
            block_two[:rows, :H],
            block_one[rows:, :H],
            block_two[rows:, :H],
            block_deep[rows:],
            misc,
        ]
    ).astype(LOW)
    stacks_cross = gather(first, groups, count)
    rest = jnp.concatenate([block_deep[:rows], piece[6].reshape(rows, H)]).astype(LOW)
    crossed = [value for value, _ in stacks_cross[3:5]]
    stacks_rest = gather(rest, groups, count, direct=True, after=crossed)
    examples = jnp.stack([labels.astype(F32), days.astype(F32)])

    matrix_one, matrix_two, aux = place(slot, stacks_cross, rows, count, [0, SPILL_ROWS])
    matrix_deep, matrix_top = place(slot, stacks_rest, rows, count, [2 * SPILL_ROWS, None], aux)

    line = aux[:, MISC_ROW]
    at = UNIT_LINES * rows
    units = line[:, :at].reshape(count, UNIT_LINES, rows).transpose(1, 0, 2).reshape(UNIT_LINES, H)
    biases = line[:, at : at + 2 * wide_piece].reshape(count, 2, wide_piece)
    biases = biases.transpose(1, 0, 2).reshape(2, count * wide_piece)
    at += 2 * wide_piece
    head_bias = line[0, at]
    both_counts = jnp.sum(line[:, at + 1 : at + 1 + 2 * DAYS].astype(F32), axis=0)
    counts = 64.0 * both_counts[:DAYS] + both_counts[DAYS:]
    inverse = jnp.broadcast_to((1.0 / counts)[:, None], (DAYS, LANES))
    sides = jnp.pad(units[3:9], ((0, 0), (0, LANES))) + jnp.pad(
        units[9:15], ((0, 0), (rows, LANES - rows))
    )

    def tail_of(at, bias):
        return jnp.concatenate(
            [aux[count - 1, at : at + EXTRA], bias[None, :H], jnp.zeros((LANES - EXTRA - 1, H), LOW)]
        )

    def edge_of(side, bias):
        lane = lax.broadcasted_iota(jnp.int32, side.shape, 1)
        side = jnp.where(lane == D, bias[H:D, None], side)
        return jnp.pad(side, ((0, TALL - H - EXTRA), (0, 0)))

    tail_one, edge_one = tail_of(0, biases[0]), edge_of(sides[:3], biases[0])
    tail_two, edge_two = tail_of(SPILL_ROWS, biases[1]), edge_of(sides[3:], biases[1])
    tail_deep = tail_of(2 * SPILL_ROWS, units[0])
    lines = jnp.concatenate(
        [units[1:3], jnp.full((1, H), head_bias), jnp.zeros((LANES - 3, H), LOW)]
    )
    lines = lines.astype(F32).T
    spread = Spread(groups, rows, count, by_z=True)
    spread_last = Spread(groups, rows, count, below=True)

    wide_features, mixer_one, mixer_two, low_one, low_two = forward_cross(
        features.T, (matrix_one, tail_one, edge_one), (matrix_two, tail_two, edge_two)
    )
    logits, pre_one_low, top_lines, sums, *outs = deep(
        spread, slot, low_two, examples, matrix_deep, tail_deep, matrix_top, lines, inverse
    )
    *top_stacks, _ = spread.finish(outs, slot)
    layer_grad, mixer_two_low, deep_lines, *outs = back_deep(
        spread, slot, pre_one_low, low_two, wide_features, matrix_deep, tail_deep, []
    )
    *deep_stacks, deep_over = spread.finish(outs, slot)
    top_plane = core_stage(top_stacks, groups, count, [mixer_two_low])
    part, mixer_one_low, vectors, *outs = back_two(
        spread, slot, mixer_two_low, low_one, layer_grad, wide_features, mixer_one, mixer_two,
        matrix_two, tail_two, edge_two, (top_lines, deep_lines, sums), top_plane[1:],
    )
    *two_stacks, two_over = spread.finish(outs, slot)
    top_total = plane_stage(top_plane, groups, count, [mixer_one_low])
    deep_plane = core_stage(deep_stacks, groups, count, [mixer_one_low])
    overs = (two_over, deep_over)
    outs = grad_one(
        spread_last, slot, mixer_one_low, wide_features, overs,
        deep_plane[1:] + [top_total],
    )
    last_stacks = spread_last.finish(outs, slot, overs)
    deep_total = plane_stage(deep_plane, groups, count, last_stacks[:1])
    two_plane = core_stage(two_stacks, groups, count, last_stacks[:1])
    last_plane = core_stage(last_stacks, groups, count)
    feature_grad = back_one(
        mixer_one_low, part, matrix_one, tail_one, edge_one,
        last_plane[1:] + two_plane[1:] + [deep_total],
    )

    vectors = jnp.sum(lax.all_gather(vectors, AXES, axis=0), axis=0)
    loss = vectors[11, 1]
    side_sums = vectors[5:11]

    own_top = z_scatter(top_total, groups, count)
    own_deep = z_scatter(deep_total, groups, count)
    two_total = plane_stage(two_plane, groups, count, [feature_grad])
    own_two = z_scatter(two_total, groups, count)
    own_last = z_stage(plane_stage_z(last_plane, groups, count, [feature_grad]), groups, count)
    own_one = own_last[:rows]
    spills = own_last[rows : rows + MISC_ROW]
    row = lax.broadcasted_iota(jnp.int32, spills.shape, 0)
    beyond = (row % SPILL_ROWS >= EXTRA) & (index == count - 1)
    spills = jnp.where(beyond, 0.0, spills)
    wide_biases = jnp.concatenate(
        [vectors[:2, :H], side_sums[:, D].reshape(2, EXTRA)], axis=1
    )
    wide_biases = jnp.pad(wide_biases, ((0, 0), (0, count * wide_piece - D)))
    wide_biases = lax.dynamic_slice(wide_biases, (0, index * wide_piece), (2, wide_piece))
    units = lax.dynamic_slice(vectors[2:5], (0, index * rows), (3, rows))
    side_sums = jnp.pad(side_sums[:, :D], ((0, 0), (0, WIDE - D)))
    side_sums = lax.dynamic_slice(side_sums, (0, index * rows), (6, rows + SPILL_ROWS)).T

    def whole_block(main, number):
        low = number * SPILL_ROWS
        body = jnp.concatenate([main, spills[low : low + SPILL_ROWS]])
        if number == 2:
            return body
        return jnp.concatenate([body, side_sums[:, 3 * number : 3 * number + 3]], axis=1)

    flat_grad = jnp.concatenate(
        [
            from_block(whole_block(own_one, 0), index, sizes[0], rows, count),
            wide_biases[0],
            from_block(whole_block(own_two, 1), index, sizes[2], rows, count),
            wide_biases[1],
            from_block(whole_block(own_deep, 2), index, sizes[4], rows, count),
            units[0],
            own_top.reshape(-1),
            units[1],
            units[2],
            jnp.where(index == 0, vectors[11, :1], 0.0),
        ]
    )
    new_moment_one = 0.9 * moment_one + 0.1 * flat_grad
    new_moment_two = 0.999 * moment_two + 0.001 * flat_grad * flat_grad
    corrected_one = new_moment_one / (1.0 - 0.9**STEP)
    corrected_two = new_moment_two / (1.0 - 0.999**STEP)
    new_master = master - 0.03 * (corrected_one / (jnp.sqrt(corrected_two) + 1e-08) + 0.01 * master)
    new_bias = jnp.concatenate(
        [new_master[starts[i] : starts[i] + sizes[i]] for i in (1, 3, 5, 7, 9)]
    )
    return (
        logits.reshape(-1),
        loss,
        feature_grad.T,
        flat_grad,
        new_moment_one,
        new_moment_two,
        new_master,
        new_bias,
    )


def solution(mesh):
    line = P(AXES)
    table = P(AXES, None)
    groups = bit_groups(mesh)
    return jax.shard_map(
        functools.partial(local, groups),
        mesh=mesh,
        in_specs=(table, line, line, line, line, line),
        out_specs=(line, P(), table, line, line, line, line, line),
        check_vma=False,
    )
```

profile of v0, /device:TPU:0, one launch (start us, length us, event | category | flops | bytes accessed | tf_op | source)
XLA Modules:
  0.0 313.7 jit_solution(13678245378226294798)
XLA Ops:
  16.9 5.1 %collective-permute-start.2 = (bf16[80,1024]{1,0:T(8,128)(2,1)S(1)}, bf16[80,1024]{1,0:T(8,128)(2,1)S(1)}, u32[]{:S(2)}, u32[]{:S(2)}) collective-permute-start(bf16[80,1024]{1,0:T(8,128)(2,1)S(1)} %concatenate.78), channel_id=1, source_target_pairs={{0,24},{1,25},{2,26},{3,27},{4,28},{5,29},{6,30},{7,31},{8,16},{9,... | collective-permute-start | bytes 491528 | tf_op jit(solution)/shard_map/ppermute | solution.py:106
  23.8 3.3 %collective-permute-done.2 = bf16[80,1024]{1,0:T(8,128)(2,1)S(1)} collective-permute-done((bf16[80,1024]{1,0:T(8,128)(2,1)S(1)}, bf16[80,1024]{1,0:T(8,128)(2,1)S(1)}, u32[]{:S(2)}, u32[]{:S(2)}) %collective-permute-start.2) | collective-permute-done | bytes 163872 | tf_op jit(solution)/shard_map/ppermute | solution.py:106
  27.1 8.8 %collective-permute-done.1 = bf16[80,1024]{1,0:T(8,128)(2,1)S(1)} collective-permute-done((bf16[80,1024]{1,0:T(8,128)(2,1)S(1)}, bf16[80,1024]{1,0:T(8,128)(2,1)S(1)}, u32[]{:S(2)}, u32[]{:S(2)}) %collective-permute-start.1) | collective-permute-done | bytes 163872 | tf_op jit(solution)/shard_map/ppermute | solution.py:106
  36.0 1.6 collective-permute-start.3
  37.6 1.5 collective-permute-start.4
  39.4 3.0 collective-permute-start.13
  42.4 1.3 collective-permute-start.14
  43.8 8.1 %collective-permute-done.3.refs_1_ = bf16[4,80,1024]{2,1,0:T(8,128)(2,1)S(1)} collective-permute-done((bf16[4,80,1024]{2,1,0:T(8,128)(2,1)S(1)}, bf16[4,80,1024]{2,1,0:T(8,128)(2,1)S(1)}, u32[]{:S(2)}, u32[]{:S(2)}) %collective-permute-start.3) | collective-permute-done | bytes 655392 | tf_op jit(solution)/shard_map/ppermute | solution.py:106
  51.9 1.6 collective-permute-start.5
  53.5 1.6 collective-permute-start.6
  55.8 4.3 %collective-permute-done.5.refs_3_.refs_4_ = bf16[2,80,1024]{2,1,0:T(8,128)(2,1)S(1)} collective-permute-done((bf16[2,80,1024]{2,1,0:T(8,128)(2,1)S(1)}, bf16[2,80,1024]{2,1,0:T(8,128)(2,1)S(1)}, u32[]{:S(2)}, u32[]{:S(2)}) %collective-permute-start.5) | collective-permute-done | bytes 327712 | tf_op jit(solution)/shard_map/ppermute | solution.py:106
  61.8 1.9 join.1.refs_1_
  63.8 1.5 collective-permute-start.15
  65.9 1.4 collective-permute-start.17
  68.4 5.3 %place.2 = (bf16[32,32,1024]{2,1,0:T(8,128)(2,1)}, bf16[32,32,1024]{2,1,0:T(8,128)(2,1)}, bf16[32,16,1024]{2,1,0:T(8,128)(2,1)}) custom-call(s32[1]{0:T(128)} %bitcast.index_ref.k_ref, bf16[4,80,1024]{2,1,0:T(8,128)(2,1)} %copy-done, bf16[4,80,1024]{2,1,0:T(8,128)(2,1)} %copy-done.3, bf16[4,80,1024]{2,1,0:T(8,128)(2,1)} %copy-done.4, ...), custom_call_target="tpu_custom_call" | custom-call | tf_op jit(solution)/shard_map/place/pallas_call | solution.py:181
  80.8 18.1 %forward_cross.1 = (bf16[1040,2048]{1,0:T(8,128)(2,1)}, bf16[1040,2048]{1,0:T(8,128)(2,1)}, bf16[1040,2048]{1,0:T(8,128)(2,1)}, bf16[1040,2048]{1,0:T(8,128)(2,1)}, bf16[1040,2048]{1,0:T(8,128)(2,1)}) custom-call(bf16[1027,2048]{1,0:T(8,128)(2,1)} %bitcast.92, bf16[1024,1024]{1,0:T(8,128)(2,1)} %bitcast.70, ...), custom_call_target="tpu_custom_call" | custom-call | flops 8860467200 | bytes 30298112 | tf_op jit(solution)/shard_map/forward_cross/pallas_call | solution.py:339
  103.2 4.7 %place.3 = (bf16[32,32,1024]{2,1,0:T(8,128)(2,1)}, bf16[32,32,1024]{2,1,0:T(8,128)(2,1)}) custom-call(s32[1]{0:T(128)} %bitcast.index_ref.k_ref, bf16[32,16,1024]{2,1,0:T(8,128)(2,1)} %get-tuple-element.59.refs_0_, bf16[4,64,1024]{2,1,0:T(8,128)(2,1)} %join.1.refs_1_, bf16[4,64,1024]{2,1,0:T(8,128)(2,1)} %copy-done.17, bf16[4,64,1024]{2,1,0:T(8,128)(2,1)} %copy-done.18, ...), custom_call_target="tpu_custom_call" | custom-call | tf_op jit(solution)/shard_map/place/pallas_call | solution.py:181
  108.6 33.8 %deep.1 = (f32[1,2048]{1,0:T(1,128)}, bf16[1024,2048]{1,0:T(8,128)(2,1)}, f32[16,1024]{1,0:T(8,128)}, f32[8,512]{1,0:T(8,128)}, f32[16,32,1024]{2,1,0:T(8,128)},...) custom-call(s32[1]{0:T(128)} %bitcast.index_ref.k_ref, bf16[1040,2048]{1,0:T(8,128)(2,1)} %get-tuple-element.61.l_ref, ...), custom_call_target="tpu_custom_call" | custom-call | flops 17179869184 | bytes 17747972 | tf_op jit(solution)/shard_map/deep/pallas_call | solution.py:339
  142.7 17.2 %back_deep.1 = (f32[1040,2048]{1,0:T(8,128)}, bf16[1040,2048]{1,0:T(8,128)(2,1)}, f32[16,1024]{1,0:T(8,128)}, f32[16,32,1024]{2,1,0:T(8,128)}, bf16[16,32,1024]{2,1,0:T(8,128)(2,1)}, /*index=5*/f32[32,8,1024]{2,1,0:T(8,128)}) custom-call(s32[1]{0:T(128)} %bitcast.index_ref.k_ref, bf16[1024,2048]{1,0:T(8,128)(2,1)} %get-tuple-element.65.g_ref, ...), custom_call_target="tpu_custom_call" | custom-call | flops 8724152320 | bytes 32112644 | tf_op jit(solution)/shard_map/back_deep/pallas_call | solution.py:339
  161.2 2.9 core_sum.4
  164.2 1.5 collective-permute-start.24
  166.3 1.4 collective-permute-start.26
  167.7 23.2 %back_two.1 = (bf16[1040,2048]{1,0:T(8,128)(2,1)}, bf16[1040,2048]{1,0:T(8,128)(2,1)}, f32[16,1152]{1,0:T(8,128)}, f32[16,32,1024]{2,1,0:T(8,128)}, bf16[16,32,1...) custom-call(s32[1]{0:T(128)} %bitcast.index_ref.k_ref, bf16[1040,2048]{1,0:T(8,128)(2,1)} %get-tuple-element.67.refs_2_.g_ref, ...), custom_call_target="tpu_custom_call" | custom-call | flops 8860467200 | bytes 45936644 | tf_op jit(solution)/shard_map/back_two/pallas_call | solution.py:339
  191.8 2.2 plane_sum.4.refs_5_
  195.1 2.9 core_sum.5
  198.0 1.5 collective-permute-start.29
  200.1 1.4 collective-permute-start.31
  201.5 10.6 %grad_one.1 = (f32[16,48,1024]{2,1,0:T(8,128)}, bf16[16,48,1024]{2,1,0:T(8,128)(2,1)}) custom-call(s32[1]{0:T(128)} %bitcast.index_ref.k_ref, bf16[1040,2048]{1,0:T(8,128)(2,1)} %get-tuple-element.81.refs_2_.refs_4_.g_ref, bf16[1040,2048]{1,0:T(8,128)(2,1)} %get-tuple-element.66.x_ref, f32[32,8,1024]{2,1,0:T(8,128)} %get-tuple-element.83.refs_0_, ...), custom_call_target="tpu_custom_call" | custom-call | flops 4430233600 | bytes 16646148 | tf_op jit(solution)/shard_map/grad_one/pallas_call | solution.py:339
  213.3 2.2 plane_sum.5.refs_6_
  216.7 4.4 %collective-permute-done.27.refs_1_ = bf16[16,48,1024]{2,1,0:T(8,128)(2,1)S(1)} collective-permute-done((bf16[16,48,1024]{2,1,0:T(8,128)(2,1)S(1)}, bf16[16,48,1024]{2,1,0:T(8,128)(2,1)S(1)}, u32[]{:S(2)}, u32[]{:S(2)}) %collective-permute-start.27) | collective-permute-done | bytes 1572896 | tf_op jit(solution)/shard_map/ppermute | solution.py:106
  222.2 3.7 %core_sum.6 = (f32[4,48,1024]{2,1,0:T(8,128)}, bf16[4,48,1024]{2,1,0:T(8,128)(2,1)}, bf16[4,48,1024]{2,1,0:T(8,128)(2,1)}, bf16[4,48,1024]{2,1,0:T(8,128)(2,1)}) custom-call(f32[16,48,1024]{2,1,0:T(8,128)} %get-tuple-element.91.refs_0_.refs_2_.refs_4_, bf16[16,48,1024]{2,1,0:T(8,128)(2,1)} %copy-done.2), custom_call_target="tpu_custom_call" | custom-call | tf_op jit(solution)/shard_map/core_sum/pallas_call | solution.py:225
  225.9 1.5 collective-permute-start.32
  228.5 3.0 core_sum.7
  233.1 1.8 collective-permute-start.40
  235.6 2.6 collective-permute-done.32.refs_1_
  238.2 1.6 collective-permute-start.34
  239.8 11.1 %back_one.1.refs_4_ = f32[1027,2048]{1,0:T(8,128)} custom-call(bf16[1040,2048]{1,0:T(8,128)(2,1)} %get-tuple-element.81.refs_2_.refs_4_.g_ref, bf16[1040,2048]{1,0:T(8,128)(2,1)} %get-tuple-element.82.p_ref, bf16[1024,1024]{1,0:T(8,128)(2,1)} %bitcast.71, bf16[128,1024]{1,0:T(8,128)(2,1)} %get-tuple-element.142.refs_1_.t_ref, ...), custom_call_target="tpu_custom_call" | custom-call | flops 4430233600 | bytes 21819392 | tf_op jit(solution)/shard_map/back_one/pallas_call | solution.py:339
  250.9 6.6 %collective-permute-done.33.refs_2_ = bf16[4,48,1024]{2,1,0:T(8,128)(2,1)S(1)} collective-permute-done((bf16[4,48,1024]{2,1,0:T(8,128)(2,1)S(1)}, bf16[4,48,1024]{2,1,0:T(8,128)(2,1)S(1)}, u32[]{:S(2)}, u32[]{:S(2)}) %collective-permute-start.33) | collective-permute-done | bytes 393248 | tf_op jit(solution)/shard_map/ppermute | solution.py:106
  257.6 8.5 %collective-permute-done.34.refs_3_ = bf16[4,48,1024]{2,1,0:T(8,128)(2,1)S(1)} collective-permute-done((bf16[4,48,1024]{2,1,0:T(8,128)(2,1)S(1)}, bf16[4,48,1024]{2,1,0:T(8,128)(2,1)S(1)}, u32[]{:S(2)}, u32[]{:S(2)}) %collective-permute-start.34) | collective-permute-done | bytes 393248 | tf_op jit(solution)/shard_map/ppermute | solution.py:106
  266.9 2.3 plane_sum.6
  269.2 1.6 collective-permute-start.37
  270.8 2.8 collective-permute-start.35
  275.3 2.2 plane_sum.7
  277.9 3.5 %collective-permute-done.36 = bf16[48,1024]{1,0:T(8,128)(2,1)S(1)} collective-permute-done((bf16[48,1024]{1,0:T(8,128)(2,1)}, bf16[48,1024]{1,0:T(8,128)(2,1)S(1)}, u32[]{:S(2)}, u32[]{:S(2)}) %collective-permute-start.36) | collective-permute-done | bytes 98336 | tf_op jit(solution)/shard_map/ppermute | solution.py:106
  282.9 1.8 reduce_sum.29
  286.2 11.6 %reduce-scatter.4.cloned.1.call-done = f32[1,32,1024]{2,1,0:T(8,128)} async-done(((f32[4,32,1024]{2,1,0:T(8,128)}), f32[1,32,1024]{2,1,0:T(8,128)}) %reduce-scatter.4.cloned.1.call-update) | async-done | bytes 131088 | tf_op jit(solution)/shard_map/reduce_scatter | solution.py:294
  299.8 3.4 %concatenate.90 = f32[131717]{0:T(1024)S(1)} concatenate(f32[32961]{0:T(1024)S(1)} %dynamic_slice.31, f32[33]{0:T(128)S(1)} %get-tuple-element.139, f32[32961]{0:T(1024)S(1)} %dynamic_slice.33, f32[33]{0:T(128)S(1)} %get-tuple-element.138, f32[32864]{0:T(1024)S(1)} %dynamic_slice.34, f32[32]{0:T(128)S(1)} %get-tuple-element.137, f32[32768]{0:T(1024)S(1)} %bitcast.78, ...), dimensions={0} | concatenate | bytes 1053736 | tf_op jit(solution)/shard_map/concatenate | solution.py:941
  303.3 1.4 multiply_subtract_fusion
  (288 shorter events, 47.6 us)
Async XLA Ops:
  8.0 47.7 %copy-start.44 = (s32[2048]{0:T(1024)S(1)}, s32[2048]{0:T(1024)}, u32[]{:S(2)}) copy-start(s32[2048]{0:T(1024)} %param.8) | copy-start | bytes 24580
  8.0 47.6 %copy-start.45 = (s32[2048]{0:T(1024)S(1)}, s32[2048]{0:T(1024)}, u32[]{:S(2)}) copy-start(s32[2048]{0:T(1024)} %param.7) | copy-start | bytes 24580
  8.0 265.6 %reduce-scatter.8.cloned.1.call-start = ((), (), s32[]{:S(2)}) async-start(), calls=%async_computation.5 | async-start | bytes 655360 | tf_op jit(solution)/shard_map/reduce_scatter | solution.py:294
  16.9 10.2 %collective-permute-start.2 = (bf16[80,1024]{1,0:T(8,128)(2,1)S(1)}, bf16[80,1024]{1,0:T(8,128)(2,1)S(1)}, u32[]{:S(2)}, u32[]{:S(2)}) collective-permute-start(bf16[80,1024]{1,0:T(8,128)(2,1)S(1)} %concatenate.78), channel_id=1, source_target_pairs={{0,24},{1,25},{2,26},{3,27},{4,28},{5,29},{6,30},{7,31},{8,16},{9,... | collective-permute-start | bytes 491528 | tf_op jit(solution)/shard_map/ppermute | solution.py:106
  22.0 13.9 %collective-permute-start.1 = (bf16[80,1024]{1,0:T(8,128)(2,1)S(1)}, bf16[80,1024]{1,0:T(8,128)(2,1)S(1)}, u32[]{:S(2)}, u32[]{:S(2)}) collective-permute-start(bf16[80,1024]{1,0:T(8,128)(2,1)S(1)} %concatenate.78), channel_id=1, source_target_pairs={{0,16},{1,17},{2,18},{3,19},{4,20},{5,21},{6,22},{7,23},{8,24},{9,... | collective-permute-start | bytes 491528 | tf_op jit(solution)/shard_map/ppermute | solution.py:106
  22.0 13.9 %collective-permute-start = (bf16[80,1024]{1,0:T(8,128)(2,1)S(1)}, bf16[80,1024]{1,0:T(8,128)(2,1)S(1)}, u32[]{:S(2)}, u32[]{:S(2)}) collective-permute-start(bf16[80,1024]{1,0:T(8,128)(2,1)S(1)} %concatenate.78), channel_id=1, source_target_pairs={{0,8},{1,9},{2,10},{3,11},{4,12},{5,13},{6,14},{7,15},{8,0},{9,1},... | collective-permute-start | bytes 491528 | tf_op jit(solution)/shard_map/ppermute | solution.py:106
  36.0 31.3 %copy-start = (bf16[4,80,1024]{2,1,0:T(8,128)(2,1)}, bf16[4,80,1024]{2,1,0:T(8,128)(2,1)S(1)}, u32[]{:S(2)}) copy-start(bf16[4,80,1024]{2,1,0:T(8,128)(2,1)S(1)} %pad_maximum_fusion.refs_0_) | copy-start | bytes 1966084
  36.0 15.9 %collective-permute-start.3 = (bf16[4,80,1024]{2,1,0:T(8,128)(2,1)S(1)}, bf16[4,80,1024]{2,1,0:T(8,128)(2,1)S(1)}, u32[]{:S(2)}, u32[]{:S(2)}) collective-permute-start(bf16[4,80,1024]{2,1,0:T(8,128)(2,1)S(1)} %pad_maximum_fusion.refs_0_), channel_id=1, source_target_pairs={{0,2},{1,3},{2,0},{3,1},{4,6},{5,7},{6,4},{7,5},{8,10},{9,11},{10,... | collective-permute-start | bytes 1966088 | tf_op jit(solution)/shard_map/ppermute | solution.py:106
  37.6 15.9 %collective-permute-start.4 = (bf16[4,80,1024]{2,1,0:T(8,128)(2,1)S(1)}, bf16[4,80,1024]{2,1,0:T(8,128)(2,1)S(1)}, u32[]{:S(2)}, u32[]{:S(2)}) collective-permute-start(bf16[4,80,1024]{2,1,0:T(8,128)(2,1)S(1)} %pad_maximum_fusion.refs_0_), channel_id=1, source_target_pairs={{0,4},{1,5},{2,6},{3,7},{4,0},{5,1},{6,2},{7,3},{8,12},{9,13},{10,... | collective-permute-start | bytes 1966088 | tf_op jit(solution)/shard_map/ppermute | solution.py:106
  39.3 15.7 %collective-permute-start.12 = (bf16[64,1024]{1,0:T(8,128)(2,1)S(1)}, bf16[64,1024]{1,0:T(8,128)(2,1)S(1)}, u32[]{:S(2)}, u32[]{:S(2)}) collective-permute-start(bf16[64,1024]{1,0:T(8,128)(2,1)S(1)} %constant_dynamic-update-slice_fusion.refs_0_), channel_id=1, source_target_pairs={{0,8},{1,9},{2,10},{3,11},{4,12},{5,13},{6,14},{7,15},{8,0},{9,1},... | collective-permute-start | bytes 393224 | tf_op jit(solution)/shard_map/ppermute | solution.py:106
  39.4 15.7 %collective-permute-start.13 = (bf16[64,1024]{1,0:T(8,128)(2,1)S(1)}, bf16[64,1024]{1,0:T(8,128)(2,1)S(1)}, u32[]{:S(2)}, u32[]{:S(2)}) collective-permute-start(bf16[64,1024]{1,0:T(8,128)(2,1)S(1)} %constant_dynamic-update-slice_fusion.refs_0_), channel_id=1, source_target_pairs={{0,16},{1,17},{2,18},{3,19},{4,20},{5,21},{6,22},{7,23},{8,24},{9,... | collective-permute-start | bytes 393224 | tf_op jit(solution)/shard_map/ppermute | solution.py:106
  42.4 13.2 %collective-permute-start.14 = (bf16[64,1024]{1,0:T(8,128)(2,1)S(1)}, bf16[64,1024]{1,0:T(8,128)(2,1)S(1)}, u32[]{:S(2)}, u32[]{:S(2)}) collective-permute-start(bf16[64,1024]{1,0:T(8,128)(2,1)S(1)} %constant_dynamic-update-slice_fusion.refs_0_), channel_id=1, source_target_pairs={{0,24},{1,25},{2,26},{3,27},{4,28},{5,29},{6,30},{7,31},{8,16},{9,... | collective-permute-start | bytes 393224 | tf_op jit(solution)/shard_map/ppermute | solution.py:106
  51.9 8.2 %collective-permute-start.5 = (bf16[2,80,1024]{2,1,0:T(8,128)(2,1)S(1)}, bf16[2,80,1024]{2,1,0:T(8,128)(2,1)S(1)}, u32[]{:S(2)}, u32[]{:S(2)}) collective-permute-start(bf16[2,80,1024]{2,1,0:T(8,128)(2,1)S(1)} %slice.329), channel_id=1, source_target_pairs={{0,4},{1,5},{2,6},{3,7},{4,0},{5,1},{6,2},{7,3},{8,12},{9,13},{10,... | collective-permute-start | bytes 983048 | tf_op jit(solution)/shard_map/ppermute | solution.py:106
  53.5 7.6 %collective-permute-start.6 = (bf16[2,80,1024]{2,1,0:T(8,128)(2,1)S(1)}, bf16[2,80,1024]{2,1,0:T(8,128)(2,1)S(1)}, u32[]{:S(2)}, u32[]{:S(2)}) collective-permute-start(bf16[2,80,1024]{2,1,0:T(8,128)(2,1)S(1)} %slice.330), channel_id=1, source_target_pairs={{0,2},{1,3},{2,0},{3,1},{4,6},{5,7},{6,4},{7,5},{8,10},{9,11},{10,... | collective-permute-start | bytes 983048 | tf_op jit(solution)/shard_map/ppermute | solution.py:106
  55.0 8.7 %collective-permute-start.7 = (bf16[4,80,1024]{2,1,0:T(8,128)(2,1)S(1)}, bf16[4,80,1024]{2,1,0:T(8,128)(2,1)S(1)}, u32[]{:S(2)}, u32[]{:S(2)}) collective-permute-start(bf16[4,80,1024]{2,1,0:T(8,128)(2,1)S(1)} %pad_maximum_fusion.refs_0_), channel_id=1, source_target_pairs={{0,1},{1,0},{2,3},{3,2},{4,5},{5,4},{6,7},{7,6},{8,9},{9,8},{10,11... | collective-permute-start | bytes 1966088 | tf_op jit(solution)/shard_map/ppermute | solution.py:106
  55.1 12.2 %collective-permute-start.8 = (bf16[4,80,1024]{2,1,0:T(8,128)(2,1)S(1)}, bf16[4,80,1024]{2,1,0:T(8,128)(2,1)S(1)}, u32[]{:S(2)}, u32[]{:S(2)}) collective-permute-start(bf16[4,80,1024]{2,1,0:T(8,128)(2,1)S(1)} %collective-permute-done.3.refs_1_), channel_id=1, source_target_pairs={{0,1},{1,0},{2,3},{3,2},{4,5},{5,4},{6,7},{7,6},{8,9},{9,8},{10,11... | collective-permute-start | bytes 1966088 | tf_op jit(solution)/shard_map/ppermute | solution.py:106
  55.6 11.7 %collective-permute-start.9 = (bf16[4,80,1024]{2,1,0:T(8,128)(2,1)S(1)}, bf16[4,80,1024]{2,1,0:T(8,128)(2,1)S(1)}, u32[]{:S(2)}, u32[]{:S(2)}) collective-permute-start(bf16[4,80,1024]{2,1,0:T(8,128)(2,1)S(1)} %collective-permute-done.4.refs_2_), channel_id=1, source_target_pairs={{0,1},{1,0},{2,3},{3,2},{4,5},{5,4},{6,7},{7,6},{8,9},{9,8},{10,11... | collective-permute-start | bytes 1966088 | tf_op jit(solution)/shard_map/ppermute | solution.py:106
  60.1 5.2 %collective-permute-start.10 = (bf16[2,80,1024]{2,1,0:T(8,128)(2,1)S(1)}, bf16[2,80,1024]{2,1,0:T(8,128)(2,1)S(1)}, u32[]{:S(2)}, u32[]{:S(2)}) collective-permute-start(bf16[2,80,1024]{2,1,0:T(8,128)(2,1)S(1)} %collective-permute-done.5.refs_3_.refs_4_), channel_id=1, source_target_pairs={{0,1},{1,0},{2,3},{3,2},{4,5},{5,4},{6,7},{7,6},{8,9},{9,8},{10,11... | collective-permute-start | bytes 983048 | tf_op jit(solution)/shard_map/ppermute | solution.py:106
  61.1 4.8 %collective-permute-start.11 = (bf16[2,80,1024]{2,1,0:T(8,128)(2,1)S(1)}, bf16[2,80,1024]{2,1,0:T(8,128)(2,1)S(1)}, u32[]{:S(2)}, u32[]{:S(2)}) collective-permute-start(bf16[2,80,1024]{2,1,0:T(8,128)(2,1)S(1)} %collective-permute-done.6.refs_4_.refs_5_), channel_id=1, source_target_pairs={{0,1},{1,0},{2,3},{3,2},{4,5},{5,4},{6,7},{7,6},{8,9},{9,8},{10,11... | collective-permute-start | bytes 983048 | tf_op jit(solution)/shard_map/ppermute | solution.py:106
  63.8 35.1 %collective-permute-start.15 = (bf16[4,64,1024]{2,1,0:T(8,128)(2,1)}, bf16[4,64,1024]{2,1,0:T(8,128)(2,1)S(1)}, u32[]{:S(2)}, u32[]{:S(2)}) collective-permute-start(bf16[4,64,1024]{2,1,0:T(8,128)(2,1)} %join.1.refs_1_), channel_id=1, source_target_pairs={{0,2},{1,3},{2,0},{3,1},{4,6},{5,7},{6,4},{7,5},{8,10},{9,11},{10,... | collective-permute-start | bytes 1572872 | tf_op jit(solution)/shard_map/ppermute | solution.py:106
  65.3 34.0 %collective-permute-start.16 = (bf16[4,64,1024]{2,1,0:T(8,128)(2,1)}, bf16[4,64,1024]{2,1,0:T(8,128)(2,1)S(1)}, u32[]{:S(2)}, u32[]{:S(2)}) collective-permute-start(bf16[4,64,1024]{2,1,0:T(8,128)(2,1)} %join.1.refs_1_), channel_id=1, source_target_pairs={{0,4},{1,5},{2,6},{3,7},{4,0},{5,1},{6,2},{7,3},{8,12},{9,13},{10,... | collective-permute-start | bytes 1572872 | tf_op jit(solution)/shard_map/ppermute | solution.py:106
  65.9 33.6 %collective-permute-start.17 = (bf16[4,64,1024]{2,1,0:T(8,128)(2,1)}, bf16[4,64,1024]{2,1,0:T(8,128)(2,1)S(1)}, u32[]{:S(2)}, u32[]{:S(2)}) collective-permute-start(bf16[4,64,1024]{2,1,0:T(8,128)(2,1)} %join.1.refs_1_), channel_id=1, source_target_pairs={{0,6},{1,7},{2,4},{3,5},{4,2},{5,3},{6,0},{7,1},{8,14},{9,15},{10,... | collective-permute-start | bytes 1572872 | tf_op jit(solution)/shard_map/ppermute | solution.py:106
  67.3 33.6 %collective-permute-start.18 = (bf16[4,64,1024]{2,1,0:T(8,128)(2,1)}, bf16[4,64,1024]{2,1,0:T(8,128)(2,1)}, u32[]{:S(2)}, u32[]{:S(2)}) collective-permute-start(bf16[4,64,1024]{2,1,0:T(8,128)(2,1)} %join.1.refs_1_), channel_id=1, source_target_pairs={{0,1},{1,0},{2,3},{3,2},{4,5},{5,4},{6,7},{7,6},{8,9},{9,8},{10,11... | collective-permute-start | bytes 1572872 | tf_op jit(solution)/shard_map/ppermute | solution.py:106
  98.9 2.0 collective-permute-start.19
  99.2 2.4 collective-permute-start.20
  99.5 2.9 collective-permute-start.21
  142.4 17.9 %collective-permute-start.22 = (bf16[16,32,1024]{2,1,0:T(8,128)(2,1)}, bf16[16,32,1024]{2,1,0:T(8,128)(2,1)S(1)}, u32[]{:S(2)}, u32[]{:S(2)}) collective-permute-start(bf16[16,32,1024]{2,1,0:T(8,128)(2,1)} %get-tuple-element.76), channel_id=1, source_target_pairs={{0,1},{1,0},{2,3},{3,2},{4,5},{5,4},{6,7},{7,6},{8,9},{9,8},{10,11... | collective-permute-start | bytes 3145736 | tf_op jit(solution)/shard_map/ppermute | solution.py:106
  159.9 34.2 %collective-permute-start.23 = (bf16[16,32,1024]{2,1,0:T(8,128)(2,1)}, bf16[16,32,1024]{2,1,0:T(8,128)(2,1)S(1)}, u32[]{:S(2)}, u32[]{:S(2)}) collective-permute-start(bf16[16,32,1024]{2,1,0:T(8,128)(2,1)} %get-tuple-element.86), channel_id=1, source_target_pairs={{0,1},{1,0},{2,3},{3,2},{4,5},{5,4},{6,7},{7,6},{8,9},{9,8},{10,11... | collective-permute-start | bytes 3145736 | tf_op jit(solution)/shard_map/ppermute | solution.py:106
  164.2 26.7 %collective-permute-start.24 = (bf16[4,32,1024]{2,1,0:T(8,128)(2,1)}, bf16[4,32,1024]{2,1,0:T(8,128)(2,1)S(1)}, u32[]{:S(2)}, u32[]{:S(2)}) collective-permute-start(bf16[4,32,1024]{2,1,0:T(8,128)(2,1)} %get-tuple-element.77.refs_3_), channel_id=1, source_target_pairs={{0,2},{1,3},{2,0},{3,1},{4,6},{5,7},{6,4},{7,5},{8,10},{9,11},{10,... | collective-permute-start | bytes 786440 | tf_op jit(solution)/shard_map/ppermute | solution.py:106
  165.7 25.2 %collective-permute-start.25 = (bf16[4,32,1024]{2,1,0:T(8,128)(2,1)}, bf16[4,32,1024]{2,1,0:T(8,128)(2,1)S(1)}, u32[]{:S(2)}, u32[]{:S(2)}) collective-permute-start(bf16[4,32,1024]{2,1,0:T(8,128)(2,1)} %get-tuple-element.78.refs_4_), channel_id=1, source_target_pairs={{0,4},{1,5},{2,6},{3,7},{4,0},{5,1},{6,2},{7,3},{8,12},{9,13},{10,... | collective-permute-start | bytes 786440 | tf_op jit(solution)/shard_map/ppermute | solution.py:106
  166.3 24.7 %collective-permute-start.26 = (bf16[4,32,1024]{2,1,0:T(8,128)(2,1)}, bf16[4,32,1024]{2,1,0:T(8,128)(2,1)S(1)}, u32[]{:S(2)}, u32[]{:S(2)}) collective-permute-start(bf16[4,32,1024]{2,1,0:T(8,128)(2,1)} %get-tuple-element.79.refs_5_), channel_id=1, source_target_pairs={{0,6},{1,7},{2,4},{3,5},{4,2},{5,3},{6,0},{7,1},{8,14},{9,15},{10,... | collective-permute-start | bytes 786440 | tf_op jit(solution)/shard_map/ppermute | solution.py:106
  194.0 87.7 %reduce-scatter.6.cloned.1.call-start = ((), (), s32[]{:S(2)}) async-start(), calls=%async_computation.4 | async-start | bytes 655360 | tf_op jit(solution)/shard_map/reduce_scatter | solution.py:294
  198.0 14.1 %collective-permute-start.29 = (bf16[4,32,1024]{2,1,0:T(8,128)(2,1)}, bf16[4,32,1024]{2,1,0:T(8,128)(2,1)S(1)}, u32[]{:S(2)}, u32[]{:S(2)}) collective-permute-start(bf16[4,32,1024]{2,1,0:T(8,128)(2,1)} %get-tuple-element.87.refs_2_), channel_id=1, source_target_pairs={{0,2},{1,3},{2,0},{3,1},{4,6},{5,7},{6,4},{7,5},{8,10},{9,11},{10,... | collective-permute-start | bytes 786440 | tf_op jit(solution)/shard_map/ppermute | solution.py:106
  199.5 12.6 %collective-permute-start.30 = (bf16[4,32,1024]{2,1,0:T(8,128)(2,1)}, bf16[4,32,1024]{2,1,0:T(8,128)(2,1)S(1)}, u32[]{:S(2)}, u32[]{:S(2)}) collective-permute-start(bf16[4,32,1024]{2,1,0:T(8,128)(2,1)} %get-tuple-element.88.refs_3_), channel_id=1, source_target_pairs={{0,4},{1,5},{2,6},{3,7},{4,0},{5,1},{6,2},{7,3},{8,12},{9,13},{10,... | collective-permute-start | bytes 786440 | tf_op jit(solution)/shard_map/ppermute | solution.py:106
  200.1 12.5 %collective-permute-start.31 = (bf16[4,32,1024]{2,1,0:T(8,128)(2,1)}, bf16[4,32,1024]{2,1,0:T(8,128)(2,1)S(1)}, u32[]{:S(2)}, u32[]{:S(2)}) collective-permute-start(bf16[4,32,1024]{2,1,0:T(8,128)(2,1)} %get-tuple-element.89.refs_4_), channel_id=1, source_target_pairs={{0,6},{1,7},{2,4},{3,5},{4,2},{5,3},{6,0},{7,1},{8,14},{9,15},{10,... | collective-permute-start | bytes 786440 | tf_op jit(solution)/shard_map/ppermute | solution.py:106
  215.5 67.4 %all-gather.3.cloned.1.call-start = ((), (), s32[]{:S(2)}) async-start(), calls=%async_computation.6 | async-start | bytes 2433024 | tf_op jit(solution)/shard_map/all_gather | solution.py:911
  216.1 81.7 %reduce-scatter.4.cloned.1.call-start = ((), (), s32[]{:S(2)}) async-start(), calls=%async_computation.3 | async-start | bytes 655360 | tf_op jit(solution)/shard_map/reduce_scatter | solution.py:294
  216.2 4.9 %collective-permute-start.27 = (bf16[16,48,1024]{2,1,0:T(8,128)(2,1)S(1)}, bf16[16,48,1024]{2,1,0:T(8,128)(2,1)S(1)}, u32[]{:S(2)}, u32[]{:S(2)}) collective-permute-start(bf16[16,48,1024]{2,1,0:T(8,128)(2,1)S(1)} %copy-done.46), channel_id=1, source_target_pairs={{0,1},{1,0},{2,3},{3,2},{4,5},{5,4},{6,7},{7,6},{8,9},{9,8},{10,11... | collective-permute-start | bytes 4718600 | tf_op jit(solution)/shard_map/ppermute | solution.py:106
  216.2 11.2 %collective-permute-start.28 = (bf16[16,32,1024]{2,1,0:T(8,128)(2,1)}, bf16[16,32,1024]{2,1,0:T(8,128)(2,1)S(1)}, u32[]{:S(2)}, u32[]{:S(2)}) collective-permute-start(bf16[16,32,1024]{2,1,0:T(8,128)(2,1)} %get-tuple-element.97), channel_id=1, source_target_pairs={{0,1},{1,0},{2,3},{3,2},{4,5},{5,4},{6,7},{7,6},{8,9},{9,8},{10,11... | collective-permute-start | bytes 3145736 | tf_op jit(solution)/shard_map/ppermute | solution.py:106
  225.9 12.3 %collective-permute-start.32 = (bf16[4,48,1024]{2,1,0:T(8,128)(2,1)}, bf16[4,48,1024]{2,1,0:T(8,128)(2,1)S(1)}, u32[]{:S(2)}, u32[]{:S(2)}) collective-permute-start(bf16[4,48,1024]{2,1,0:T(8,128)(2,1)} %get-tuple-element.93.refs_0_), channel_id=1, source_target_pairs={{0,2},{1,3},{2,0},{3,1},{4,6},{5,7},{6,4},{7,5},{8,10},{9,11},{10,... | collective-permute-start | bytes 1179656 | tf_op jit(solution)/shard_map/ppermute | solution.py:106
  231.4 39.3 %collective-permute-start.38 = (bf16[4,32,1024]{2,1,0:T(8,128)(2,1)}, bf16[4,32,1024]{2,1,0:T(8,128)(2,1)S(1)}, u32[]{:S(2)}, u32[]{:S(2)}) collective-permute-start(bf16[4,32,1024]{2,1,0:T(8,128)(2,1)} %get-tuple-element.98.refs_3_), channel_id=1, source_target_pairs={{0,2},{1,3},{2,0},{3,1},{4,6},{5,7},{6,4},{7,5},{8,10},{9,11},{10,... | collective-permute-start | bytes 786440 | tf_op jit(solution)/shard_map/ppermute | solution.py:106
  231.9 42.6 %collective-permute-start.39 = (bf16[4,32,1024]{2,1,0:T(8,128)(2,1)}, bf16[4,32,1024]{2,1,0:T(8,128)(2,1)S(1)}, u32[]{:S(2)}, u32[]{:S(2)}) collective-permute-start(bf16[4,32,1024]{2,1,0:T(8,128)(2,1)} %get-tuple-element.99.refs_4_), channel_id=1, source_target_pairs={{0,4},{1,5},{2,6},{3,7},{4,0},{5,1},{6,2},{7,3},{8,12},{9,13},{10,... | collective-permute-start | bytes 786440 | tf_op jit(solution)/shard_map/ppermute | solution.py:106
  233.1 41.5 %collective-permute-start.40 = (bf16[4,32,1024]{2,1,0:T(8,128)(2,1)}, bf16[4,32,1024]{2,1,0:T(8,128)(2,1)S(1)}, u32[]{:S(2)}, u32[]{:S(2)}) collective-permute-start(bf16[4,32,1024]{2,1,0:T(8,128)(2,1)} %get-tuple-element.100.refs_5_), channel_id=1, source_target_pairs={{0,6},{1,7},{2,4},{3,5},{4,2},{5,3},{6,0},{7,1},{8,14},{9,15},{10,... | collective-permute-start | bytes 786440 | tf_op jit(solution)/shard_map/ppermute | solution.py:106
  234.9 22.6 %collective-permute-start.33 = (bf16[4,48,1024]{2,1,0:T(8,128)(2,1)S(1)}, bf16[4,48,1024]{2,1,0:T(8,128)(2,1)S(1)}, u32[]{:S(2)}, u32[]{:S(2)}) collective-permute-start(bf16[4,48,1024]{2,1,0:T(8,128)(2,1)S(1)} %copy-done.27), channel_id=1, source_target_pairs={{0,4},{1,5},{2,6},{3,7},{4,0},{5,1},{6,2},{7,3},{8,12},{9,13},{10,... | collective-permute-start | bytes 1179656 | tf_op jit(solution)/shard_map/ppermute | solution.py:106
  238.2 27.9 %collective-permute-start.34 = (bf16[4,48,1024]{2,1,0:T(8,128)(2,1)S(1)}, bf16[4,48,1024]{2,1,0:T(8,128)(2,1)S(1)}, u32[]{:S(2)}, u32[]{:S(2)}) collective-permute-start(bf16[4,48,1024]{2,1,0:T(8,128)(2,1)S(1)} %copy-done.26), channel_id=1, source_target_pairs={{0,6},{1,7},{2,4},{3,5},{4,2},{5,3},{6,0},{7,1},{8,14},{9,15},{10,... | collective-permute-start | bytes 1179656 | tf_op jit(solution)/shard_map/ppermute | solution.py:106
  269.2 8.7 %collective-permute-start.37 = (bf16[48,1024]{1,0:T(8,128)(2,1)}, bf16[48,1024]{1,0:T(8,128)(2,1)S(1)}, u32[]{:S(2)}, u32[]{:S(2)}) collective-permute-start(bf16[48,1024]{1,0:T(8,128)(2,1)} %get-tuple-element.106), channel_id=1, source_target_pairs={{0,24},{1,25},{2,26},{3,27},{4,28},{5,29},{6,30},{7,31},{8,16},{9,... | collective-permute-start | bytes 294920 | tf_op jit(solution)/shard_map/ppermute | solution.py:106
  270.8 10.7 %collective-permute-start.36 = (bf16[48,1024]{1,0:T(8,128)(2,1)}, bf16[48,1024]{1,0:T(8,128)(2,1)S(1)}, u32[]{:S(2)}, u32[]{:S(2)}) collective-permute-start(bf16[48,1024]{1,0:T(8,128)(2,1)} %get-tuple-element.105), channel_id=1, source_target_pairs={{0,16},{1,17},{2,18},{3,19},{4,20},{5,21},{6,22},{7,23},{8,24},{9,... | collective-permute-start | bytes 294920 | tf_op jit(solution)/shard_map/ppermute | solution.py:106
  270.8 10.7 %collective-permute-start.35 = (bf16[48,1024]{1,0:T(8,128)(2,1)}, bf16[48,1024]{1,0:T(8,128)(2,1)S(1)}, u32[]{:S(2)}, u32[]{:S(2)}) collective-permute-start(bf16[48,1024]{1,0:T(8,128)(2,1)} %get-tuple-element.104), channel_id=1, source_target_pairs={{0,8},{1,9},{2,10},{3,11},{4,12},{5,13},{6,14},{7,15},{8,0},{9,1},... | collective-permute-start | bytes 294920 | tf_op jit(solution)/shard_map/ppermute | solution.py:106
  (44 other events, 233.7 us)
Sparse Core Ops, SparseCore 0:
  194.1 20.4 reduce-scatter.7
  217.5 20.0 reduce-scatter.5
  277.7 20.0 reduce-scatter.3
Sparse Core Ops, SparseCore 1:
  218.9 62.8 all-gather.2
where the time goes:
time: 315 us; the launch traced here: 314 us
  Pallas kernels  147 us (47%)
  waiting for transfers between devices  65.7 us (21%)
  starting transfers between devices  41.4 us (13%)
  local copies, waits for them, and re-layouts  33.3 us (11%)
  between operations  16.7 us (5%)
  other arithmetic  9.18 us (3%)
    pallas_call x6, Pallas kernels, run(): pl.pallas_call(kernel, grid=(batch // tile,), in_specs=in_specs, out_spec...  114 us
    ppermute x41, waiting for transfers between devices, swap(): return lax.ppermute(value, AXES, [(k, k ^ mask) for k in range(count)])  53.5 us
    ppermute x41, starting transfers between devices, swap(): return lax.ppermute(value, AXES, [(k, k ^ mask) for k in range(count)])  41.3 us
    pallas_call x8, Pallas kernels, adder(): pl.pallas_call(kernel, out_shape=outs, in_specs=[VMEM] * len(ins) + [pl.B...  21.4 us
    reduce_scatter x3, waiting for transfers between devices, z_scatter(): lax.psum_scatter(total, AXES, scatter_dimension=0, axis_index_groups=team...  11.6 us
    unnamed x100, local copies, waits for them, and re-layouts  10.5 us
    pallas_call x2, Pallas kernels, place(): pl.pallas_call(kernel, out_shape=out_shape, in_specs=[SMEM] + [VMEM] * (l...  9.97 us
    slice x7, local copies, waits for them, and re-layouts, local(): piece = [master[a:a + l] for a, l in zip(starts, sizes)]  6.66 us
  transfers between devices with their start and end apart: 45, of which 15 were waited for; matrix products, arithmetic and copies ran while one was open for 5% of the time, Pallas kernels for 35%

commit v1 on v0

--- a/solution.py
+++ b/solution.py
@@ -916,7 +916,7 @@
     own_deep = z_scatter(deep_total, groups, count)
     two_total = plane_stage(two_plane, groups, count, [feature_grad])
     own_two = z_scatter(two_total, groups, count)
-    own_last = z_stage(plane_stage_z(last_plane, groups, count, [feature_grad]), groups, count)
+    own_last = z_stage(plane_stage_z(last_plane, groups, count, [feature_grad, two_total]), groups, count)
     own_one = own_last[:rows]
     spills = own_last[rows : rows + MISC_ROW]
     row = lax.broadcasted_iota(jnp.int32, spills.shape, 0)

time: 315 us -> 307 us (0.975)
  waiting for transfers between devices: 65.7 us -> 57.2 us
    reduce_scatter x3, waiting for transfers between devices: 11.6 us -> 3.4 us  [z_scatter(): lax.psum_scatter(total, AXES, scatter_dimension=0, axis_index_groups=team...]
    unnamed x100 -> x94, local copies, waits for them, and re-layouts: 10.5 us -> 10.5 us
  transfers between devices with their start and end apart: 45 -> 45, of which waited for: 15 -> 14; matrix products, arithmetic and copies ran while one was open for 5% -> 5% of each run, Pallas kernels for 35% -> 36%
where the time goes in v1:
time: 307 us; the launch traced here: 306 us
  Pallas kernels  147 us (48%)
  waiting for transfers between devices  57.2 us (19%)
  starting transfers between devices  41.1 us (13%)
  local copies, waits for them, and re-layouts  33.4 us (11%)
  between operations  16.7 us (5%)
  other arithmetic  10.1 us (3%)
    pallas_call x6, Pallas kernels, run(): pl.pallas_call(kernel, grid=(batch // tile,), in_specs=in_specs, out_spec...  114 us
    ppermute x41, waiting for transfers between devices, swap(): return lax.ppermute(value, AXES, [(k, k ^ mask) for k in range(count)])  53.2 us
    ppermute x41, starting transfers between devices, swap(): return lax.ppermute(value, AXES, [(k, k ^ mask) for k in range(count)])  40.9 us
    pallas_call x8, Pallas kernels, adder(): pl.pallas_call(kernel, out_shape=outs, in_specs=[VMEM] * len(ins) + [pl.B...  21.5 us
    unnamed x94, local copies, waits for them, and re-layouts  10.5 us
    pallas_call x2, Pallas kernels, place(): pl.pallas_call(kernel, out_shape=out_shape, in_specs=[SMEM] + [VMEM] * (l...  9.91 us
    slice x7, local copies, waits for them, and re-layouts, local(): piece = [master[a:a + l] for a, l in zip(starts, sizes)]  6.66 us
  transfers between devices with their start and end apart: 45, of which 14 were waited for; matrix products, arithmetic and copies ran while one was open for 5% of the time, Pallas kernels for 36%

profile of v1, /device:TPU:0, one launch (start us, length us, event | category | flops | bytes accessed | tf_op | source)
XLA Modules:
  0.0 305.7 jit_solution(13845808730180449110)
XLA Ops:
  16.9 5.1 %collective-permute-start.2 = (bf16[80,1024]{1,0:T(8,128)(2,1)S(1)}, bf16[80,1024]{1,0:T(8,128)(2,1)S(1)}, u32[]{:S(2)}, u32[]{:S(2)}) collective-permute-start(bf16[80,1024]{1,0:T(8,128)(2,1)S(1)} %concatenate.78), channel_id=1, source_target_pairs={{0,24},{1,25},{2,26},{3,27},{4,28},{5,29},{6,30},{7,31},{8,16},{9,... | collective-permute-start | bytes 491528 | tf_op jit(solution)/shard_map/ppermute | solution.py:106
  23.8 3.3 %collective-permute-done.2 = bf16[80,1024]{1,0:T(8,128)(2,1)S(1)} collective-permute-done((bf16[80,1024]{1,0:T(8,128)(2,1)S(1)}, bf16[80,1024]{1,0:T(8,128)(2,1)S(1)}, u32[]{:S(2)}, u32[]{:S(2)}) %collective-permute-start.2) | collective-permute-done | bytes 163872 | tf_op jit(solution)/shard_map/ppermute | solution.py:106
  27.1 8.8 %collective-permute-done.1 = bf16[80,1024]{1,0:T(8,128)(2,1)S(1)} collective-permute-done((bf16[80,1024]{1,0:T(8,128)(2,1)S(1)}, bf16[80,1024]{1,0:T(8,128)(2,1)S(1)}, u32[]{:S(2)}, u32[]{:S(2)}) %collective-permute-start.1) | collective-permute-done | bytes 163872 | tf_op jit(solution)/shard_map/ppermute | solution.py:106
  36.0 1.6 collective-permute-start.3
  37.6 1.5 collective-permute-start.4
  39.4 3.0 collective-permute-start.13
  42.4 1.3 collective-permute-start.14
  43.8 8.1 %collective-permute-done.3.refs_1_ = bf16[4,80,1024]{2,1,0:T(8,128)(2,1)S(1)} collective-permute-done((bf16[4,80,1024]{2,1,0:T(8,128)(2,1)S(1)}, bf16[4,80,1024]{2,1,0:T(8,128)(2,1)S(1)}, u32[]{:S(2)}, u32[]{:S(2)}) %collective-permute-start.3) | collective-permute-done | bytes 655392 | tf_op jit(solution)/shard_map/ppermute | solution.py:106
  51.9 1.6 collective-permute-start.5
  53.5 1.6 collective-permute-start.6
  55.8 4.3 %collective-permute-done.5.refs_3_.refs_4_ = bf16[2,80,1024]{2,1,0:T(8,128)(2,1)S(1)} collective-permute-done((bf16[2,80,1024]{2,1,0:T(8,128)(2,1)S(1)}, bf16[2,80,1024]{2,1,0:T(8,128)(2,1)S(1)}, u32[]{:S(2)}, u32[]{:S(2)}) %collective-permute-start.5) | collective-permute-done | bytes 327712 | tf_op jit(solution)/shard_map/ppermute | solution.py:106
  61.9 1.9 join.1.refs_1_
  63.8 1.5 collective-permute-start.15
  65.9 1.4 collective-permute-start.17
  68.4 5.2 %place.2 = (bf16[32,32,1024]{2,1,0:T(8,128)(2,1)}, bf16[32,32,1024]{2,1,0:T(8,128)(2,1)}, bf16[32,16,1024]{2,1,0:T(8,128)(2,1)}) custom-call(s32[1]{0:T(128)} %bitcast.index_ref.k_ref, bf16[4,80,1024]{2,1,0:T(8,128)(2,1)} %copy-done, bf16[4,80,1024]{2,1,0:T(8,128)(2,1)} %copy-done.3, bf16[4,80,1024]{2,1,0:T(8,128)(2,1)} %copy-done.4, ...), custom_call_target="tpu_custom_call" | custom-call | tf_op jit(solution)/shard_map/place/pallas_call | solution.py:181
  80.7 18.1 %forward_cross.1 = (bf16[1040,2048]{1,0:T(8,128)(2,1)}, bf16[1040,2048]{1,0:T(8,128)(2,1)}, bf16[1040,2048]{1,0:T(8,128)(2,1)}, bf16[1040,2048]{1,0:T(8,128)(2,1)}, bf16[1040,2048]{1,0:T(8,128)(2,1)}) custom-call(bf16[1027,2048]{1,0:T(8,128)(2,1)} %bitcast.92, bf16[1024,1024]{1,0:T(8,128)(2,1)} %bitcast.70, ...), custom_call_target="tpu_custom_call" | custom-call | flops 8860467200 | bytes 30298112 | tf_op jit(solution)/shard_map/forward_cross/pallas_call | solution.py:339
  103.1 4.7 %place.3 = (bf16[32,32,1024]{2,1,0:T(8,128)(2,1)}, bf16[32,32,1024]{2,1,0:T(8,128)(2,1)}) custom-call(s32[1]{0:T(128)} %bitcast.index_ref.k_ref, bf16[32,16,1024]{2,1,0:T(8,128)(2,1)} %get-tuple-element.59.refs_0_, bf16[4,64,1024]{2,1,0:T(8,128)(2,1)} %join.1.refs_1_, bf16[4,64,1024]{2,1,0:T(8,128)(2,1)} %copy-done.17, bf16[4,64,1024]{2,1,0:T(8,128)(2,1)} %copy-done.18, ...), custom_call_target="tpu_custom_call" | custom-call | tf_op jit(solution)/shard_map/place/pallas_call | solution.py:181
  108.5 33.8 %deep.1 = (f32[1,2048]{1,0:T(1,128)}, bf16[1024,2048]{1,0:T(8,128)(2,1)}, f32[16,1024]{1,0:T(8,128)}, f32[8,512]{1,0:T(8,128)}, f32[16,32,1024]{2,1,0:T(8,128)},...) custom-call(s32[1]{0:T(128)} %bitcast.index_ref.k_ref, bf16[1040,2048]{1,0:T(8,128)(2,1)} %get-tuple-element.61.l_ref, ...), custom_call_target="tpu_custom_call" | custom-call | flops 17179869184 | bytes 17747972 | tf_op jit(solution)/shard_map/deep/pallas_call | solution.py:339
  142.6 17.1 %back_deep.1 = (f32[1040,2048]{1,0:T(8,128)}, bf16[1040,2048]{1,0:T(8,128)(2,1)}, f32[16,1024]{1,0:T(8,128)}, f32[16,32,1024]{2,1,0:T(8,128)}, bf16[16,32,1024]{2,1,0:T(8,128)(2,1)}, /*index=5*/f32[32,8,1024]{2,1,0:T(8,128)}) custom-call(s32[1]{0:T(128)} %bitcast.index_ref.k_ref, bf16[1024,2048]{1,0:T(8,128)(2,1)} %get-tuple-element.65.g_ref, ...), custom_call_target="tpu_custom_call" | custom-call | flops 8724152320 | bytes 32112644 | tf_op jit(solution)/shard_map/back_deep/pallas_call | solution.py:339
  161.1 2.9 core_sum.4
  164.0 1.5 collective-permute-start.24
  166.1 1.4 collective-permute-start.26
  167.5 23.2 %back_two.1 = (bf16[1040,2048]{1,0:T(8,128)(2,1)}, bf16[1040,2048]{1,0:T(8,128)(2,1)}, f32[16,1152]{1,0:T(8,128)}, f32[16,32,1024]{2,1,0:T(8,128)}, bf16[16,32,1...) custom-call(s32[1]{0:T(128)} %bitcast.index_ref.k_ref, bf16[1040,2048]{1,0:T(8,128)(2,1)} %get-tuple-element.67.refs_2_.g_ref, ...), custom_call_target="tpu_custom_call" | custom-call | flops 8860467200 | bytes 45936644 | tf_op jit(solution)/shard_map/back_two/pallas_call | solution.py:339
  191.6 2.2 plane_sum.4.refs_5_
  194.8 2.9 core_sum.5
  197.8 1.5 collective-permute-start.29
  199.9 1.4 collective-permute-start.31
  201.3 10.6 %grad_one.1 = (f32[16,48,1024]{2,1,0:T(8,128)}, bf16[16,48,1024]{2,1,0:T(8,128)(2,1)}) custom-call(s32[1]{0:T(128)} %bitcast.index_ref.k_ref, bf16[1040,2048]{1,0:T(8,128)(2,1)} %get-tuple-element.81.refs_2_.refs_4_.g_ref, bf16[1040,2048]{1,0:T(8,128)(2,1)} %get-tuple-element.66.x_ref, f32[32,8,1024]{2,1,0:T(8,128)} %get-tuple-element.83.refs_0_, ...), custom_call_target="tpu_custom_call" | custom-call | flops 4430233600 | bytes 16646148 | tf_op jit(solution)/shard_map/grad_one/pallas_call | solution.py:339
  213.1 2.2 plane_sum.5.refs_6_
  216.5 4.4 %collective-permute-done.28.refs_1_ = bf16[16,32,1024]{2,1,0:T(8,128)(2,1)S(1)} collective-permute-done((bf16[16,32,1024]{2,1,0:T(8,128)(2,1)S(1)}, bf16[16,32,1024]{2,1,0:T(8,128)(2,1)S(1)}, u32[]{:S(2)}, u32[]{:S(2)}) %collective-permute-start.28) | collective-permute-done | bytes 1048608 | tf_op jit(solution)/shard_map/ppermute | solution.py:106
  221.9 2.9 core_sum.7
  224.8 1.5 collective-permute-start.35
  227.0 1.3 collective-permute-start.37
  229.5 3.7 %core_sum.6 = (f32[4,48,1024]{2,1,0:T(8,128)}, bf16[4,48,1024]{2,1,0:T(8,128)(2,1)}, bf16[4,48,1024]{2,1,0:T(8,128)(2,1)}, bf16[4,48,1024]{2,1,0:T(8,128)(2,1)}) custom-call(f32[16,48,1024]{2,1,0:T(8,128)} %get-tuple-element.91.refs_0_.refs_2_.refs_4_, bf16[16,48,1024]{2,1,0:T(8,128)(2,1)} %copy-done.2), custom_call_target="tpu_custom_call" | custom-call | tf_op jit(solution)/shard_map/core_sum/pallas_call | solution.py:225
  233.2 1.5 collective-permute-start.32
  235.4 1.3 collective-permute-start.34
  236.7 11.2 %back_one.1.refs_4_ = f32[1027,2048]{1,0:T(8,128)} custom-call(bf16[1040,2048]{1,0:T(8,128)(2,1)} %get-tuple-element.81.refs_2_.refs_4_.g_ref, bf16[1040,2048]{1,0:T(8,128)(2,1)} %get-tuple-element.82.p_ref, bf16[1024,1024]{1,0:T(8,128)(2,1)} %bitcast.71, bf16[128,1024]{1,0:T(8,128)(2,1)} %get-tuple-element.142.refs_1_.t_ref, ...), custom_call_target="tpu_custom_call" | custom-call | flops 4430233600 | bytes 21819392 | tf_op jit(solution)/shard_map/back_one/pallas_call | solution.py:339
  248.7 2.2 plane_sum.6.refs_5_
  252.0 7.8 %collective-permute-done.34.refs_3_ = bf16[4,48,1024]{2,1,0:T(8,128)(2,1)S(1)} collective-permute-done((bf16[4,48,1024]{2,1,0:T(8,128)(2,1)}, bf16[4,48,1024]{2,1,0:T(8,128)(2,1)S(1)}, u32[]{:S(2)}, u32[]{:S(2)}) %collective-permute-start.34) | collective-permute-done | bytes 393248 | tf_op jit(solution)/shard_map/ppermute | solution.py:106
  260.5 2.4 plane_sum.7
  262.9 2.1 collective-permute-start.40
  265.0 2.3 collective-permute-start.38
  268.3 4.0 %collective-permute-done.40 = bf16[48,1024]{1,0:T(8,128)(2,1)S(1)} collective-permute-done((bf16[48,1024]{1,0:T(8,128)(2,1)}, bf16[48,1024]{1,0:T(8,128)(2,1)S(1)}, u32[]{:S(2)}, u32[]{:S(2)}) %collective-permute-start.40) | collective-permute-done | bytes 98336 | tf_op jit(solution)/shard_map/ppermute | solution.py:106
  272.2 8.4 %collective-permute-done.39 = bf16[48,1024]{1,0:T(8,128)(2,1)S(1)} collective-permute-done((bf16[48,1024]{1,0:T(8,128)(2,1)}, bf16[48,1024]{1,0:T(8,128)(2,1)S(1)}, u32[]{:S(2)}, u32[]{:S(2)}) %collective-permute-start.39) | collective-permute-done | bytes 98336 | tf_op jit(solution)/shard_map/ppermute | solution.py:106
  283.0 1.8 reduce_sum.29
  286.3 3.4 %reduce-scatter.4.cloned.1.call-done = f32[1,32,1024]{2,1,0:T(8,128)} async-done(((f32[4,32,1024]{2,1,0:T(8,128)}), f32[1,32,1024]{2,1,0:T(8,128)}) %reduce-scatter.4.cloned.1.call-update) | async-done | bytes 131088 | tf_op jit(solution)/shard_map/reduce_scatter | solution.py:294
  291.7 3.4 %concatenate.90 = f32[131717]{0:T(1024)S(1)} concatenate(f32[32961]{0:T(1024)S(1)} %dynamic_slice.31, f32[33]{0:T(128)S(1)} %get-tuple-element.139, f32[32961]{0:T(1024)S(1)} %dynamic_slice.33, f32[33]{0:T(128)S(1)} %get-tuple-element.138, f32[32864]{0:T(1024)S(1)} %dynamic_slice.34, f32[32]{0:T(128)S(1)} %get-tuple-element.137, f32[32768]{0:T(1024)S(1)} %bitcast.78, ...), dimensions={0} | concatenate | bytes 1053736 | tf_op jit(solution)/shard_map/concatenate | solution.py:941
  295.2 1.4 multiply_subtract_fusion
  (282 shorter events, 48.4 us)
Async XLA Ops:
  8.0 47.7 %copy-start.41 = (s32[2048]{0:T(1024)S(1)}, s32[2048]{0:T(1024)}, u32[]{:S(2)}) copy-start(s32[2048]{0:T(1024)} %param.8) | copy-start | bytes 24580
  8.0 47.6 %copy-start.42 = (s32[2048]{0:T(1024)S(1)}, s32[2048]{0:T(1024)}, u32[]{:S(2)}) copy-start(s32[2048]{0:T(1024)} %param.7) | copy-start | bytes 24580
  8.0 259.3 %reduce-scatter.8.cloned.1.call-start = ((), (), s32[]{:S(2)}) async-start(), calls=%async_computation.5 | async-start | bytes 655360 | tf_op jit(solution)/shard_map/reduce_scatter | solution.py:294
  16.9 10.2 %collective-permute-start.2 = (bf16[80,1024]{1,0:T(8,128)(2,1)S(1)}, bf16[80,1024]{1,0:T(8,128)(2,1)S(1)}, u32[]{:S(2)}, u32[]{:S(2)}) collective-permute-start(bf16[80,1024]{1,0:T(8,128)(2,1)S(1)} %concatenate.78), channel_id=1, source_target_pairs={{0,24},{1,25},{2,26},{3,27},{4,28},{5,29},{6,30},{7,31},{8,16},{9,... | collective-permute-start | bytes 491528 | tf_op jit(solution)/shard_map/ppermute | solution.py:106
  22.0 13.9 %collective-permute-start.1 = (bf16[80,1024]{1,0:T(8,128)(2,1)S(1)}, bf16[80,1024]{1,0:T(8,128)(2,1)S(1)}, u32[]{:S(2)}, u32[]{:S(2)}) collective-permute-start(bf16[80,1024]{1,0:T(8,128)(2,1)S(1)} %concatenate.78), channel_id=1, source_target_pairs={{0,16},{1,17},{2,18},{3,19},{4,20},{5,21},{6,22},{7,23},{8,24},{9,... | collective-permute-start | bytes 491528 | tf_op jit(solution)/shard_map/ppermute | solution.py:106
  22.0 13.9 %collective-permute-start = (bf16[80,1024]{1,0:T(8,128)(2,1)S(1)}, bf16[80,1024]{1,0:T(8,128)(2,1)S(1)}, u32[]{:S(2)}, u32[]{:S(2)}) collective-permute-start(bf16[80,1024]{1,0:T(8,128)(2,1)S(1)} %concatenate.78), channel_id=1, source_target_pairs={{0,8},{1,9},{2,10},{3,11},{4,12},{5,13},{6,14},{7,15},{8,0},{9,1},... | collective-permute-start | bytes 491528 | tf_op jit(solution)/shard_map/ppermute | solution.py:106
  36.0 31.4 %copy-start = (bf16[4,80,1024]{2,1,0:T(8,128)(2,1)}, bf16[4,80,1024]{2,1,0:T(8,128)(2,1)S(1)}, u32[]{:S(2)}) copy-start(bf16[4,80,1024]{2,1,0:T(8,128)(2,1)S(1)} %pad_maximum_fusion.refs_0_) | copy-start | bytes 1966084
  36.0 15.9 %collective-permute-start.3 = (bf16[4,80,1024]{2,1,0:T(8,128)(2,1)S(1)}, bf16[4,80,1024]{2,1,0:T(8,128)(2,1)S(1)}, u32[]{:S(2)}, u32[]{:S(2)}) collective-permute-start(bf16[4,80,1024]{2,1,0:T(8,128)(2,1)S(1)} %pad_maximum_fusion.refs_0_), channel_id=1, source_target_pairs={{0,2},{1,3},{2,0},{3,1},{4,6},{5,7},{6,4},{7,5},{8,10},{9,11},{10,... | collective-permute-start | bytes 1966088 | tf_op jit(solution)/shard_map/ppermute | solution.py:106
  37.6 15.9 %collective-permute-start.4 = (bf16[4,80,1024]{2,1,0:T(8,128)(2,1)S(1)}, bf16[4,80,1024]{2,1,0:T(8,128)(2,1)S(1)}, u32[]{:S(2)}, u32[]{:S(2)}) collective-permute-start(bf16[4,80,1024]{2,1,0:T(8,128)(2,1)S(1)} %pad_maximum_fusion.refs_0_), channel_id=1, source_target_pairs={{0,4},{1,5},{2,6},{3,7},{4,0},{5,1},{6,2},{7,3},{8,12},{9,13},{10,... | collective-permute-start | bytes 1966088 | tf_op jit(solution)/shard_map/ppermute | solution.py:106
  39.3 15.7 %collective-permute-start.12 = (bf16[64,1024]{1,0:T(8,128)(2,1)S(1)}, bf16[64,1024]{1,0:T(8,128)(2,1)S(1)}, u32[]{:S(2)}, u32[]{:S(2)}) collective-permute-start(bf16[64,1024]{1,0:T(8,128)(2,1)S(1)} %constant_dynamic-update-slice_fusion.refs_0_), channel_id=1, source_target_pairs={{0,8},{1,9},{2,10},{3,11},{4,12},{5,13},{6,14},{7,15},{8,0},{9,1},... | collective-permute-start | bytes 393224 | tf_op jit(solution)/shard_map/ppermute | solution.py:106
  39.4 15.7 %collective-permute-start.13 = (bf16[64,1024]{1,0:T(8,128)(2,1)S(1)}, bf16[64,1024]{1,0:T(8,128)(2,1)S(1)}, u32[]{:S(2)}, u32[]{:S(2)}) collective-permute-start(bf16[64,1024]{1,0:T(8,128)(2,1)S(1)} %constant_dynamic-update-slice_fusion.refs_0_), channel_id=1, source_target_pairs={{0,16},{1,17},{2,18},{3,19},{4,20},{5,21},{6,22},{7,23},{8,24},{9,... | collective-permute-start | bytes 393224 | tf_op jit(solution)/shard_map/ppermute | solution.py:106
  42.4 13.2 %collective-permute-start.14 = (bf16[64,1024]{1,0:T(8,128)(2,1)S(1)}, bf16[64,1024]{1,0:T(8,128)(2,1)S(1)}, u32[]{:S(2)}, u32[]{:S(2)}) collective-permute-start(bf16[64,1024]{1,0:T(8,128)(2,1)S(1)} %constant_dynamic-update-slice_fusion.refs_0_), channel_id=1, source_target_pairs={{0,24},{1,25},{2,26},{3,27},{4,28},{5,29},{6,30},{7,31},{8,16},{9,... | collective-permute-start | bytes 393224 | tf_op jit(solution)/shard_map/ppermute | solution.py:106
  51.9 8.2 %collective-permute-start.5 = (bf16[2,80,1024]{2,1,0:T(8,128)(2,1)S(1)}, bf16[2,80,1024]{2,1,0:T(8,128)(2,1)S(1)}, u32[]{:S(2)}, u32[]{:S(2)}) collective-permute-start(bf16[2,80,1024]{2,1,0:T(8,128)(2,1)S(1)} %slice.329), channel_id=1, source_target_pairs={{0,4},{1,5},{2,6},{3,7},{4,0},{5,1},{6,2},{7,3},{8,12},{9,13},{10,... | collective-permute-start | bytes 983048 | tf_op jit(solution)/shard_map/ppermute | solution.py:106
  53.5 7.6 %collective-permute-start.6 = (bf16[2,80,1024]{2,1,0:T(8,128)(2,1)S(1)}, bf16[2,80,1024]{2,1,0:T(8,128)(2,1)S(1)}, u32[]{:S(2)}, u32[]{:S(2)}) collective-permute-start(bf16[2,80,1024]{2,1,0:T(8,128)(2,1)S(1)} %slice.330), channel_id=1, source_target_pairs={{0,2},{1,3},{2,0},{3,1},{4,6},{5,7},{6,4},{7,5},{8,10},{9,11},{10,... | collective-permute-start | bytes 983048 | tf_op jit(solution)/shard_map/ppermute | solution.py:106
  55.0 8.7 %collective-permute-start.7 = (bf16[4,80,1024]{2,1,0:T(8,128)(2,1)S(1)}, bf16[4,80,1024]{2,1,0:T(8,128)(2,1)S(1)}, u32[]{:S(2)}, u32[]{:S(2)}) collective-permute-start(bf16[4,80,1024]{2,1,0:T(8,128)(2,1)S(1)} %pad_maximum_fusion.refs_0_), channel_id=1, source_target_pairs={{0,1},{1,0},{2,3},{3,2},{4,5},{5,4},{6,7},{7,6},{8,9},{9,8},{10,11... | collective-permute-start | bytes 1966088 | tf_op jit(solution)/shard_map/ppermute | solution.py:106
  55.1 12.2 %collective-permute-start.8 = (bf16[4,80,1024]{2,1,0:T(8,128)(2,1)S(1)}, bf16[4,80,1024]{2,1,0:T(8,128)(2,1)S(1)}, u32[]{:S(2)}, u32[]{:S(2)}) collective-permute-start(bf16[4,80,1024]{2,1,0:T(8,128)(2,1)S(1)} %collective-permute-done.3.refs_1_), channel_id=1, source_target_pairs={{0,1},{1,0},{2,3},{3,2},{4,5},{5,4},{6,7},{7,6},{8,9},{9,8},{10,11... | collective-permute-start | bytes 1966088 | tf_op jit(solution)/shard_map/ppermute | solution.py:106
  55.6 11.7 %collective-permute-start.9 = (bf16[4,80,1024]{2,1,0:T(8,128)(2,1)S(1)}, bf16[4,80,1024]{2,1,0:T(8,128)(2,1)S(1)}, u32[]{:S(2)}, u32[]{:S(2)}) collective-permute-start(bf16[4,80,1024]{2,1,0:T(8,128)(2,1)S(1)} %collective-permute-done.4.refs_2_), channel_id=1, source_target_pairs={{0,1},{1,0},{2,3},{3,2},{4,5},{5,4},{6,7},{7,6},{8,9},{9,8},{10,11... | collective-permute-start | bytes 1966088 | tf_op jit(solution)/shard_map/ppermute | solution.py:106
  60.1 5.2 %collective-permute-start.10 = (bf16[2,80,1024]{2,1,0:T(8,128)(2,1)S(1)}, bf16[2,80,1024]{2,1,0:T(8,128)(2,1)S(1)}, u32[]{:S(2)}, u32[]{:S(2)}) collective-permute-start(bf16[2,80,1024]{2,1,0:T(8,128)(2,1)S(1)} %collective-permute-done.5.refs_3_.refs_4_), channel_id=1, source_target_pairs={{0,1},{1,0},{2,3},{3,2},{4,5},{5,4},{6,7},{7,6},{8,9},{9,8},{10,11... | collective-permute-start | bytes 983048 | tf_op jit(solution)/shard_map/ppermute | solution.py:106
  61.1 4.8 %collective-permute-start.11 = (bf16[2,80,1024]{2,1,0:T(8,128)(2,1)S(1)}, bf16[2,80,1024]{2,1,0:T(8,128)(2,1)S(1)}, u32[]{:S(2)}, u32[]{:S(2)}) collective-permute-start(bf16[2,80,1024]{2,1,0:T(8,128)(2,1)S(1)} %collective-permute-done.6.refs_4_.refs_5_), channel_id=1, source_target_pairs={{0,1},{1,0},{2,3},{3,2},{4,5},{5,4},{6,7},{7,6},{8,9},{9,8},{10,11... | collective-permute-start | bytes 983048 | tf_op jit(solution)/shard_map/ppermute | solution.py:106
  63.8 35.0 %collective-permute-start.15 = (bf16[4,64,1024]{2,1,0:T(8,128)(2,1)}, bf16[4,64,1024]{2,1,0:T(8,128)(2,1)S(1)}, u32[]{:S(2)}, u32[]{:S(2)}) collective-permute-start(bf16[4,64,1024]{2,1,0:T(8,128)(2,1)} %join.1.refs_1_), channel_id=1, source_target_pairs={{0,2},{1,3},{2,0},{3,1},{4,6},{5,7},{6,4},{7,5},{8,10},{9,11},{10,... | collective-permute-start | bytes 1572872 | tf_op jit(solution)/shard_map/ppermute | solution.py:106
  65.3 33.8 %collective-permute-start.16 = (bf16[4,64,1024]{2,1,0:T(8,128)(2,1)}, bf16[4,64,1024]{2,1,0:T(8,128)(2,1)S(1)}, u32[]{:S(2)}, u32[]{:S(2)}) collective-permute-start(bf16[4,64,1024]{2,1,0:T(8,128)(2,1)} %join.1.refs_1_), channel_id=1, source_target_pairs={{0,4},{1,5},{2,6},{3,7},{4,0},{5,1},{6,2},{7,3},{8,12},{9,13},{10,... | collective-permute-start | bytes 1572872 | tf_op jit(solution)/shard_map/ppermute | solution.py:106
  65.9 33.5 %collective-permute-start.17 = (bf16[4,64,1024]{2,1,0:T(8,128)(2,1)}, bf16[4,64,1024]{2,1,0:T(8,128)(2,1)S(1)}, u32[]{:S(2)}, u32[]{:S(2)}) collective-permute-start(bf16[4,64,1024]{2,1,0:T(8,128)(2,1)} %join.1.refs_1_), channel_id=1, source_target_pairs={{0,6},{1,7},{2,4},{3,5},{4,2},{5,3},{6,0},{7,1},{8,14},{9,15},{10,... | collective-permute-start | bytes 1572872 | tf_op jit(solution)/shard_map/ppermute | solution.py:106
  67.3 33.5 %collective-permute-start.18 = (bf16[4,64,1024]{2,1,0:T(8,128)(2,1)}, bf16[4,64,1024]{2,1,0:T(8,128)(2,1)}, u32[]{:S(2)}, u32[]{:S(2)}) collective-permute-start(bf16[4,64,1024]{2,1,0:T(8,128)(2,1)} %join.1.refs_1_), channel_id=1, source_target_pairs={{0,1},{1,0},{2,3},{3,2},{4,5},{5,4},{6,7},{7,6},{8,9},{9,8},{10,11... | collective-permute-start | bytes 1572872 | tf_op jit(solution)/shard_map/ppermute | solution.py:106
  98.8 2.0 collective-permute-start.19
  99.2 2.4 collective-permute-start.20
  99.4 2.9 collective-permute-start.21
  142.3 17.8 %collective-permute-start.22 = (bf16[16,32,1024]{2,1,0:T(8,128)(2,1)}, bf16[16,32,1024]{2,1,0:T(8,128)(2,1)S(1)}, u32[]{:S(2)}, u32[]{:S(2)}) collective-permute-start(bf16[16,32,1024]{2,1,0:T(8,128)(2,1)} %get-tuple-element.76), channel_id=1, source_target_pairs={{0,1},{1,0},{2,3},{3,2},{4,5},{5,4},{6,7},{7,6},{8,9},{9,8},{10,11... | collective-permute-start | bytes 3145736 | tf_op jit(solution)/shard_map/ppermute | solution.py:106
  159.8 34.1 %collective-permute-start.23 = (bf16[16,32,1024]{2,1,0:T(8,128)(2,1)}, bf16[16,32,1024]{2,1,0:T(8,128)(2,1)S(1)}, u32[]{:S(2)}, u32[]{:S(2)}) collective-permute-start(bf16[16,32,1024]{2,1,0:T(8,128)(2,1)} %get-tuple-element.86), channel_id=1, source_target_pairs={{0,1},{1,0},{2,3},{3,2},{4,5},{5,4},{6,7},{7,6},{8,9},{9,8},{10,11... | collective-permute-start | bytes 3145736 | tf_op jit(solution)/shard_map/ppermute | solution.py:106
  164.0 26.7 %collective-permute-start.24 = (bf16[4,32,1024]{2,1,0:T(8,128)(2,1)}, bf16[4,32,1024]{2,1,0:T(8,128)(2,1)S(1)}, u32[]{:S(2)}, u32[]{:S(2)}) collective-permute-start(bf16[4,32,1024]{2,1,0:T(8,128)(2,1)} %get-tuple-element.77.refs_3_), channel_id=1, source_target_pairs={{0,2},{1,3},{2,0},{3,1},{4,6},{5,7},{6,4},{7,5},{8,10},{9,11},{10,... | collective-permute-start | bytes 786440 | tf_op jit(solution)/shard_map/ppermute | solution.py:106
  165.6 25.2 %collective-permute-start.25 = (bf16[4,32,1024]{2,1,0:T(8,128)(2,1)}, bf16[4,32,1024]{2,1,0:T(8,128)(2,1)S(1)}, u32[]{:S(2)}, u32[]{:S(2)}) collective-permute-start(bf16[4,32,1024]{2,1,0:T(8,128)(2,1)} %get-tuple-element.78.refs_4_), channel_id=1, source_target_pairs={{0,4},{1,5},{2,6},{3,7},{4,0},{5,1},{6,2},{7,3},{8,12},{9,13},{10,... | collective-permute-start | bytes 786440 | tf_op jit(solution)/shard_map/ppermute | solution.py:106
  166.1 24.6 %collective-permute-start.26 = (bf16[4,32,1024]{2,1,0:T(8,128)(2,1)}, bf16[4,32,1024]{2,1,0:T(8,128)(2,1)S(1)}, u32[]{:S(2)}, u32[]{:S(2)}) collective-permute-start(bf16[4,32,1024]{2,1,0:T(8,128)(2,1)} %get-tuple-element.79.refs_5_), channel_id=1, source_target_pairs={{0,6},{1,7},{2,4},{3,5},{4,2},{5,3},{6,0},{7,1},{8,14},{9,15},{10,... | collective-permute-start | bytes 786440 | tf_op jit(solution)/shard_map/ppermute | solution.py:106
  193.8 88.0 %reduce-scatter.6.cloned.1.call-start = ((), (), s32[]{:S(2)}) async-start(), calls=%async_computation.4 | async-start | bytes 655360 | tf_op jit(solution)/shard_map/reduce_scatter | solution.py:294
  197.8 14.1 %collective-permute-start.29 = (bf16[4,32,1024]{2,1,0:T(8,128)(2,1)}, bf16[4,32,1024]{2,1,0:T(8,128)(2,1)S(1)}, u32[]{:S(2)}, u32[]{:S(2)}) collective-permute-start(bf16[4,32,1024]{2,1,0:T(8,128)(2,1)} %get-tuple-element.87.refs_2_), channel_id=1, source_target_pairs={{0,2},{1,3},{2,0},{3,1},{4,6},{5,7},{6,4},{7,5},{8,10},{9,11},{10,... | collective-permute-start | bytes 786440 | tf_op jit(solution)/shard_map/ppermute | solution.py:106
  199.3 12.6 %collective-permute-start.30 = (bf16[4,32,1024]{2,1,0:T(8,128)(2,1)}, bf16[4,32,1024]{2,1,0:T(8,128)(2,1)S(1)}, u32[]{:S(2)}, u32[]{:S(2)}) collective-permute-start(bf16[4,32,1024]{2,1,0:T(8,128)(2,1)} %get-tuple-element.88.refs_3_), channel_id=1, source_target_pairs={{0,4},{1,5},{2,6},{3,7},{4,0},{5,1},{6,2},{7,3},{8,12},{9,13},{10,... | collective-permute-start | bytes 786440 | tf_op jit(solution)/shard_map/ppermute | solution.py:106
  199.9 12.5 %collective-permute-start.31 = (bf16[4,32,1024]{2,1,0:T(8,128)(2,1)}, bf16[4,32,1024]{2,1,0:T(8,128)(2,1)S(1)}, u32[]{:S(2)}, u32[]{:S(2)}) collective-permute-start(bf16[4,32,1024]{2,1,0:T(8,128)(2,1)} %get-tuple-element.89.refs_4_), channel_id=1, source_target_pairs={{0,6},{1,7},{2,4},{3,5},{4,2},{5,3},{6,0},{7,1},{8,14},{9,15},{10,... | collective-permute-start | bytes 786440 | tf_op jit(solution)/shard_map/ppermute | solution.py:106
  215.3 67.7 %all-gather.3.cloned.1.call-start = ((), (), s32[]{:S(2)}) async-start(), calls=%async_computation.6 | async-start | bytes 2433024 | tf_op jit(solution)/shard_map/all_gather | solution.py:911
  215.9 73.8 %reduce-scatter.4.cloned.1.call-start = ((), (), s32[]{:S(2)}) async-start(), calls=%async_computation.3 | async-start | bytes 655360 | tf_op jit(solution)/shard_map/reduce_scatter | solution.py:294
  215.9 12.4 %collective-permute-start.27 = (bf16[16,48,1024]{2,1,0:T(8,128)(2,1)}, bf16[16,48,1024]{2,1,0:T(8,128)(2,1)S(1)}, u32[]{:S(2)}, u32[]{:S(2)}) collective-permute-start(bf16[16,48,1024]{2,1,0:T(8,128)(2,1)} %get-tuple-element.92), channel_id=1, source_target_pairs={{0,1},{1,0},{2,3},{3,2},{4,5},{5,4},{6,7},{7,6},{8,9},{9,8},{10,11... | collective-permute-start | bytes 4718600 | tf_op jit(solution)/shard_map/ppermute | solution.py:106
  216.0 4.9 %collective-permute-start.28 = (bf16[16,32,1024]{2,1,0:T(8,128)(2,1)S(1)}, bf16[16,32,1024]{2,1,0:T(8,128)(2,1)S(1)}, u32[]{:S(2)}, u32[]{:S(2)}) collective-permute-start(bf16[16,32,1024]{2,1,0:T(8,128)(2,1)S(1)} %copy-done.43), channel_id=1, source_target_pairs={{0,1},{1,0},{2,3},{3,2},{4,5},{5,4},{6,7},{7,6},{8,9},{9,8},{10,11... | collective-permute-start | bytes 3145736 | tf_op jit(solution)/shard_map/ppermute | solution.py:106
  224.8 10.6 %collective-permute-start.35 = (bf16[4,32,1024]{2,1,0:T(8,128)(2,1)}, bf16[4,32,1024]{2,1,0:T(8,128)(2,1)S(1)}, u32[]{:S(2)}, u32[]{:S(2)}) collective-permute-start(bf16[4,32,1024]{2,1,0:T(8,128)(2,1)} %get-tuple-element.98.refs_3_), channel_id=1, source_target_pairs={{0,2},{1,3},{2,0},{3,1},{4,6},{5,7},{6,4},{7,5},{8,10},{9,11},{10,... | collective-permute-start | bytes 786440 | tf_op jit(solution)/shard_map/ppermute | solution.py:106
  226.4 21.5 %collective-permute-start.36 = (bf16[4,32,1024]{2,1,0:T(8,128)(2,1)}, bf16[4,32,1024]{2,1,0:T(8,128)(2,1)S(1)}, u32[]{:S(2)}, u32[]{:S(2)}) collective-permute-start(bf16[4,32,1024]{2,1,0:T(8,128)(2,1)} %get-tuple-element.99.refs_4_), channel_id=1, source_target_pairs={{0,4},{1,5},{2,6},{3,7},{4,0},{5,1},{6,2},{7,3},{8,12},{9,13},{10,... | collective-permute-start | bytes 786440 | tf_op jit(solution)/shard_map/ppermute | solution.py:106
  227.0 20.8 %collective-permute-start.37 = (bf16[4,32,1024]{2,1,0:T(8,128)(2,1)}, bf16[4,32,1024]{2,1,0:T(8,128)(2,1)S(1)}, u32[]{:S(2)}, u32[]{:S(2)}) collective-permute-start(bf16[4,32,1024]{2,1,0:T(8,128)(2,1)} %get-tuple-element.100.refs_5_), channel_id=1, source_target_pairs={{0,6},{1,7},{2,4},{3,5},{4,2},{5,3},{6,0},{7,1},{8,14},{9,15},{10,... | collective-permute-start | bytes 786440 | tf_op jit(solution)/shard_map/ppermute | solution.py:106
  233.2 17.6 %collective-permute-start.32 = (bf16[4,48,1024]{2,1,0:T(8,128)(2,1)}, bf16[4,48,1024]{2,1,0:T(8,128)(2,1)S(1)}, u32[]{:S(2)}, u32[]{:S(2)}) collective-permute-start(bf16[4,48,1024]{2,1,0:T(8,128)(2,1)} %get-tuple-element.93.refs_0_), channel_id=1, source_target_pairs={{0,2},{1,3},{2,0},{3,1},{4,6},{5,7},{6,4},{7,5},{8,10},{9,11},{10,... | collective-permute-start | bytes 1179656 | tf_op jit(solution)/shard_map/ppermute | solution.py:106
  234.7 17.2 %collective-permute-start.33 = (bf16[4,48,1024]{2,1,0:T(8,128)(2,1)}, bf16[4,48,1024]{2,1,0:T(8,128)(2,1)S(1)}, u32[]{:S(2)}, u32[]{:S(2)}) collective-permute-start(bf16[4,48,1024]{2,1,0:T(8,128)(2,1)} %get-tuple-element.94.refs_1_), channel_id=1, source_target_pairs={{0,4},{1,5},{2,6},{3,7},{4,0},{5,1},{6,2},{7,3},{8,12},{9,13},{10,... | collective-permute-start | bytes 1179656 | tf_op jit(solution)/shard_map/ppermute | solution.py:106
  235.4 24.3 %collective-permute-start.34 = (bf16[4,48,1024]{2,1,0:T(8,128)(2,1)}, bf16[4,48,1024]{2,1,0:T(8,128)(2,1)S(1)}, u32[]{:S(2)}, u32[]{:S(2)}) collective-permute-start(bf16[4,48,1024]{2,1,0:T(8,128)(2,1)} %get-tuple-element.95.refs_2_), channel_id=1, source_target_pairs={{0,6},{1,7},{2,4},{3,5},{4,2},{5,3},{6,0},{7,1},{8,14},{9,15},{10,... | collective-permute-start | bytes 1179656 | tf_op jit(solution)/shard_map/ppermute | solution.py:106
  262.9 9.3 %collective-permute-start.40 = (bf16[48,1024]{1,0:T(8,128)(2,1)}, bf16[48,1024]{1,0:T(8,128)(2,1)S(1)}, u32[]{:S(2)}, u32[]{:S(2)}) collective-permute-start(bf16[48,1024]{1,0:T(8,128)(2,1)} %get-tuple-element.107), channel_id=1, source_target_pairs={{0,24},{1,25},{2,26},{3,27},{4,28},{5,29},{6,30},{7,31},{8,16},{9,... | collective-permute-start | bytes 294920 | tf_op jit(solution)/shard_map/ppermute | solution.py:106
  265.0 15.7 %collective-permute-start.39 = (bf16[48,1024]{1,0:T(8,128)(2,1)}, bf16[48,1024]{1,0:T(8,128)(2,1)S(1)}, u32[]{:S(2)}, u32[]{:S(2)}) collective-permute-start(bf16[48,1024]{1,0:T(8,128)(2,1)} %get-tuple-element.106), channel_id=1, source_target_pairs={{0,16},{1,17},{2,18},{3,19},{4,20},{5,21},{6,22},{7,23},{8,24},{9,... | collective-permute-start | bytes 294920 | tf_op jit(solution)/shard_map/ppermute | solution.py:106
  265.0 15.7 %collective-permute-start.38 = (bf16[48,1024]{1,0:T(8,128)(2,1)}, bf16[48,1024]{1,0:T(8,128)(2,1)S(1)}, u32[]{:S(2)}, u32[]{:S(2)}) collective-permute-start(bf16[48,1024]{1,0:T(8,128)(2,1)} %get-tuple-element.105), channel_id=1, source_target_pairs={{0,8},{1,9},{2,10},{3,11},{4,12},{5,13},{6,14},{7,15},{8,0},{9,1},... | collective-permute-start | bytes 294920 | tf_op jit(solution)/shard_map/ppermute | solution.py:106
  (41 other events, 186.0 us)
Sparse Core Ops, SparseCore 0:
  193.9 20.4 reduce-scatter.7
  217.3 19.9 reduce-scatter.5
  268.4 21.2 reduce-scatter.3
Sparse Core Ops, SparseCore 1:
  218.7 61.4 all-gather.2

commit v2 on v1

--- a/solution.py
+++ b/solution.py
@@ -873,6 +873,7 @@
     )
     lines = lines.astype(F32).T
     spread = Spread(groups, rows, count, by_z=True)
+    spread_two = Spread(groups, rows, count)
     spread_last = Spread(groups, rows, count, below=True)
 
     wide_features, mixer_one, mixer_two, low_one, low_two = forward_cross(
@@ -888,10 +889,10 @@
     *deep_stacks, deep_over = spread.finish(outs, slot)
     top_plane = core_stage(top_stacks, groups, count, [mixer_two_low])
     part, mixer_one_low, vectors, *outs = back_two(
-        spread, slot, mixer_two_low, low_one, layer_grad, wide_features, mixer_one, mixer_two,
+        spread_two, slot, mixer_two_low, low_one, layer_grad, wide_features, mixer_one, mixer_two,
         matrix_two, tail_two, edge_two, (top_lines, deep_lines, sums), top_plane[1:],
     )
-    *two_stacks, two_over = spread.finish(outs, slot)
+    *two_stacks, two_over = spread_two.finish(outs, slot)
     top_total = plane_stage(top_plane, groups, count, [mixer_one_low])
     deep_plane = core_stage(deep_stacks, groups, count, [mixer_one_low])
     overs = (two_over, deep_over)
@@ -914,9 +915,8 @@
 
     own_top = z_scatter(top_total, groups, count)
     own_deep = z_scatter(deep_total, groups, count)
-    two_total = plane_stage(two_plane, groups, count, [feature_grad])
-    own_two = z_scatter(two_total, groups, count)
-    own_last = z_stage(plane_stage_z(last_plane, groups, count, [feature_grad, two_total]), groups, count)
+    own_two = z_stage(plane_stage_z(two_plane, groups, count, [feature_grad]), groups, count)
+    own_last = z_stage(plane_stage_z(last_plane, groups, count, [feature_grad, own_two]), groups, count)
     own_one = own_last[:rows]
     spills = own_last[rows : rows + MISC_ROW]
     row = lax.broadcasted_iota(jnp.int32, spills.shape, 0)

time: 307 us -> 308 us (level)
  waiting for transfers between devices: 57.2 us -> 53.6 us
  starting transfers between devices: 41.1 us -> 44.3 us
    reduce_scatter x3 -> x2, waiting for transfers between devices: 3.4 us -> 0.02 us  [z_scatter(): lax.psum_scatter(total, AXES, scatter_dimension=0, axis_index_groups=team...]
    ppermute x41 -> x44, starting transfers between devices: 40.9 us -> 44.2 us  [swap(): return lax.ppermute(value, AXES, [(k, k ^ mask) for k in range(count)])]
    ppermute x41 -> x44, waiting for transfers between devices: 53.2 us -> 53 us  [swap(): return lax.ppermute(value, AXES, [(k, k ^ mask) for k in range(count)])]
    unnamed x94 -> x104, local copies, waits for them, and re-layouts: 10.5 us -> 10.6 us
  transfers between devices with their start and end apart: 45 -> 47, of which waited for: 14 -> 16; matrix products, arithmetic and copies ran while one was open for 5% -> 5% of each run, Pallas kernels for 36% -> 36%
where the time goes in v2:
time: 308 us; the launch traced here: 307 us
  Pallas kernels  147 us (48%)
  waiting for transfers between devices  53.6 us (17%)
  starting transfers between devices  44.3 us (14%)
  local copies, waits for them, and re-layouts  33.6 us (11%)
  between operations  17 us (6%)
  other arithmetic  10.8 us (4%)
    pallas_call x6, Pallas kernels, run(): pl.pallas_call(kernel, grid=(batch // tile,), in_specs=in_specs, out_spec...  114 us
    ppermute x44, waiting for transfers between devices, swap(): return lax.ppermute(value, AXES, [(k, k ^ mask) for k in range(count)])  53 us
    ppermute x44, starting transfers between devices, swap(): return lax.ppermute(value, AXES, [(k, k ^ mask) for k in range(count)])  44.2 us
    pallas_call x8, Pallas kernels, adder(): pl.pallas_call(kernel, out_shape=outs, in_specs=[VMEM] * len(ins) + [pl.B...  21.4 us
    unnamed x104, local copies, waits for them, and re-layouts  10.6 us
    pallas_call x2, Pallas kernels, place(): pl.pallas_call(kernel, out_shape=out_shape, in_specs=[SMEM] + [VMEM] * (l...  10 us
    slice x7, local copies, waits for them, and re-layouts, local(): piece = [master[a:a + l] for a, l in zip(starts, sizes)]  6.66 us
  transfers between devices with their start and end apart: 47, of which 16 were waited for; matrix products, arithmetic and copies ran while one was open for 5% of the time, Pallas kernels for 36%

profile of v2, /device:TPU:0, one launch (start us, length us, event | category | flops | bytes accessed | tf_op | source)
XLA Modules:
  0.0 306.8 jit_solution(6654971290914041499)
XLA Ops:
  16.9 5.1 %collective-permute-start.2 = (bf16[80,1024]{1,0:T(8,128)(2,1)S(1)}, bf16[80,1024]{1,0:T(8,128)(2,1)S(1)}, u32[]{:S(2)}, u32[]{:S(2)}) collective-permute-start(bf16[80,1024]{1,0:T(8,128)(2,1)S(1)} %concatenate.78), channel_id=1, source_target_pairs={{0,24},{1,25},{2,26},{3,27},{4,28},{5,29},{6,30},{7,31},{8,16},{9,... | collective-permute-start | bytes 491528 | tf_op jit(solution)/shard_map/ppermute | solution.py:106
  23.8 3.3 %collective-permute-done.2 = bf16[80,1024]{1,0:T(8,128)(2,1)S(1)} collective-permute-done((bf16[80,1024]{1,0:T(8,128)(2,1)S(1)}, bf16[80,1024]{1,0:T(8,128)(2,1)S(1)}, u32[]{:S(2)}, u32[]{:S(2)}) %collective-permute-start.2) | collective-permute-done | bytes 163872 | tf_op jit(solution)/shard_map/ppermute | solution.py:106
  27.1 8.8 %collective-permute-done.1 = bf16[80,1024]{1,0:T(8,128)(2,1)S(1)} collective-permute-done((bf16[80,1024]{1,0:T(8,128)(2,1)S(1)}, bf16[80,1024]{1,0:T(8,128)(2,1)S(1)}, u32[]{:S(2)}, u32[]{:S(2)}) %collective-permute-start.1) | collective-permute-done | bytes 163872 | tf_op jit(solution)/shard_map/ppermute | solution.py:106
  36.0 1.6 collective-permute-start.3
  37.6 1.5 collective-permute-start.4
  39.4 3.0 collective-permute-start.13
  43.8 8.1 %collective-permute-done.3.refs_1_ = bf16[4,80,1024]{2,1,0:T(8,128)(2,1)S(1)} collective-permute-done((bf16[4,80,1024]{2,1,0:T(8,128)(2,1)S(1)}, bf16[4,80,1024]{2,1,0:T(8,128)(2,1)S(1)}, u32[]{:S(2)}, u32[]{:S(2)}) %collective-permute-start.3) | collective-permute-done | bytes 655392 | tf_op jit(solution)/shard_map/ppermute | solution.py:106
  51.9 1.6 collective-permute-start.5
  53.5 1.6 collective-permute-start.6
  55.8 4.3 %collective-permute-done.5.refs_3_.refs_4_ = bf16[2,80,1024]{2,1,0:T(8,128)(2,1)S(1)} collective-permute-done((bf16[2,80,1024]{2,1,0:T(8,128)(2,1)S(1)}, bf16[2,80,1024]{2,1,0:T(8,128)(2,1)S(1)}, u32[]{:S(2)}, u32[]{:S(2)}) %collective-permute-start.5) | collective-permute-done | bytes 327712 | tf_op jit(solution)/shard_map/ppermute | solution.py:106
  61.8 1.9 join.1.refs_1_
  63.8 1.5 collective-permute-start.15
  65.9 1.4 collective-permute-start.17
  68.4 5.3 %place.2 = (bf16[32,32,1024]{2,1,0:T(8,128)(2,1)}, bf16[32,32,1024]{2,1,0:T(8,128)(2,1)}, bf16[32,16,1024]{2,1,0:T(8,128)(2,1)}) custom-call(s32[1]{0:T(128)} %bitcast.index_ref.k_ref, bf16[4,80,1024]{2,1,0:T(8,128)(2,1)} %copy-done, bf16[4,80,1024]{2,1,0:T(8,128)(2,1)} %copy-done.3, bf16[4,80,1024]{2,1,0:T(8,128)(2,1)} %copy-done.4, ...), custom_call_target="tpu_custom_call" | custom-call | tf_op jit(solution)/shard_map/place/pallas_call | solution.py:181
  80.7 18.1 %forward_cross.1 = (bf16[1040,2048]{1,0:T(8,128)(2,1)}, bf16[1040,2048]{1,0:T(8,128)(2,1)}, bf16[1040,2048]{1,0:T(8,128)(2,1)}, bf16[1040,2048]{1,0:T(8,128)(2,1)}, bf16[1040,2048]{1,0:T(8,128)(2,1)}) custom-call(bf16[1027,2048]{1,0:T(8,128)(2,1)} %bitcast.90, bf16[1024,1024]{1,0:T(8,128)(2,1)} %bitcast.69, ...), custom_call_target="tpu_custom_call" | custom-call | flops 8860467200 | bytes 30298112 | tf_op jit(solution)/shard_map/forward_cross/pallas_call | solution.py:339
  103.2 4.7 %place.3 = (bf16[32,32,1024]{2,1,0:T(8,128)(2,1)}, bf16[32,32,1024]{2,1,0:T(8,128)(2,1)}) custom-call(s32[1]{0:T(128)} %bitcast.index_ref.k_ref, bf16[32,16,1024]{2,1,0:T(8,128)(2,1)} %get-tuple-element.63.refs_0_, bf16[4,64,1024]{2,1,0:T(8,128)(2,1)} %join.1.refs_1_, bf16[4,64,1024]{2,1,0:T(8,128)(2,1)} %copy-done.18, bf16[4,64,1024]{2,1,0:T(8,128)(2,1)} %copy-done.19, ...), custom_call_target="tpu_custom_call" | custom-call | tf_op jit(solution)/shard_map/place/pallas_call | solution.py:181
  108.5 33.8 %deep.1 = (f32[1,2048]{1,0:T(1,128)}, bf16[1024,2048]{1,0:T(8,128)(2,1)}, f32[16,1024]{1,0:T(8,128)}, f32[8,512]{1,0:T(8,128)}, f32[16,32,1024]{2,1,0:T(8,128)},...) custom-call(s32[1]{0:T(128)} %bitcast.index_ref.k_ref, bf16[1040,2048]{1,0:T(8,128)(2,1)} %get-tuple-element.65.l_ref, ...), custom_call_target="tpu_custom_call" | custom-call | flops 17179869184 | bytes 17747972 | tf_op jit(solution)/shard_map/deep/pallas_call | solution.py:339
  142.7 17.1 %back_deep.1 = (f32[1040,2048]{1,0:T(8,128)}, bf16[1040,2048]{1,0:T(8,128)(2,1)}, f32[16,1024]{1,0:T(8,128)}, f32[16,32,1024]{2,1,0:T(8,128)}, bf16[16,32,1024]{2,1,0:T(8,128)(2,1)}, /*index=5*/f32[32,8,1024]{2,1,0:T(8,128)}) custom-call(s32[1]{0:T(128)} %bitcast.index_ref.k_ref, bf16[1024,2048]{1,0:T(8,128)(2,1)} %get-tuple-element.69.g_ref, ...), custom_call_target="tpu_custom_call" | custom-call | flops 8724152320 | bytes 32112644 | tf_op jit(solution)/shard_map/back_deep/pallas_call | solution.py:339
  161.2 2.9 core_sum.4
  164.1 1.5 collective-permute-start.24
  167.6 23.3 %back_two.1 = (bf16[1040,2048]{1,0:T(8,128)(2,1)}, bf16[1040,2048]{1,0:T(8,128)(2,1)}, f32[16,1152]{1,0:T(8,128)}, f32[16,32,1024]{2,1,0:T(8,128)}, bf16[16,32,1...) custom-call(s32[1]{0:T(128)} %bitcast.index_ref.k_ref, bf16[1040,2048]{1,0:T(8,128)(2,1)} %get-tuple-element.71.refs_2_.g_ref, ...), custom_call_target="tpu_custom_call" | custom-call | flops 8860467200 | bytes 45936644 | tf_op jit(solution)/shard_map/back_two/pallas_call | solution.py:339
  191.8 2.2 plane_sum.4.refs_5_
  195.0 2.9 core_sum.5
  198.0 1.5 collective-permute-start.29
  200.1 1.3 collective-permute-start.31
  201.4 10.6 %grad_one.1 = (f32[16,48,1024]{2,1,0:T(8,128)}, bf16[16,48,1024]{2,1,0:T(8,128)(2,1)}) custom-call(s32[1]{0:T(128)} %bitcast.index_ref.k_ref, bf16[1040,2048]{1,0:T(8,128)(2,1)} %get-tuple-element.85.refs_2_.refs_4_.g_ref, bf16[1040,2048]{1,0:T(8,128)(2,1)} %get-tuple-element.70.x_ref, f32[32,8,1024]{2,1,0:T(8,128)} %get-tuple-element.87.refs_0_, ...), custom_call_target="tpu_custom_call" | custom-call | flops 4430233600 | bytes 16646148 | tf_op jit(solution)/shard_map/grad_one/pallas_call | solution.py:339
  213.3 2.2 plane_sum.5.refs_6_
  216.7 4.4 %collective-permute-done.28.refs_1_ = bf16[16,32,1024]{2,1,0:T(8,128)(2,1)S(1)} collective-permute-done((bf16[16,32,1024]{2,1,0:T(8,128)(2,1)S(1)}, bf16[16,32,1024]{2,1,0:T(8,128)(2,1)S(1)}, u32[]{:S(2)}, u32[]{:S(2)}) %collective-permute-start.28) | collective-permute-done | bytes 1048608 | tf_op jit(solution)/shard_map/ppermute | solution.py:106
  222.0 3.0 core_sum.7
  225.0 1.5 collective-permute-start.35
  229.6 3.8 %core_sum.6 = (f32[4,48,1024]{2,1,0:T(8,128)}, bf16[4,48,1024]{2,1,0:T(8,128)(2,1)}, bf16[4,48,1024]{2,1,0:T(8,128)(2,1)}, bf16[4,48,1024]{2,1,0:T(8,128)(2,1)}) custom-call(f32[16,48,1024]{2,1,0:T(8,128)} %get-tuple-element.95.refs_0_.refs_2_.refs_4_, bf16[16,48,1024]{2,1,0:T(8,128)(2,1)} %copy-done.2), custom_call_target="tpu_custom_call" | custom-call | tf_op jit(solution)/shard_map/core_sum/pallas_call | solution.py:225
  233.4 11.3 %back_one.1.refs_4_ = f32[1027,2048]{1,0:T(8,128)} custom-call(bf16[1040,2048]{1,0:T(8,128)(2,1)} %get-tuple-element.85.refs_2_.refs_4_.g_ref, bf16[1040,2048]{1,0:T(8,128)(2,1)} %get-tuple-element.86.p_ref, bf16[1024,1024]{1,0:T(8,128)(2,1)} %bitcast.70, bf16[128,1024]{1,0:T(8,128)(2,1)} %get-tuple-element.150.refs_1_.t_ref, ...), custom_call_target="tpu_custom_call" | custom-call | flops 4430233600 | bytes 21819392 | tf_op jit(solution)/shard_map/back_one/pallas_call | solution.py:339
  245.6 2.1 plane_sum.6
  247.7 2.2 collective-permute-start.40
  249.9 1.5 collective-permute-start.32
  252.0 1.4 collective-permute-start.34
  255.6 3.2 %collective-permute-done.39 = bf16[32,1024]{1,0:T(8,128)(2,1)S(1)} collective-permute-done((bf16[32,1024]{1,0:T(8,128)(2,1)}, bf16[32,1024]{1,0:T(8,128)(2,1)S(1)}, u32[]{:S(2)}, u32[]{:S(2)}) %collective-permute-start.39) | collective-permute-done | bytes 65568 | tf_op jit(solution)/shard_map/ppermute | solution.py:106
  259.4 1.6 convert_add_fusion.1.refs_5_
  261.0 2.7 collective-permute-done.33.refs_2_
  263.8 10.0 %collective-permute-done.34.refs_3_ = bf16[4,48,1024]{2,1,0:T(8,128)(2,1)S(1)} collective-permute-done((bf16[4,48,1024]{2,1,0:T(8,128)(2,1)S(1)}, bf16[4,48,1024]{2,1,0:T(8,128)(2,1)S(1)}, u32[]{:S(2)}, u32[]{:S(2)}) %collective-permute-start.34) | collective-permute-done | bytes 393248 | tf_op jit(solution)/shard_map/ppermute | solution.py:106
  274.5 2.3 plane_sum.7
  276.9 1.6 collective-permute-start.43
  278.5 2.8 collective-permute-start.41
  282.2 1.4 collective-permute-done.43
  283.6 2.0 collective-permute-done.42
  288.0 1.8 reduce_sum.29
  292.4 3.4 %concatenate.90 = f32[131717]{0:T(1024)S(1)} concatenate(f32[32961]{0:T(1024)S(1)} %dynamic_slice.31, f32[33]{0:T(128)S(1)} %get-tuple-element.147, f32[32961]{0:T(1024)S(1)} %dynamic_slice.33, f32[33]{0:T(128)S(1)} %get-tuple-element.146, f32[32864]{0:T(1024)S(1)} %dynamic_slice.34, f32[32]{0:T(128)S(1)} %get-tuple-element.145, f32[32768]{0:T(1024)S(1)} %bitcast.77, ...), dimensions={0} | concatenate | bytes 1053736 | tf_op jit(solution)/shard_map/concatenate | solution.py:941
  295.8 1.4 multiply_subtract_fusion
  (296 shorter events, 53.2 us)
Async XLA Ops:
  8.0 47.7 %copy-start.45 = (s32[2048]{0:T(1024)S(1)}, s32[2048]{0:T(1024)}, u32[]{:S(2)}) copy-start(s32[2048]{0:T(1024)} %param.8) | copy-start | bytes 24580
  8.0 273.2 %reduce-scatter.5.cloned.1.call-start = ((), (), s32[]{:S(2)}) async-start(), calls=%async_computation.3 | async-start | bytes 655360 | tf_op jit(solution)/shard_map/reduce_scatter | solution.py:294
  16.9 10.2 %collective-permute-start.2 = (bf16[80,1024]{1,0:T(8,128)(2,1)S(1)}, bf16[80,1024]{1,0:T(8,128)(2,1)S(1)}, u32[]{:S(2)}, u32[]{:S(2)}) collective-permute-start(bf16[80,1024]{1,0:T(8,128)(2,1)S(1)} %concatenate.78), channel_id=1, source_target_pairs={{0,24},{1,25},{2,26},{3,27},{4,28},{5,29},{6,30},{7,31},{8,16},{9,... | collective-permute-start | bytes 491528 | tf_op jit(solution)/shard_map/ppermute | solution.py:106
  22.0 13.9 %collective-permute-start.1 = (bf16[80,1024]{1,0:T(8,128)(2,1)S(1)}, bf16[80,1024]{1,0:T(8,128)(2,1)S(1)}, u32[]{:S(2)}, u32[]{:S(2)}) collective-permute-start(bf16[80,1024]{1,0:T(8,128)(2,1)S(1)} %concatenate.78), channel_id=1, source_target_pairs={{0,16},{1,17},{2,18},{3,19},{4,20},{5,21},{6,22},{7,23},{8,24},{9,... | collective-permute-start | bytes 491528 | tf_op jit(solution)/shard_map/ppermute | solution.py:106
  22.0 13.9 %collective-permute-start = (bf16[80,1024]{1,0:T(8,128)(2,1)S(1)}, bf16[80,1024]{1,0:T(8,128)(2,1)S(1)}, u32[]{:S(2)}, u32[]{:S(2)}) collective-permute-start(bf16[80,1024]{1,0:T(8,128)(2,1)S(1)} %concatenate.78), channel_id=1, source_target_pairs={{0,8},{1,9},{2,10},{3,11},{4,12},{5,13},{6,14},{7,15},{8,0},{9,1},... | collective-permute-start | bytes 491528 | tf_op jit(solution)/shard_map/ppermute | solution.py:106
  36.0 15.9 %collective-permute-start.3 = (bf16[4,80,1024]{2,1,0:T(8,128)(2,1)S(1)}, bf16[4,80,1024]{2,1,0:T(8,128)(2,1)S(1)}, u32[]{:S(2)}, u32[]{:S(2)}) collective-permute-start(bf16[4,80,1024]{2,1,0:T(8,128)(2,1)S(1)} %pad_maximum_fusion.refs_0_), channel_id=1, source_target_pairs={{0,2},{1,3},{2,0},{3,1},{4,6},{5,7},{6,4},{7,5},{8,10},{9,11},{10,... | collective-permute-start | bytes 1966088 | tf_op jit(solution)/shard_map/ppermute | solution.py:106
  37.6 15.9 %collective-permute-start.4 = (bf16[4,80,1024]{2,1,0:T(8,128)(2,1)S(1)}, bf16[4,80,1024]{2,1,0:T(8,128)(2,1)S(1)}, u32[]{:S(2)}, u32[]{:S(2)}) collective-permute-start(bf16[4,80,1024]{2,1,0:T(8,128)(2,1)S(1)} %pad_maximum_fusion.refs_0_), channel_id=1, source_target_pairs={{0,4},{1,5},{2,6},{3,7},{4,0},{5,1},{6,2},{7,3},{8,12},{9,13},{10,... | collective-permute-start | bytes 1966088 | tf_op jit(solution)/shard_map/ppermute | solution.py:106
  39.3 15.7 %collective-permute-start.12 = (bf16[64,1024]{1,0:T(8,128)(2,1)S(1)}, bf16[64,1024]{1,0:T(8,128)(2,1)S(1)}, u32[]{:S(2)}, u32[]{:S(2)}) collective-permute-start(bf16[64,1024]{1,0:T(8,128)(2,1)S(1)} %constant_dynamic-update-slice_fusion.refs_0_), channel_id=1, source_target_pairs={{0,8},{1,9},{2,10},{3,11},{4,12},{5,13},{6,14},{7,15},{8,0},{9,1},... | collective-permute-start | bytes 393224 | tf_op jit(solution)/shard_map/ppermute | solution.py:106
  39.4 15.7 %collective-permute-start.13 = (bf16[64,1024]{1,0:T(8,128)(2,1)S(1)}, bf16[64,1024]{1,0:T(8,128)(2,1)S(1)}, u32[]{:S(2)}, u32[]{:S(2)}) collective-permute-start(bf16[64,1024]{1,0:T(8,128)(2,1)S(1)} %constant_dynamic-update-slice_fusion.refs_0_), channel_id=1, source_target_pairs={{0,16},{1,17},{2,18},{3,19},{4,20},{5,21},{6,22},{7,23},{8,24},{9,... | collective-permute-start | bytes 393224 | tf_op jit(solution)/shard_map/ppermute | solution.py:106
  42.4 13.2 %collective-permute-start.14 = (bf16[64,1024]{1,0:T(8,128)(2,1)S(1)}, bf16[64,1024]{1,0:T(8,128)(2,1)S(1)}, u32[]{:S(2)}, u32[]{:S(2)}) collective-permute-start(bf16[64,1024]{1,0:T(8,128)(2,1)S(1)} %constant_dynamic-update-slice_fusion.refs_0_), channel_id=1, source_target_pairs={{0,24},{1,25},{2,26},{3,27},{4,28},{5,29},{6,30},{7,31},{8,16},{9,... | collective-permute-start | bytes 393224 | tf_op jit(solution)/shard_map/ppermute | solution.py:106
  51.9 8.2 %collective-permute-start.5 = (bf16[2,80,1024]{2,1,0:T(8,128)(2,1)S(1)}, bf16[2,80,1024]{2,1,0:T(8,128)(2,1)S(1)}, u32[]{:S(2)}, u32[]{:S(2)}) collective-permute-start(bf16[2,80,1024]{2,1,0:T(8,128)(2,1)S(1)} %slice.329), channel_id=1, source_target_pairs={{0,4},{1,5},{2,6},{3,7},{4,0},{5,1},{6,2},{7,3},{8,12},{9,13},{10,... | collective-permute-start | bytes 983048 | tf_op jit(solution)/shard_map/ppermute | solution.py:106
  53.5 7.6 %collective-permute-start.6 = (bf16[2,80,1024]{2,1,0:T(8,128)(2,1)S(1)}, bf16[2,80,1024]{2,1,0:T(8,128)(2,1)S(1)}, u32[]{:S(2)}, u32[]{:S(2)}) collective-permute-start(bf16[2,80,1024]{2,1,0:T(8,128)(2,1)S(1)} %slice.330), channel_id=1, source_target_pairs={{0,2},{1,3},{2,0},{3,1},{4,6},{5,7},{6,4},{7,5},{8,10},{9,11},{10,... | collective-permute-start | bytes 983048 | tf_op jit(solution)/shard_map/ppermute | solution.py:106
  55.0 8.7 %collective-permute-start.7 = (bf16[4,80,1024]{2,1,0:T(8,128)(2,1)S(1)}, bf16[4,80,1024]{2,1,0:T(8,128)(2,1)S(1)}, u32[]{:S(2)}, u32[]{:S(2)}) collective-permute-start(bf16[4,80,1024]{2,1,0:T(8,128)(2,1)S(1)} %pad_maximum_fusion.refs_0_), channel_id=1, source_target_pairs={{0,1},{1,0},{2,3},{3,2},{4,5},{5,4},{6,7},{7,6},{8,9},{9,8},{10,11... | collective-permute-start | bytes 1966088 | tf_op jit(solution)/shard_map/ppermute | solution.py:106
  55.1 12.2 %collective-permute-start.8 = (bf16[4,80,1024]{2,1,0:T(8,128)(2,1)S(1)}, bf16[4,80,1024]{2,1,0:T(8,128)(2,1)S(1)}, u32[]{:S(2)}, u32[]{:S(2)}) collective-permute-start(bf16[4,80,1024]{2,1,0:T(8,128)(2,1)S(1)} %collective-permute-done.3.refs_1_), channel_id=1, source_target_pairs={{0,1},{1,0},{2,3},{3,2},{4,5},{5,4},{6,7},{7,6},{8,9},{9,8},{10,11... | collective-permute-start | bytes 1966088 | tf_op jit(solution)/shard_map/ppermute | solution.py:106
  55.6 11.7 %collective-permute-start.9 = (bf16[4,80,1024]{2,1,0:T(8,128)(2,1)S(1)}, bf16[4,80,1024]{2,1,0:T(8,128)(2,1)S(1)}, u32[]{:S(2)}, u32[]{:S(2)}) collective-permute-start(bf16[4,80,1024]{2,1,0:T(8,128)(2,1)S(1)} %collective-permute-done.4.refs_2_), channel_id=1, source_target_pairs={{0,1},{1,0},{2,3},{3,2},{4,5},{5,4},{6,7},{7,6},{8,9},{9,8},{10,11... | collective-permute-start | bytes 1966088 | tf_op jit(solution)/shard_map/ppermute | solution.py:106
  60.1 5.2 %collective-permute-start.10 = (bf16[2,80,1024]{2,1,0:T(8,128)(2,1)S(1)}, bf16[2,80,1024]{2,1,0:T(8,128)(2,1)S(1)}, u32[]{:S(2)}, u32[]{:S(2)}) collective-permute-start(bf16[2,80,1024]{2,1,0:T(8,128)(2,1)S(1)} %collective-permute-done.5.refs_3_.refs_4_), channel_id=1, source_target_pairs={{0,1},{1,0},{2,3},{3,2},{4,5},{5,4},{6,7},{7,6},{8,9},{9,8},{10,11... | collective-permute-start | bytes 983048 | tf_op jit(solution)/shard_map/ppermute | solution.py:106
  61.1 4.8 %collective-permute-start.11 = (bf16[2,80,1024]{2,1,0:T(8,128)(2,1)S(1)}, bf16[2,80,1024]{2,1,0:T(8,128)(2,1)S(1)}, u32[]{:S(2)}, u32[]{:S(2)}) collective-permute-start(bf16[2,80,1024]{2,1,0:T(8,128)(2,1)S(1)} %collective-permute-done.6.refs_4_.refs_5_), channel_id=1, source_target_pairs={{0,1},{1,0},{2,3},{3,2},{4,5},{5,4},{6,7},{7,6},{8,9},{9,8},{10,11... | collective-permute-start | bytes 983048 | tf_op jit(solution)/shard_map/ppermute | solution.py:106
  63.8 35.1 %collective-permute-start.15 = (bf16[4,64,1024]{2,1,0:T(8,128)(2,1)}, bf16[4,64,1024]{2,1,0:T(8,128)(2,1)S(1)}, u32[]{:S(2)}, u32[]{:S(2)}) collective-permute-start(bf16[4,64,1024]{2,1,0:T(8,128)(2,1)} %join.1.refs_1_), channel_id=1, source_target_pairs={{0,2},{1,3},{2,0},{3,1},{4,6},{5,7},{6,4},{7,5},{8,10},{9,11},{10,... | collective-permute-start | bytes 1572872 | tf_op jit(solution)/shard_map/ppermute | solution.py:106
  65.3 33.9 %collective-permute-start.16 = (bf16[4,64,1024]{2,1,0:T(8,128)(2,1)}, bf16[4,64,1024]{2,1,0:T(8,128)(2,1)S(1)}, u32[]{:S(2)}, u32[]{:S(2)}) collective-permute-start(bf16[4,64,1024]{2,1,0:T(8,128)(2,1)} %join.1.refs_1_), channel_id=1, source_target_pairs={{0,4},{1,5},{2,6},{3,7},{4,0},{5,1},{6,2},{7,3},{8,12},{9,13},{10,... | collective-permute-start | bytes 1572872 | tf_op jit(solution)/shard_map/ppermute | solution.py:106
  65.9 33.5 %collective-permute-start.17 = (bf16[4,64,1024]{2,1,0:T(8,128)(2,1)}, bf16[4,64,1024]{2,1,0:T(8,128)(2,1)S(1)}, u32[]{:S(2)}, u32[]{:S(2)}) collective-permute-start(bf16[4,64,1024]{2,1,0:T(8,128)(2,1)} %join.1.refs_1_), channel_id=1, source_target_pairs={{0,6},{1,7},{2,4},{3,5},{4,2},{5,3},{6,0},{7,1},{8,14},{9,15},{10,... | collective-permute-start | bytes 1572872 | tf_op jit(solution)/shard_map/ppermute | solution.py:106
  67.3 33.5 %collective-permute-start.18 = (bf16[4,64,1024]{2,1,0:T(8,128)(2,1)}, bf16[4,64,1024]{2,1,0:T(8,128)(2,1)}, u32[]{:S(2)}, u32[]{:S(2)}) collective-permute-start(bf16[4,64,1024]{2,1,0:T(8,128)(2,1)} %join.1.refs_1_), channel_id=1, source_target_pairs={{0,1},{1,0},{2,3},{3,2},{4,5},{5,4},{6,7},{7,6},{8,9},{9,8},{10,11... | collective-permute-start | bytes 1572872 | tf_op jit(solution)/shard_map/ppermute | solution.py:106
  98.8 2.0 collective-permute-start.19
  99.2 2.4 collective-permute-start.20
  99.4 2.9 collective-permute-start.21
  142.4 17.8 %collective-permute-start.22 = (bf16[16,32,1024]{2,1,0:T(8,128)(2,1)}, bf16[16,32,1024]{2,1,0:T(8,128)(2,1)S(1)}, u32[]{:S(2)}, u32[]{:S(2)}) collective-permute-start(bf16[16,32,1024]{2,1,0:T(8,128)(2,1)} %get-tuple-element.80), channel_id=1, source_target_pairs={{0,1},{1,0},{2,3},{3,2},{4,5},{5,4},{6,7},{7,6},{8,9},{9,8},{10,11... | collective-permute-start | bytes 3145736 | tf_op jit(solution)/shard_map/ppermute | solution.py:106
  159.8 34.2 %collective-permute-start.23 = (bf16[16,32,1024]{2,1,0:T(8,128)(2,1)}, bf16[16,32,1024]{2,1,0:T(8,128)(2,1)S(1)}, u32[]{:S(2)}, u32[]{:S(2)}) collective-permute-start(bf16[16,32,1024]{2,1,0:T(8,128)(2,1)} %get-tuple-element.90), channel_id=1, source_target_pairs={{0,1},{1,0},{2,3},{3,2},{4,5},{5,4},{6,7},{7,6},{8,9},{9,8},{10,11... | collective-permute-start | bytes 3145736 | tf_op jit(solution)/shard_map/ppermute | solution.py:106
  164.1 26.8 %collective-permute-start.24 = (bf16[4,32,1024]{2,1,0:T(8,128)(2,1)}, bf16[4,32,1024]{2,1,0:T(8,128)(2,1)S(1)}, u32[]{:S(2)}, u32[]{:S(2)}) collective-permute-start(bf16[4,32,1024]{2,1,0:T(8,128)(2,1)} %get-tuple-element.81.refs_3_), channel_id=1, source_target_pairs={{0,2},{1,3},{2,0},{3,1},{4,6},{5,7},{6,4},{7,5},{8,10},{9,11},{10,... | collective-permute-start | bytes 786440 | tf_op jit(solution)/shard_map/ppermute | solution.py:106
  165.6 25.3 %collective-permute-start.25 = (bf16[4,32,1024]{2,1,0:T(8,128)(2,1)}, bf16[4,32,1024]{2,1,0:T(8,128)(2,1)S(1)}, u32[]{:S(2)}, u32[]{:S(2)}) collective-permute-start(bf16[4,32,1024]{2,1,0:T(8,128)(2,1)} %get-tuple-element.82.refs_4_), channel_id=1, source_target_pairs={{0,4},{1,5},{2,6},{3,7},{4,0},{5,1},{6,2},{7,3},{8,12},{9,13},{10,... | collective-permute-start | bytes 786440 | tf_op jit(solution)/shard_map/ppermute | solution.py:106
  166.3 24.7 %collective-permute-start.26 = (bf16[4,32,1024]{2,1,0:T(8,128)(2,1)}, bf16[4,32,1024]{2,1,0:T(8,128)(2,1)S(1)}, u32[]{:S(2)}, u32[]{:S(2)}) collective-permute-start(bf16[4,32,1024]{2,1,0:T(8,128)(2,1)} %get-tuple-element.83.refs_5_), channel_id=1, source_target_pairs={{0,6},{1,7},{2,4},{3,5},{4,2},{5,3},{6,0},{7,1},{8,14},{9,15},{10,... | collective-permute-start | bytes 786440 | tf_op jit(solution)/shard_map/ppermute | solution.py:106
  194.0 92.8 %reduce-scatter.3.cloned.1.call-start = ((), (), s32[]{:S(2)}) async-start(), calls=%async_computation.2 | async-start | bytes 655360 | tf_op jit(solution)/shard_map/reduce_scatter | solution.py:294
  198.0 14.1 %collective-permute-start.29 = (bf16[4,32,1024]{2,1,0:T(8,128)(2,1)}, bf16[4,32,1024]{2,1,0:T(8,128)(2,1)S(1)}, u32[]{:S(2)}, u32[]{:S(2)}) collective-permute-start(bf16[4,32,1024]{2,1,0:T(8,128)(2,1)} %get-tuple-element.91.refs_2_), channel_id=1, source_target_pairs={{0,2},{1,3},{2,0},{3,1},{4,6},{5,7},{6,4},{7,5},{8,10},{9,11},{10,... | collective-permute-start | bytes 786440 | tf_op jit(solution)/shard_map/ppermute | solution.py:106
  199.5 12.6 %collective-permute-start.30 = (bf16[4,32,1024]{2,1,0:T(8,128)(2,1)}, bf16[4,32,1024]{2,1,0:T(8,128)(2,1)S(1)}, u32[]{:S(2)}, u32[]{:S(2)}) collective-permute-start(bf16[4,32,1024]{2,1,0:T(8,128)(2,1)} %get-tuple-element.92.refs_3_), channel_id=1, source_target_pairs={{0,4},{1,5},{2,6},{3,7},{4,0},{5,1},{6,2},{7,3},{8,12},{9,13},{10,... | collective-permute-start | bytes 786440 | tf_op jit(solution)/shard_map/ppermute | solution.py:106
  200.1 12.5 %collective-permute-start.31 = (bf16[4,32,1024]{2,1,0:T(8,128)(2,1)}, bf16[4,32,1024]{2,1,0:T(8,128)(2,1)S(1)}, u32[]{:S(2)}, u32[]{:S(2)}) collective-permute-start(bf16[4,32,1024]{2,1,0:T(8,128)(2,1)} %get-tuple-element.93.refs_4_), channel_id=1, source_target_pairs={{0,6},{1,7},{2,4},{3,5},{4,2},{5,3},{6,0},{7,1},{8,14},{9,15},{10,... | collective-permute-start | bytes 786440 | tf_op jit(solution)/shard_map/ppermute | solution.py:106
  215.5 72.5 %all-gather.3.cloned.1.call-start = ((), (), s32[]{:S(2)}) async-start(), calls=%async_computation.4 | async-start | bytes 2433024 | tf_op jit(solution)/shard_map/all_gather | solution.py:912
  216.1 12.4 %collective-permute-start.27 = (bf16[16,48,1024]{2,1,0:T(8,128)(2,1)S(1)}, bf16[16,48,1024]{2,1,0:T(8,128)(2,1)S(1)}, u32[]{:S(2)}, u32[]{:S(2)}) collective-permute-start(bf16[16,48,1024]{2,1,0:T(8,128)(2,1)S(1)} %copy-done.47), channel_id=1, source_target_pairs={{0,1},{1,0},{2,3},{3,2},{4,5},{5,4},{6,7},{7,6},{8,9},{9,8},{10,11... | collective-permute-start | bytes 4718600 | tf_op jit(solution)/shard_map/ppermute | solution.py:106
  216.2 4.9 %collective-permute-start.28 = (bf16[16,32,1024]{2,1,0:T(8,128)(2,1)S(1)}, bf16[16,32,1024]{2,1,0:T(8,128)(2,1)S(1)}, u32[]{:S(2)}, u32[]{:S(2)}) collective-permute-start(bf16[16,32,1024]{2,1,0:T(8,128)(2,1)S(1)} %copy-done.48), channel_id=1, source_target_pairs={{0,1},{1,0},{2,3},{3,2},{4,5},{5,4},{6,7},{7,6},{8,9},{9,8},{10,11... | collective-permute-start | bytes 3145736 | tf_op jit(solution)/shard_map/ppermute | solution.py:106
  225.0 19.7 %collective-permute-start.35 = (bf16[4,32,1024]{2,1,0:T(8,128)(2,1)}, bf16[4,32,1024]{2,1,0:T(8,128)(2,1)S(1)}, u32[]{:S(2)}, u32[]{:S(2)}) collective-permute-start(bf16[4,32,1024]{2,1,0:T(8,128)(2,1)} %get-tuple-element.102.refs_3_), channel_id=1, source_target_pairs={{0,2},{1,3},{2,0},{3,1},{4,6},{5,7},{6,4},{7,5},{8,10},{9,11},{10,... | collective-permute-start | bytes 786440 | tf_op jit(solution)/shard_map/ppermute | solution.py:106
  226.5 18.1 %collective-permute-start.36 = (bf16[4,32,1024]{2,1,0:T(8,128)(2,1)}, bf16[4,32,1024]{2,1,0:T(8,128)(2,1)S(1)}, u32[]{:S(2)}, u32[]{:S(2)}) collective-permute-start(bf16[4,32,1024]{2,1,0:T(8,128)(2,1)} %get-tuple-element.103.refs_4_), channel_id=1, source_target_pairs={{0,4},{1,5},{2,6},{3,7},{4,0},{5,1},{6,2},{7,3},{8,12},{9,13},{10,... | collective-permute-start | bytes 786440 | tf_op jit(solution)/shard_map/ppermute | solution.py:106
  227.2 17.5 %collective-permute-start.37 = (bf16[4,32,1024]{2,1,0:T(8,128)(2,1)}, bf16[4,32,1024]{2,1,0:T(8,128)(2,1)S(1)}, u32[]{:S(2)}, u32[]{:S(2)}) collective-permute-start(bf16[4,32,1024]{2,1,0:T(8,128)(2,1)} %get-tuple-element.104.refs_5_), channel_id=1, source_target_pairs={{0,6},{1,7},{2,4},{3,5},{4,2},{5,3},{6,0},{7,1},{8,14},{9,15},{10,... | collective-permute-start | bytes 786440 | tf_op jit(solution)/shard_map/ppermute | solution.py:106
  247.7 6.8 %collective-permute-start.40 = (bf16[32,1024]{1,0:T(8,128)(2,1)}, bf16[32,1024]{1,0:T(8,128)(2,1)S(1)}, u32[]{:S(2)}, u32[]{:S(2)}) collective-permute-start(bf16[32,1024]{1,0:T(8,128)(2,1)} %get-tuple-element.111), channel_id=1, source_target_pairs={{0,24},{1,25},{2,26},{3,27},{4,28},{5,29},{6,30},{7,31},{8,16},{9,... | collective-permute-start | bytes 196616 | tf_op jit(solution)/shard_map/ppermute | solution.py:106
  249.9 11.2 %collective-permute-start.32 = (bf16[4,48,1024]{2,1,0:T(8,128)(2,1)S(1)}, bf16[4,48,1024]{2,1,0:T(8,128)(2,1)S(1)}, u32[]{:S(2)}, u32[]{:S(2)}) collective-permute-start(bf16[4,48,1024]{2,1,0:T(8,128)(2,1)S(1)} %copy-done.29), channel_id=1, source_target_pairs={{0,2},{1,3},{2,0},{3,1},{4,6},{5,7},{6,4},{7,5},{8,10},{9,11},{10,... | collective-permute-start | bytes 1179656 | tf_op jit(solution)/shard_map/ppermute | solution.py:106
  251.4 12.4 %collective-permute-start.33 = (bf16[4,48,1024]{2,1,0:T(8,128)(2,1)S(1)}, bf16[4,48,1024]{2,1,0:T(8,128)(2,1)S(1)}, u32[]{:S(2)}, u32[]{:S(2)}) collective-permute-start(bf16[4,48,1024]{2,1,0:T(8,128)(2,1)S(1)} %copy-done.28), channel_id=1, source_target_pairs={{0,4},{1,5},{2,6},{3,7},{4,0},{5,1},{6,2},{7,3},{8,12},{9,13},{10,... | collective-permute-start | bytes 1179656 | tf_op jit(solution)/shard_map/ppermute | solution.py:106
  252.0 21.8 %collective-permute-start.34 = (bf16[4,48,1024]{2,1,0:T(8,128)(2,1)S(1)}, bf16[4,48,1024]{2,1,0:T(8,128)(2,1)S(1)}, u32[]{:S(2)}, u32[]{:S(2)}) collective-permute-start(bf16[4,48,1024]{2,1,0:T(8,128)(2,1)S(1)} %copy-done.27), channel_id=1, source_target_pairs={{0,6},{1,7},{2,4},{3,5},{4,2},{5,3},{6,0},{7,1},{8,14},{9,15},{10,... | collective-permute-start | bytes 1179656 | tf_op jit(solution)/shard_map/ppermute | solution.py:106
  253.3 5.4 %collective-permute-start.39 = (bf16[32,1024]{1,0:T(8,128)(2,1)}, bf16[32,1024]{1,0:T(8,128)(2,1)S(1)}, u32[]{:S(2)}, u32[]{:S(2)}) collective-permute-start(bf16[32,1024]{1,0:T(8,128)(2,1)} %get-tuple-element.110), channel_id=1, source_target_pairs={{0,16},{1,17},{2,18},{3,19},{4,20},{5,21},{6,22},{7,23},{8,24},{9,... | collective-permute-start | bytes 196616 | tf_op jit(solution)/shard_map/ppermute | solution.py:106
  254.5 5.0 %collective-permute-start.38 = (bf16[32,1024]{1,0:T(8,128)(2,1)}, bf16[32,1024]{1,0:T(8,128)(2,1)S(1)}, u32[]{:S(2)}, u32[]{:S(2)}) collective-permute-start(bf16[32,1024]{1,0:T(8,128)(2,1)} %get-tuple-element.109), channel_id=1, source_target_pairs={{0,8},{1,9},{2,10},{3,11},{4,12},{5,13},{6,14},{7,15},{8,0},{9,1},... | collective-permute-start | bytes 196616 | tf_op jit(solution)/shard_map/ppermute | solution.py:106
  276.9 6.7 %collective-permute-start.43 = (bf16[48,1024]{1,0:T(8,128)(2,1)}, bf16[48,1024]{1,0:T(8,128)(2,1)S(1)}, u32[]{:S(2)}, u32[]{:S(2)}) collective-permute-start(bf16[48,1024]{1,0:T(8,128)(2,1)} %get-tuple-element.115), channel_id=1, source_target_pairs={{0,24},{1,25},{2,26},{3,27},{4,28},{5,29},{6,30},{7,31},{8,16},{9,... | collective-permute-start | bytes 294920 | tf_op jit(solution)/shard_map/ppermute | solution.py:106
  278.5 7.1 %collective-permute-start.42 = (bf16[48,1024]{1,0:T(8,128)(2,1)}, bf16[48,1024]{1,0:T(8,128)(2,1)S(1)}, u32[]{:S(2)}, u32[]{:S(2)}) collective-permute-start(bf16[48,1024]{1,0:T(8,128)(2,1)} %get-tuple-element.114), channel_id=1, source_target_pairs={{0,16},{1,17},{2,18},{3,19},{4,20},{5,21},{6,22},{7,23},{8,24},{9,... | collective-permute-start | bytes 294920 | tf_op jit(solution)/shard_map/ppermute | solution.py:106
  278.5 7.1 %collective-permute-start.41 = (bf16[48,1024]{1,0:T(8,128)(2,1)}, bf16[48,1024]{1,0:T(8,128)(2,1)S(1)}, u32[]{:S(2)}, u32[]{:S(2)}) collective-permute-start(bf16[48,1024]{1,0:T(8,128)(2,1)} %get-tuple-element.113), channel_id=1, source_target_pairs={{0,8},{1,9},{2,10},{3,11},{4,12},{5,13},{6,14},{7,15},{8,0},{9,1},... | collective-permute-start | bytes 294920 | tf_op jit(solution)/shard_map/ppermute | solution.py:106
  (48 other events, 281.4 us)
Sparse Core Ops, SparseCore 0:
  194.1 20.5 reduce-scatter.4
  217.5 20.0 reduce-scatter.2
Sparse Core Ops, SparseCore 1:
  218.9 60.8 all-gather.2

commit v3 on v2

--- a/solution.py
+++ b/solution.py
@@ -915,8 +915,9 @@
 
     own_top = z_scatter(top_total, groups, count)
     own_deep = z_scatter(deep_total, groups, count)
-    own_two = z_stage(plane_stage_z(two_plane, groups, count, [feature_grad]), groups, count)
-    own_last = z_stage(plane_stage_z(last_plane, groups, count, [feature_grad, own_two]), groups, count)
+    two_z = plane_stage_z(two_plane, groups, count, [feature_grad])
+    own_two = z_stage(two_z, groups, count)
+    own_last = z_stage(plane_stage_z(last_plane, groups, count, [feature_grad] + two_z[1:]), groups, count)
     own_one = own_last[:rows]
     spills = own_last[rows : rows + MISC_ROW]
     row = lax.broadcasted_iota(jnp.int32, spills.shape, 0)

time: 308 us -> 301 us (0.977)
  waiting for transfers between devices: 53.6 us -> 47.5 us
    ppermute x44, waiting for transfers between devices: 53 us -> 46.8 us  [swap(): return lax.ppermute(value, AXES, [(k, k ^ mask) for k in range(count)])]
    unnamed x104 -> x96, local copies, waits for them, and re-layouts: 10.6 us -> 10.5 us
  transfers between devices with their start and end apart: 47 -> 47, of which waited for: 16 -> 13; matrix products, arithmetic and copies ran while one was open for 5% -> 4% of each run, Pallas kernels for 36% -> 36%
where the time goes in v3:
time: 301 us; the launch traced here: 300 us
  Pallas kernels  147 us (49%)
  waiting for transfers between devices  47.5 us (16%)
  starting transfers between devices  45.4 us (15%)
  local copies, waits for them, and re-layouts  33.4 us (11%)
  between operations  17 us (6%)
  other arithmetic  9.22 us (3%)
    pallas_call x6, Pallas kernels, run(): pl.pallas_call(kernel, grid=(batch // tile,), in_specs=in_specs, out_spec...  114 us
    ppermute x44, waiting for transfers between devices, swap(): return lax.ppermute(value, AXES, [(k, k ^ mask) for k in range(count)])  46.8 us
    ppermute x44, starting transfers between devices, swap(): return lax.ppermute(value, AXES, [(k, k ^ mask) for k in range(count)])  45.3 us
    pallas_call x8, Pallas kernels, adder(): pl.pallas_call(kernel, out_shape=outs, in_specs=[VMEM] * len(ins) + [pl.B...  21.3 us
    unnamed x96, local copies, waits for them, and re-layouts  10.5 us
    pallas_call x2, Pallas kernels, place(): pl.pallas_call(kernel, out_shape=out_shape, in_specs=[SMEM] + [VMEM] * (l...  9.97 us
    slice x7, local copies, waits for them, and re-layouts, local(): piece = [master[a:a + l] for a, l in zip(starts, sizes)]  6.66 us
  transfers between devices with their start and end apart: 47, of which 13 were waited for; matrix products, arithmetic and copies ran while one was open for 4% of the time, Pallas kernels for 36%

profile of v3, /device:TPU:0, one launch (start us, length us, event | category | flops | bytes accessed | tf_op | source)
XLA Modules:
  0.0 299.8 jit_solution(14457552980076626011)
XLA Ops:
  13.1 1.3 slice.265
  16.9 5.1 %collective-permute-start.2 = (bf16[80,1024]{1,0:T(8,128)(2,1)S(1)}, bf16[80,1024]{1,0:T(8,128)(2,1)S(1)}, u32[]{:S(2)}, u32[]{:S(2)}) collective-permute-start(bf16[80,1024]{1,0:T(8,128)(2,1)S(1)} %concatenate.78), channel_id=1, source_target_pairs={{0,24},{1,25},{2,26},{3,27},{4,28},{5,29},{6,30},{7,31},{8,16},{9,... | collective-permute-start | bytes 491528 | tf_op jit(solution)/shard_map/ppermute | solution.py:106
  23.8 3.3 %collective-permute-done.2 = bf16[80,1024]{1,0:T(8,128)(2,1)S(1)} collective-permute-done((bf16[80,1024]{1,0:T(8,128)(2,1)S(1)}, bf16[80,1024]{1,0:T(8,128)(2,1)S(1)}, u32[]{:S(2)}, u32[]{:S(2)}) %collective-permute-start.2) | collective-permute-done | bytes 163872 | tf_op jit(solution)/shard_map/ppermute | solution.py:106
  27.1 8.8 %collective-permute-done.1 = bf16[80,1024]{1,0:T(8,128)(2,1)S(1)} collective-permute-done((bf16[80,1024]{1,0:T(8,128)(2,1)S(1)}, bf16[80,1024]{1,0:T(8,128)(2,1)S(1)}, u32[]{:S(2)}, u32[]{:S(2)}) %collective-permute-start.1) | collective-permute-done | bytes 163872 | tf_op jit(solution)/shard_map/ppermute | solution.py:106
  36.0 1.6 collective-permute-start.3
  37.6 1.5 collective-permute-start.4
  39.4 3.0 %collective-permute-start.13 = (bf16[64,1024]{1,0:T(8,128)(2,1)S(1)}, bf16[64,1024]{1,0:T(8,128)(2,1)S(1)}, u32[]{:S(2)}, u32[]{:S(2)}) collective-permute-start(bf16[64,1024]{1,0:T(8,128)(2,1)S(1)} %constant_dynamic-update-slice_fusion.refs_0_), channel_id=1, source_target_pairs={{0,16},{1,17},{2,18},{3,19},{4,20},{5,21},{6,22},{7,23},{8,24},{9,... | collective-permute-start | bytes 393224 | tf_op jit(solution)/shard_map/ppermute | solution.py:106
  42.4 1.3 collective-permute-start.14
  43.8 8.1 %collective-permute-done.3.refs_1_ = bf16[4,80,1024]{2,1,0:T(8,128)(2,1)S(1)} collective-permute-done((bf16[4,80,1024]{2,1,0:T(8,128)(2,1)S(1)}, bf16[4,80,1024]{2,1,0:T(8,128)(2,1)S(1)}, u32[]{:S(2)}, u32[]{:S(2)}) %collective-permute-start.3) | collective-permute-done | bytes 655392 | tf_op jit(solution)/shard_map/ppermute | solution.py:106
  51.9 1.6 collective-permute-start.5
  53.5 1.6 collective-permute-start.6
  55.8 4.3 %collective-permute-done.5.refs_3_.refs_4_ = bf16[2,80,1024]{2,1,0:T(8,128)(2,1)S(1)} collective-permute-done((bf16[2,80,1024]{2,1,0:T(8,128)(2,1)S(1)}, bf16[2,80,1024]{2,1,0:T(8,128)(2,1)S(1)}, u32[]{:S(2)}, u32[]{:S(2)}) %collective-permute-start.5) | collective-permute-done | bytes 327712 | tf_op jit(solution)/shard_map/ppermute | solution.py:106
  61.8 1.9 join.1.refs_1_
  63.7 1.5 collective-permute-start.15
  65.9 1.3 collective-permute-start.17
  68.4 5.3 %place.2 = (bf16[32,32,1024]{2,1,0:T(8,128)(2,1)}, bf16[32,32,1024]{2,1,0:T(8,128)(2,1)}, bf16[32,16,1024]{2,1,0:T(8,128)(2,1)}) custom-call(s32[1]{0:T(128)} %bitcast.index_ref.k_ref, bf16[4,80,1024]{2,1,0:T(8,128)(2,1)} %copy-done, bf16[4,80,1024]{2,1,0:T(8,128)(2,1)} %copy-done.3, bf16[4,80,1024]{2,1,0:T(8,128)(2,1)} %copy-done.4, ...), custom_call_target="tpu_custom_call" | custom-call | tf_op jit(solution)/shard_map/place/pallas_call | solution.py:181
  80.7 18.1 %forward_cross.1 = (bf16[1040,2048]{1,0:T(8,128)(2,1)}, bf16[1040,2048]{1,0:T(8,128)(2,1)}, bf16[1040,2048]{1,0:T(8,128)(2,1)}, bf16[1040,2048]{1,0:T(8,128)(2,1)}, bf16[1040,2048]{1,0:T(8,128)(2,1)}) custom-call(bf16[1027,2048]{1,0:T(8,128)(2,1)} %bitcast.90, bf16[1024,1024]{1,0:T(8,128)(2,1)} %bitcast.69, ...), custom_call_target="tpu_custom_call" | custom-call | flops 8860467200 | bytes 30298112 | tf_op jit(solution)/shard_map/forward_cross/pallas_call | solution.py:339
  103.1 4.7 %place.3 = (bf16[32,32,1024]{2,1,0:T(8,128)(2,1)}, bf16[32,32,1024]{2,1,0:T(8,128)(2,1)}) custom-call(s32[1]{0:T(128)} %bitcast.index_ref.k_ref, bf16[32,16,1024]{2,1,0:T(8,128)(2,1)} %get-tuple-element.63.refs_0_, bf16[4,64,1024]{2,1,0:T(8,128)(2,1)} %join.1.refs_1_, bf16[4,64,1024]{2,1,0:T(8,128)(2,1)} %copy-done.17, bf16[4,64,1024]{2,1,0:T(8,128)(2,1)} %copy-done.18, ...), custom_call_target="tpu_custom_call" | custom-call | tf_op jit(solution)/shard_map/place/pallas_call | solution.py:181
  108.5 33.8 %deep.1 = (f32[1,2048]{1,0:T(1,128)}, bf16[1024,2048]{1,0:T(8,128)(2,1)}, f32[16,1024]{1,0:T(8,128)}, f32[8,512]{1,0:T(8,128)}, f32[16,32,1024]{2,1,0:T(8,128)},...) custom-call(s32[1]{0:T(128)} %bitcast.index_ref.k_ref, bf16[1040,2048]{1,0:T(8,128)(2,1)} %get-tuple-element.65.l_ref, ...), custom_call_target="tpu_custom_call" | custom-call | flops 17179869184 | bytes 17747972 | tf_op jit(solution)/shard_map/deep/pallas_call | solution.py:339
  142.7 17.1 %back_deep.1 = (f32[1040,2048]{1,0:T(8,128)}, bf16[1040,2048]{1,0:T(8,128)(2,1)}, f32[16,1024]{1,0:T(8,128)}, f32[16,32,1024]{2,1,0:T(8,128)}, bf16[16,32,1024]{2,1,0:T(8,128)(2,1)}, /*index=5*/f32[32,8,1024]{2,1,0:T(8,128)}) custom-call(s32[1]{0:T(128)} %bitcast.index_ref.k_ref, bf16[1024,2048]{1,0:T(8,128)(2,1)} %get-tuple-element.69.g_ref, ...), custom_call_target="tpu_custom_call" | custom-call | flops 8724152320 | bytes 32112644 | tf_op jit(solution)/shard_map/back_deep/pallas_call | solution.py:339
  161.2 2.9 core_sum.4
  164.1 1.5 collective-permute-start.24
  166.3 1.3 collective-permute-start.26
  167.6 23.3 %back_two.1 = (bf16[1040,2048]{1,0:T(8,128)(2,1)}, bf16[1040,2048]{1,0:T(8,128)(2,1)}, f32[16,1152]{1,0:T(8,128)}, f32[16,32,1024]{2,1,0:T(8,128)}, bf16[16,32,1...) custom-call(s32[1]{0:T(128)} %bitcast.index_ref.k_ref, bf16[1040,2048]{1,0:T(8,128)(2,1)} %get-tuple-element.71.refs_2_.g_ref, ...), custom_call_target="tpu_custom_call" | custom-call | flops 8860467200 | bytes 45936644 | tf_op jit(solution)/shard_map/back_two/pallas_call | solution.py:339
  191.8 2.2 plane_sum.4.refs_5_
  195.0 2.9 core_sum.5
  198.0 1.5 collective-permute-start.29
  200.1 1.3 collective-permute-start.31
  201.4 10.6 %grad_one.1 = (f32[16,48,1024]{2,1,0:T(8,128)}, bf16[16,48,1024]{2,1,0:T(8,128)(2,1)}) custom-call(s32[1]{0:T(128)} %bitcast.index_ref.k_ref, bf16[1040,2048]{1,0:T(8,128)(2,1)} %get-tuple-element.85.refs_2_.refs_4_.g_ref, bf16[1040,2048]{1,0:T(8,128)(2,1)} %get-tuple-element.70.x_ref, f32[32,8,1024]{2,1,0:T(8,128)} %get-tuple-element.87.refs_0_, ...), custom_call_target="tpu_custom_call" | custom-call | flops 4430233600 | bytes 16646148 | tf_op jit(solution)/shard_map/grad_one/pallas_call | solution.py:339
  213.3 2.2 plane_sum.5.refs_6_
  216.6 4.4 %collective-permute-done.28.refs_1_ = bf16[16,32,1024]{2,1,0:T(8,128)(2,1)S(1)} collective-permute-done((bf16[16,32,1024]{2,1,0:T(8,128)(2,1)S(1)}, bf16[16,32,1024]{2,1,0:T(8,128)(2,1)S(1)}, u32[]{:S(2)}, u32[]{:S(2)}) %collective-permute-start.28) | collective-permute-done | bytes 1048608 | tf_op jit(solution)/shard_map/ppermute | solution.py:106
  222.0 2.9 core_sum.7
  225.0 1.5 collective-permute-start.35
  229.6 3.7 %core_sum.6 = (f32[4,48,1024]{2,1,0:T(8,128)}, bf16[4,48,1024]{2,1,0:T(8,128)(2,1)}, bf16[4,48,1024]{2,1,0:T(8,128)(2,1)}, bf16[4,48,1024]{2,1,0:T(8,128)(2,1)}) custom-call(f32[16,48,1024]{2,1,0:T(8,128)} %get-tuple-element.95.refs_0_.refs_2_.refs_4_, bf16[16,48,1024]{2,1,0:T(8,128)(2,1)} %copy-done.2), custom_call_target="tpu_custom_call" | custom-call | tf_op jit(solution)/shard_map/core_sum/pallas_call | solution.py:225
  233.3 1.5 collective-permute-start.32
  236.8 11.2 %back_one.1.refs_4_ = f32[1027,2048]{1,0:T(8,128)} custom-call(bf16[1040,2048]{1,0:T(8,128)(2,1)} %get-tuple-element.85.refs_2_.refs_4_.g_ref, bf16[1040,2048]{1,0:T(8,128)(2,1)} %get-tuple-element.86.p_ref, bf16[1024,1024]{1,0:T(8,128)(2,1)} %bitcast.70, bf16[128,1024]{1,0:T(8,128)(2,1)} %get-tuple-element.150.refs_1_.t_ref, ...), custom_call_target="tpu_custom_call" | custom-call | flops 4430233600 | bytes 21819392 | tf_op jit(solution)/shard_map/back_one/pallas_call | solution.py:339
  248.8 2.0 plane_sum.6
  250.8 2.1 collective-permute-start.43
  253.0 2.2 collective-permute-start.41
  256.2 3.7 %collective-permute-done.34.refs_3_ = bf16[4,48,1024]{2,1,0:T(8,128)(2,1)S(1)} collective-permute-done((bf16[4,48,1024]{2,1,0:T(8,128)(2,1)}, bf16[4,48,1024]{2,1,0:T(8,128)(2,1)S(1)}, u32[]{:S(2)}, u32[]{:S(2)}) %collective-permute-start.34) | collective-permute-done | bytes 393248 | tf_op jit(solution)/shard_map/ppermute | solution.py:106
  260.6 2.3 plane_sum.7
  262.9 2.2 collective-permute-start.40
  265.1 2.2 collective-permute-start.38
  267.4 5.0 %collective-permute-done.40 = bf16[48,1024]{1,0:T(8,128)(2,1)S(1)} collective-permute-done((bf16[48,1024]{1,0:T(8,128)(2,1)}, bf16[48,1024]{1,0:T(8,128)(2,1)S(1)}, u32[]{:S(2)}, u32[]{:S(2)}) %collective-permute-start.40) | collective-permute-done | bytes 98336 | tf_op jit(solution)/shard_map/ppermute | solution.py:106
  272.4 6.1 %collective-permute-done.39 = bf16[48,1024]{1,0:T(8,128)(2,1)S(1)} collective-permute-done((bf16[48,1024]{1,0:T(8,128)(2,1)}, bf16[48,1024]{1,0:T(8,128)(2,1)S(1)}, u32[]{:S(2)}, u32[]{:S(2)}) %collective-permute-start.39) | collective-permute-done | bytes 98336 | tf_op jit(solution)/shard_map/ppermute | solution.py:106
  281.1 1.8 reduce_sum.29
  285.5 3.4 %concatenate.90 = f32[131717]{0:T(1024)S(1)} concatenate(f32[32961]{0:T(1024)S(1)} %dynamic_slice.31, f32[33]{0:T(128)S(1)} %get-tuple-element.147, f32[32961]{0:T(1024)S(1)} %dynamic_slice.33, f32[33]{0:T(128)S(1)} %get-tuple-element.146, f32[32864]{0:T(1024)S(1)} %dynamic_slice.34, f32[32]{0:T(128)S(1)} %get-tuple-element.145, f32[32768]{0:T(1024)S(1)} %bitcast.77, ...), dimensions={0} | concatenate | bytes 1053736 | tf_op jit(solution)/shard_map/concatenate | solution.py:942
  288.9 1.4 multiply_subtract_fusion
  (288 shorter events, 48.0 us)
Async XLA Ops:
  8.0 47.7 %copy-start.42 = (s32[2048]{0:T(1024)S(1)}, s32[2048]{0:T(1024)}, u32[]{:S(2)}) copy-start(s32[2048]{0:T(1024)} %param.8) | copy-start | bytes 24580
  8.0 247.2 %reduce-scatter.5.cloned.1.call-start = ((), (), s32[]{:S(2)}) async-start(), calls=%async_computation.3 | async-start | bytes 655360 | tf_op jit(solution)/shard_map/reduce_scatter | solution.py:294
  16.9 10.2 %collective-permute-start.2 = (bf16[80,1024]{1,0:T(8,128)(2,1)S(1)}, bf16[80,1024]{1,0:T(8,128)(2,1)S(1)}, u32[]{:S(2)}, u32[]{:S(2)}) collective-permute-start(bf16[80,1024]{1,0:T(8,128)(2,1)S(1)} %concatenate.78), channel_id=1, source_target_pairs={{0,24},{1,25},{2,26},{3,27},{4,28},{5,29},{6,30},{7,31},{8,16},{9,... | collective-permute-start | bytes 491528 | tf_op jit(solution)/shard_map/ppermute | solution.py:106
  22.0 13.9 %collective-permute-start.1 = (bf16[80,1024]{1,0:T(8,128)(2,1)S(1)}, bf16[80,1024]{1,0:T(8,128)(2,1)S(1)}, u32[]{:S(2)}, u32[]{:S(2)}) collective-permute-start(bf16[80,1024]{1,0:T(8,128)(2,1)S(1)} %concatenate.78), channel_id=1, source_target_pairs={{0,16},{1,17},{2,18},{3,19},{4,20},{5,21},{6,22},{7,23},{8,24},{9,... | collective-permute-start | bytes 491528 | tf_op jit(solution)/shard_map/ppermute | solution.py:106
  22.0 13.9 %collective-permute-start = (bf16[80,1024]{1,0:T(8,128)(2,1)S(1)}, bf16[80,1024]{1,0:T(8,128)(2,1)S(1)}, u32[]{:S(2)}, u32[]{:S(2)}) collective-permute-start(bf16[80,1024]{1,0:T(8,128)(2,1)S(1)} %concatenate.78), channel_id=1, source_target_pairs={{0,8},{1,9},{2,10},{3,11},{4,12},{5,13},{6,14},{7,15},{8,0},{9,1},... | collective-permute-start | bytes 491528 | tf_op jit(solution)/shard_map/ppermute | solution.py:106
  36.0 15.9 %collective-permute-start.3 = (bf16[4,80,1024]{2,1,0:T(8,128)(2,1)S(1)}, bf16[4,80,1024]{2,1,0:T(8,128)(2,1)S(1)}, u32[]{:S(2)}, u32[]{:S(2)}) collective-permute-start(bf16[4,80,1024]{2,1,0:T(8,128)(2,1)S(1)} %pad_maximum_fusion.refs_0_), channel_id=1, source_target_pairs={{0,2},{1,3},{2,0},{3,1},{4,6},{5,7},{6,4},{7,5},{8,10},{9,11},{10,... | collective-permute-start | bytes 1966088 | tf_op jit(solution)/shard_map/ppermute | solution.py:106
  37.6 15.9 %collective-permute-start.4 = (bf16[4,80,1024]{2,1,0:T(8,128)(2,1)S(1)}, bf16[4,80,1024]{2,1,0:T(8,128)(2,1)S(1)}, u32[]{:S(2)}, u32[]{:S(2)}) collective-permute-start(bf16[4,80,1024]{2,1,0:T(8,128)(2,1)S(1)} %pad_maximum_fusion.refs_0_), channel_id=1, source_target_pairs={{0,4},{1,5},{2,6},{3,7},{4,0},{5,1},{6,2},{7,3},{8,12},{9,13},{10,... | collective-permute-start | bytes 1966088 | tf_op jit(solution)/shard_map/ppermute | solution.py:106
  39.3 15.7 %collective-permute-start.12 = (bf16[64,1024]{1,0:T(8,128)(2,1)S(1)}, bf16[64,1024]{1,0:T(8,128)(2,1)S(1)}, u32[]{:S(2)}, u32[]{:S(2)}) collective-permute-start(bf16[64,1024]{1,0:T(8,128)(2,1)S(1)} %constant_dynamic-update-slice_fusion.refs_0_), channel_id=1, source_target_pairs={{0,8},{1,9},{2,10},{3,11},{4,12},{5,13},{6,14},{7,15},{8,0},{9,1},... | collective-permute-start | bytes 393224 | tf_op jit(solution)/shard_map/ppermute | solution.py:106
  39.4 15.7 %collective-permute-start.13 = (bf16[64,1024]{1,0:T(8,128)(2,1)S(1)}, bf16[64,1024]{1,0:T(8,128)(2,1)S(1)}, u32[]{:S(2)}, u32[]{:S(2)}) collective-permute-start(bf16[64,1024]{1,0:T(8,128)(2,1)S(1)} %constant_dynamic-update-slice_fusion.refs_0_), channel_id=1, source_target_pairs={{0,16},{1,17},{2,18},{3,19},{4,20},{5,21},{6,22},{7,23},{8,24},{9,... | collective-permute-start | bytes 393224 | tf_op jit(solution)/shard_map/ppermute | solution.py:106
  42.4 13.2 %collective-permute-start.14 = (bf16[64,1024]{1,0:T(8,128)(2,1)S(1)}, bf16[64,1024]{1,0:T(8,128)(2,1)S(1)}, u32[]{:S(2)}, u32[]{:S(2)}) collective-permute-start(bf16[64,1024]{1,0:T(8,128)(2,1)S(1)} %constant_dynamic-update-slice_fusion.refs_0_), channel_id=1, source_target_pairs={{0,24},{1,25},{2,26},{3,27},{4,28},{5,29},{6,30},{7,31},{8,16},{9,... | collective-permute-start | bytes 393224 | tf_op jit(solution)/shard_map/ppermute | solution.py:106
  51.9 8.2 %collective-permute-start.5 = (bf16[2,80,1024]{2,1,0:T(8,128)(2,1)S(1)}, bf16[2,80,1024]{2,1,0:T(8,128)(2,1)S(1)}, u32[]{:S(2)}, u32[]{:S(2)}) collective-permute-start(bf16[2,80,1024]{2,1,0:T(8,128)(2,1)S(1)} %slice.329), channel_id=1, source_target_pairs={{0,4},{1,5},{2,6},{3,7},{4,0},{5,1},{6,2},{7,3},{8,12},{9,13},{10,... | collective-permute-start | bytes 983048 | tf_op jit(solution)/shard_map/ppermute | solution.py:106
  53.5 7.6 %collective-permute-start.6 = (bf16[2,80,1024]{2,1,0:T(8,128)(2,1)S(1)}, bf16[2,80,1024]{2,1,0:T(8,128)(2,1)S(1)}, u32[]{:S(2)}, u32[]{:S(2)}) collective-permute-start(bf16[2,80,1024]{2,1,0:T(8,128)(2,1)S(1)} %slice.330), channel_id=1, source_target_pairs={{0,2},{1,3},{2,0},{3,1},{4,6},{5,7},{6,4},{7,5},{8,10},{9,11},{10,... | collective-permute-start | bytes 983048 | tf_op jit(solution)/shard_map/ppermute | solution.py:106
  55.0 8.7 %collective-permute-start.7 = (bf16[4,80,1024]{2,1,0:T(8,128)(2,1)S(1)}, bf16[4,80,1024]{2,1,0:T(8,128)(2,1)S(1)}, u32[]{:S(2)}, u32[]{:S(2)}) collective-permute-start(bf16[4,80,1024]{2,1,0:T(8,128)(2,1)S(1)} %pad_maximum_fusion.refs_0_), channel_id=1, source_target_pairs={{0,1},{1,0},{2,3},{3,2},{4,5},{5,4},{6,7},{7,6},{8,9},{9,8},{10,11... | collective-permute-start | bytes 1966088 | tf_op jit(solution)/shard_map/ppermute | solution.py:106
  55.1 12.2 %collective-permute-start.8 = (bf16[4,80,1024]{2,1,0:T(8,128)(2,1)S(1)}, bf16[4,80,1024]{2,1,0:T(8,128)(2,1)S(1)}, u32[]{:S(2)}, u32[]{:S(2)}) collective-permute-start(bf16[4,80,1024]{2,1,0:T(8,128)(2,1)S(1)} %collective-permute-done.3.refs_1_), channel_id=1, source_target_pairs={{0,1},{1,0},{2,3},{3,2},{4,5},{5,4},{6,7},{7,6},{8,9},{9,8},{10,11... | collective-permute-start | bytes 1966088 | tf_op jit(solution)/shard_map/ppermute | solution.py:106
  55.6 11.7 %collective-permute-start.9 = (bf16[4,80,1024]{2,1,0:T(8,128)(2,1)S(1)}, bf16[4,80,1024]{2,1,0:T(8,128)(2,1)S(1)}, u32[]{:S(2)}, u32[]{:S(2)}) collective-permute-start(bf16[4,80,1024]{2,1,0:T(8,128)(2,1)S(1)} %collective-permute-done.4.refs_2_), channel_id=1, source_target_pairs={{0,1},{1,0},{2,3},{3,2},{4,5},{5,4},{6,7},{7,6},{8,9},{9,8},{10,11... | collective-permute-start | bytes 1966088 | tf_op jit(solution)/shard_map/ppermute | solution.py:106
  60.1 5.2 %collective-permute-start.10 = (bf16[2,80,1024]{2,1,0:T(8,128)(2,1)S(1)}, bf16[2,80,1024]{2,1,0:T(8,128)(2,1)S(1)}, u32[]{:S(2)}, u32[]{:S(2)}) collective-permute-start(bf16[2,80,1024]{2,1,0:T(8,128)(2,1)S(1)} %collective-permute-done.5.refs_3_.refs_4_), channel_id=1, source_target_pairs={{0,1},{1,0},{2,3},{3,2},{4,5},{5,4},{6,7},{7,6},{8,9},{9,8},{10,11... | collective-permute-start | bytes 983048 | tf_op jit(solution)/shard_map/ppermute | solution.py:106
  61.1 4.8 %collective-permute-start.11 = (bf16[2,80,1024]{2,1,0:T(8,128)(2,1)S(1)}, bf16[2,80,1024]{2,1,0:T(8,128)(2,1)S(1)}, u32[]{:S(2)}, u32[]{:S(2)}) collective-permute-start(bf16[2,80,1024]{2,1,0:T(8,128)(2,1)S(1)} %collective-permute-done.6.refs_4_.refs_5_), channel_id=1, source_target_pairs={{0,1},{1,0},{2,3},{3,2},{4,5},{5,4},{6,7},{7,6},{8,9},{9,8},{10,11... | collective-permute-start | bytes 983048 | tf_op jit(solution)/shard_map/ppermute | solution.py:106
  63.7 35.1 %collective-permute-start.15 = (bf16[4,64,1024]{2,1,0:T(8,128)(2,1)}, bf16[4,64,1024]{2,1,0:T(8,128)(2,1)S(1)}, u32[]{:S(2)}, u32[]{:S(2)}) collective-permute-start(bf16[4,64,1024]{2,1,0:T(8,128)(2,1)} %join.1.refs_1_), channel_id=1, source_target_pairs={{0,2},{1,3},{2,0},{3,1},{4,6},{5,7},{6,4},{7,5},{8,10},{9,11},{10,... | collective-permute-start | bytes 1572872 | tf_op jit(solution)/shard_map/ppermute | solution.py:106
  65.3 33.9 %collective-permute-start.16 = (bf16[4,64,1024]{2,1,0:T(8,128)(2,1)}, bf16[4,64,1024]{2,1,0:T(8,128)(2,1)S(1)}, u32[]{:S(2)}, u32[]{:S(2)}) collective-permute-start(bf16[4,64,1024]{2,1,0:T(8,128)(2,1)} %join.1.refs_1_), channel_id=1, source_target_pairs={{0,4},{1,5},{2,6},{3,7},{4,0},{5,1},{6,2},{7,3},{8,12},{9,13},{10,... | collective-permute-start | bytes 1572872 | tf_op jit(solution)/shard_map/ppermute | solution.py:106
  65.9 33.5 %collective-permute-start.17 = (bf16[4,64,1024]{2,1,0:T(8,128)(2,1)}, bf16[4,64,1024]{2,1,0:T(8,128)(2,1)S(1)}, u32[]{:S(2)}, u32[]{:S(2)}) collective-permute-start(bf16[4,64,1024]{2,1,0:T(8,128)(2,1)} %join.1.refs_1_), channel_id=1, source_target_pairs={{0,6},{1,7},{2,4},{3,5},{4,2},{5,3},{6,0},{7,1},{8,14},{9,15},{10,... | collective-permute-start | bytes 1572872 | tf_op jit(solution)/shard_map/ppermute | solution.py:106
  67.2 33.5 %collective-permute-start.18 = (bf16[4,64,1024]{2,1,0:T(8,128)(2,1)}, bf16[4,64,1024]{2,1,0:T(8,128)(2,1)}, u32[]{:S(2)}, u32[]{:S(2)}) collective-permute-start(bf16[4,64,1024]{2,1,0:T(8,128)(2,1)} %join.1.refs_1_), channel_id=1, source_target_pairs={{0,1},{1,0},{2,3},{3,2},{4,5},{5,4},{6,7},{7,6},{8,9},{9,8},{10,11... | collective-permute-start | bytes 1572872 | tf_op jit(solution)/shard_map/ppermute | solution.py:106
  98.8 2.0 collective-permute-start.19
  99.2 2.4 collective-permute-start.20
  99.4 2.9 collective-permute-start.21
  142.3 17.8 %collective-permute-start.22 = (bf16[16,32,1024]{2,1,0:T(8,128)(2,1)}, bf16[16,32,1024]{2,1,0:T(8,128)(2,1)S(1)}, u32[]{:S(2)}, u32[]{:S(2)}) collective-permute-start(bf16[16,32,1024]{2,1,0:T(8,128)(2,1)} %get-tuple-element.80), channel_id=1, source_target_pairs={{0,1},{1,0},{2,3},{3,2},{4,5},{5,4},{6,7},{7,6},{8,9},{9,8},{10,11... | collective-permute-start | bytes 3145736 | tf_op jit(solution)/shard_map/ppermute | solution.py:106
  159.8 34.2 %collective-permute-start.23 = (bf16[16,32,1024]{2,1,0:T(8,128)(2,1)}, bf16[16,32,1024]{2,1,0:T(8,128)(2,1)S(1)}, u32[]{:S(2)}, u32[]{:S(2)}) collective-permute-start(bf16[16,32,1024]{2,1,0:T(8,128)(2,1)} %get-tuple-element.90), channel_id=1, source_target_pairs={{0,1},{1,0},{2,3},{3,2},{4,5},{5,4},{6,7},{7,6},{8,9},{9,8},{10,11... | collective-permute-start | bytes 3145736 | tf_op jit(solution)/shard_map/ppermute | solution.py:106
  164.1 26.8 %collective-permute-start.24 = (bf16[4,32,1024]{2,1,0:T(8,128)(2,1)}, bf16[4,32,1024]{2,1,0:T(8,128)(2,1)S(1)}, u32[]{:S(2)}, u32[]{:S(2)}) collective-permute-start(bf16[4,32,1024]{2,1,0:T(8,128)(2,1)} %get-tuple-element.81.refs_3_), channel_id=1, source_target_pairs={{0,2},{1,3},{2,0},{3,1},{4,6},{5,7},{6,4},{7,5},{8,10},{9,11},{10,... | collective-permute-start | bytes 786440 | tf_op jit(solution)/shard_map/ppermute | solution.py:106
  165.6 25.3 %collective-permute-start.25 = (bf16[4,32,1024]{2,1,0:T(8,128)(2,1)}, bf16[4,32,1024]{2,1,0:T(8,128)(2,1)S(1)}, u32[]{:S(2)}, u32[]{:S(2)}) collective-permute-start(bf16[4,32,1024]{2,1,0:T(8,128)(2,1)} %get-tuple-element.82.refs_4_), channel_id=1, source_target_pairs={{0,4},{1,5},{2,6},{3,7},{4,0},{5,1},{6,2},{7,3},{8,12},{9,13},{10,... | collective-permute-start | bytes 786440 | tf_op jit(solution)/shard_map/ppermute | solution.py:106
  166.3 24.7 %collective-permute-start.26 = (bf16[4,32,1024]{2,1,0:T(8,128)(2,1)}, bf16[4,32,1024]{2,1,0:T(8,128)(2,1)S(1)}, u32[]{:S(2)}, u32[]{:S(2)}) collective-permute-start(bf16[4,32,1024]{2,1,0:T(8,128)(2,1)} %get-tuple-element.83.refs_5_), channel_id=1, source_target_pairs={{0,6},{1,7},{2,4},{3,5},{4,2},{5,3},{6,0},{7,1},{8,14},{9,15},{10,... | collective-permute-start | bytes 786440 | tf_op jit(solution)/shard_map/ppermute | solution.py:106
  194.0 85.7 %reduce-scatter.3.cloned.1.call-start = ((), (), s32[]{:S(2)}) async-start(), calls=%async_computation.2 | async-start | bytes 655360 | tf_op jit(solution)/shard_map/reduce_scatter | solution.py:294
  198.0 14.1 %collective-permute-start.29 = (bf16[4,32,1024]{2,1,0:T(8,128)(2,1)}, bf16[4,32,1024]{2,1,0:T(8,128)(2,1)S(1)}, u32[]{:S(2)}, u32[]{:S(2)}) collective-permute-start(bf16[4,32,1024]{2,1,0:T(8,128)(2,1)} %get-tuple-element.91.refs_2_), channel_id=1, source_target_pairs={{0,2},{1,3},{2,0},{3,1},{4,6},{5,7},{6,4},{7,5},{8,10},{9,11},{10,... | collective-permute-start | bytes 786440 | tf_op jit(solution)/shard_map/ppermute | solution.py:106
  199.5 12.6 %collective-permute-start.30 = (bf16[4,32,1024]{2,1,0:T(8,128)(2,1)}, bf16[4,32,1024]{2,1,0:T(8,128)(2,1)S(1)}, u32[]{:S(2)}, u32[]{:S(2)}) collective-permute-start(bf16[4,32,1024]{2,1,0:T(8,128)(2,1)} %get-tuple-element.92.refs_3_), channel_id=1, source_target_pairs={{0,4},{1,5},{2,6},{3,7},{4,0},{5,1},{6,2},{7,3},{8,12},{9,13},{10,... | collective-permute-start | bytes 786440 | tf_op jit(solution)/shard_map/ppermute | solution.py:106
  200.1 12.5 %collective-permute-start.31 = (bf16[4,32,1024]{2,1,0:T(8,128)(2,1)}, bf16[4,32,1024]{2,1,0:T(8,128)(2,1)S(1)}, u32[]{:S(2)}, u32[]{:S(2)}) collective-permute-start(bf16[4,32,1024]{2,1,0:T(8,128)(2,1)} %get-tuple-element.93.refs_4_), channel_id=1, source_target_pairs={{0,6},{1,7},{2,4},{3,5},{4,2},{5,3},{6,0},{7,1},{8,14},{9,15},{10,... | collective-permute-start | bytes 786440 | tf_op jit(solution)/shard_map/ppermute | solution.py:106
  215.5 65.6 %all-gather.3.cloned.1.call-start = ((), (), s32[]{:S(2)}) async-start(), calls=%async_computation.4 | async-start | bytes 2433024 | tf_op jit(solution)/shard_map/all_gather | solution.py:912
  216.1 12.4 %collective-permute-start.27 = (bf16[16,48,1024]{2,1,0:T(8,128)(2,1)}, bf16[16,48,1024]{2,1,0:T(8,128)(2,1)S(1)}, u32[]{:S(2)}, u32[]{:S(2)}) collective-permute-start(bf16[16,48,1024]{2,1,0:T(8,128)(2,1)} %get-tuple-element.96), channel_id=1, source_target_pairs={{0,1},{1,0},{2,3},{3,2},{4,5},{5,4},{6,7},{7,6},{8,9},{9,8},{10,11... | collective-permute-start | bytes 4718600 | tf_op jit(solution)/shard_map/ppermute | solution.py:106
  216.2 4.9 %collective-permute-start.28 = (bf16[16,32,1024]{2,1,0:T(8,128)(2,1)S(1)}, bf16[16,32,1024]{2,1,0:T(8,128)(2,1)S(1)}, u32[]{:S(2)}, u32[]{:S(2)}) collective-permute-start(bf16[16,32,1024]{2,1,0:T(8,128)(2,1)S(1)} %copy-done.44), channel_id=1, source_target_pairs={{0,1},{1,0},{2,3},{3,2},{4,5},{5,4},{6,7},{7,6},{8,9},{9,8},{10,11... | collective-permute-start | bytes 3145736 | tf_op jit(solution)/shard_map/ppermute | solution.py:106
  225.0 10.6 %collective-permute-start.35 = (bf16[4,32,1024]{2,1,0:T(8,128)(2,1)}, bf16[4,32,1024]{2,1,0:T(8,128)(2,1)S(1)}, u32[]{:S(2)}, u32[]{:S(2)}) collective-permute-start(bf16[4,32,1024]{2,1,0:T(8,128)(2,1)} %get-tuple-element.102.refs_3_), channel_id=1, source_target_pairs={{0,2},{1,3},{2,0},{3,1},{4,6},{5,7},{6,4},{7,5},{8,10},{9,11},{10,... | collective-permute-start | bytes 786440 | tf_op jit(solution)/shard_map/ppermute | solution.py:106
  226.5 21.5 %collective-permute-start.36 = (bf16[4,32,1024]{2,1,0:T(8,128)(2,1)}, bf16[4,32,1024]{2,1,0:T(8,128)(2,1)S(1)}, u32[]{:S(2)}, u32[]{:S(2)}) collective-permute-start(bf16[4,32,1024]{2,1,0:T(8,128)(2,1)} %get-tuple-element.103.refs_4_), channel_id=1, source_target_pairs={{0,4},{1,5},{2,6},{3,7},{4,0},{5,1},{6,2},{7,3},{8,12},{9,13},{10,... | collective-permute-start | bytes 786440 | tf_op jit(solution)/shard_map/ppermute | solution.py:106
  227.2 20.8 %collective-permute-start.37 = (bf16[4,32,1024]{2,1,0:T(8,128)(2,1)}, bf16[4,32,1024]{2,1,0:T(8,128)(2,1)S(1)}, u32[]{:S(2)}, u32[]{:S(2)}) collective-permute-start(bf16[4,32,1024]{2,1,0:T(8,128)(2,1)} %get-tuple-element.104.refs_5_), channel_id=1, source_target_pairs={{0,6},{1,7},{2,4},{3,5},{4,2},{5,3},{6,0},{7,1},{8,14},{9,15},{10,... | collective-permute-start | bytes 786440 | tf_op jit(solution)/shard_map/ppermute | solution.py:106
  233.3 19.6 %collective-permute-start.32 = (bf16[4,48,1024]{2,1,0:T(8,128)(2,1)}, bf16[4,48,1024]{2,1,0:T(8,128)(2,1)S(1)}, u32[]{:S(2)}, u32[]{:S(2)}) collective-permute-start(bf16[4,48,1024]{2,1,0:T(8,128)(2,1)} %get-tuple-element.97.refs_0_), channel_id=1, source_target_pairs={{0,2},{1,3},{2,0},{3,1},{4,6},{5,7},{6,4},{7,5},{8,10},{9,11},{10,... | collective-permute-start | bytes 1179656 | tf_op jit(solution)/shard_map/ppermute | solution.py:106
  234.8 21.3 %collective-permute-start.33 = (bf16[4,48,1024]{2,1,0:T(8,128)(2,1)}, bf16[4,48,1024]{2,1,0:T(8,128)(2,1)S(1)}, u32[]{:S(2)}, u32[]{:S(2)}) collective-permute-start(bf16[4,48,1024]{2,1,0:T(8,128)(2,1)} %get-tuple-element.98.refs_1_), channel_id=1, source_target_pairs={{0,4},{1,5},{2,6},{3,7},{4,0},{5,1},{6,2},{7,3},{8,12},{9,13},{10,... | collective-permute-start | bytes 1179656 | tf_op jit(solution)/shard_map/ppermute | solution.py:106
  235.6 24.3 %collective-permute-start.34 = (bf16[4,48,1024]{2,1,0:T(8,128)(2,1)}, bf16[4,48,1024]{2,1,0:T(8,128)(2,1)S(1)}, u32[]{:S(2)}, u32[]{:S(2)}) collective-permute-start(bf16[4,48,1024]{2,1,0:T(8,128)(2,1)} %get-tuple-element.99.refs_2_), channel_id=1, source_target_pairs={{0,6},{1,7},{2,4},{3,5},{4,2},{5,3},{6,0},{7,1},{8,14},{9,15},{10,... | collective-permute-start | bytes 1179656 | tf_op jit(solution)/shard_map/ppermute | solution.py:106
  250.8 14.3 %collective-permute-start.43 = (bf16[32,1024]{1,0:T(8,128)(2,1)}, bf16[32,1024]{1,0:T(8,128)(2,1)S(1)}, u32[]{:S(2)}, u32[]{:S(2)}) collective-permute-start(bf16[32,1024]{1,0:T(8,128)(2,1)} %get-tuple-element.110.refs_7_), channel_id=1, source_target_pairs={{0,24},{1,25},{2,26},{3,27},{4,28},{5,29},{6,30},{7,31},{8,16},{9,... | collective-permute-start | bytes 196616 | tf_op jit(solution)/shard_map/ppermute | solution.py:106
  252.9 14.4 %collective-permute-start.42 = (bf16[32,1024]{1,0:T(8,128)(2,1)}, bf16[32,1024]{1,0:T(8,128)(2,1)S(1)}, u32[]{:S(2)}, u32[]{:S(2)}) collective-permute-start(bf16[32,1024]{1,0:T(8,128)(2,1)} %get-tuple-element.109.refs_6_), channel_id=1, source_target_pairs={{0,16},{1,17},{2,18},{3,19},{4,20},{5,21},{6,22},{7,23},{8,24},{9,... | collective-permute-start | bytes 196616 | tf_op jit(solution)/shard_map/ppermute | solution.py:106
  253.0 14.4 %collective-permute-start.41 = (bf16[32,1024]{1,0:T(8,128)(2,1)}, bf16[32,1024]{1,0:T(8,128)(2,1)S(1)}, u32[]{:S(2)}, u32[]{:S(2)}) collective-permute-start(bf16[32,1024]{1,0:T(8,128)(2,1)} %get-tuple-element.108.refs_5_), channel_id=1, source_target_pairs={{0,8},{1,9},{2,10},{3,11},{4,12},{5,13},{6,14},{7,15},{8,0},{9,1},... | collective-permute-start | bytes 196616 | tf_op jit(solution)/shard_map/ppermute | solution.py:106
  262.9 9.5 %collective-permute-start.40 = (bf16[48,1024]{1,0:T(8,128)(2,1)}, bf16[48,1024]{1,0:T(8,128)(2,1)S(1)}, u32[]{:S(2)}, u32[]{:S(2)}) collective-permute-start(bf16[48,1024]{1,0:T(8,128)(2,1)} %get-tuple-element.114), channel_id=1, source_target_pairs={{0,24},{1,25},{2,26},{3,27},{4,28},{5,29},{6,30},{7,31},{8,16},{9,... | collective-permute-start | bytes 294920 | tf_op jit(solution)/shard_map/ppermute | solution.py:106
  265.1 13.4 %collective-permute-start.39 = (bf16[48,1024]{1,0:T(8,128)(2,1)}, bf16[48,1024]{1,0:T(8,128)(2,1)S(1)}, u32[]{:S(2)}, u32[]{:S(2)}) collective-permute-start(bf16[48,1024]{1,0:T(8,128)(2,1)} %get-tuple-element.113), channel_id=1, source_target_pairs={{0,16},{1,17},{2,18},{3,19},{4,20},{5,21},{6,22},{7,23},{8,24},{9,... | collective-permute-start | bytes 294920 | tf_op jit(solution)/shard_map/ppermute | solution.py:106
  265.1 13.4 %collective-permute-start.38 = (bf16[48,1024]{1,0:T(8,128)(2,1)}, bf16[48,1024]{1,0:T(8,128)(2,1)S(1)}, u32[]{:S(2)}, u32[]{:S(2)}) collective-permute-start(bf16[48,1024]{1,0:T(8,128)(2,1)} %get-tuple-element.112), channel_id=1, source_target_pairs={{0,8},{1,9},{2,10},{3,11},{4,12},{5,13},{6,14},{7,15},{8,0},{9,1},... | collective-permute-start | bytes 294920 | tf_op jit(solution)/shard_map/ppermute | solution.py:106
  (44 other events, 252.7 us)
Sparse Core Ops, SparseCore 0:
  194.1 20.5 reduce-scatter.4
  217.5 19.9 reduce-scatter.2
Sparse Core Ops, SparseCore 1:
  218.9 62.2 all-gather.2
